TPU v7x, 32 devices: a whole 2x2x4 slice. The times are simulated.
32 devices in a mesh: groups: 2 (over x), lat: 8 (over z, y), lon: 2 (over core).
Axes of the slice: x: 2, y: 2, z: 4, core: 2. Of those that a mesh axis runs over, the one named last changes fastest.
Arguments:
- first_guess: float32 [4, 512, 2048], P(None, ('groups', 'lat'), 'lon'), parts along dimension 1, may hold values from -1.5 to 1.5
- range_coef: float32 [512, 2048], P(('groups', 'lat'), 'lon'), parts along dimension 0, may hold values from 0.5 to 2
- land_sea: int32 [512, 2048], P(('groups', 'lat'), 'lon'), parts along dimension 0, may hold values from 0 to 1
- lat_kernel: float32 [65], replicated, may hold values from 0.001 to 0.06
- lon_kernel: float32 [65], replicated, may hold values from 0.001 to 0.06
- observations: bfloat16 [4, 512, 2048], P('lon', ('groups', 'lat')), parts along dimension 1, may hold values from -6 to 6
- obs_precision: bfloat16 [4, 512, 2048], P('lon', ('groups', 'lat')), parts along dimension 1, may hold values from 1 to 10
- track_counts: int32 [4, 512], P('lon', ('groups', 'lat')), parts along dimension 1, may hold values from 0 to 3
Outputs:
- solution: float32 [4, 512, 2048], P(None, ('groups', 'lat'), 'lon'), parts along dimension 1
- residual: float32 [4, 512, 2048], P(None, ('groups', 'lat'), 'lon'), parts along dimension 1
There are 2 independent parts, one for each index of `groups`. A program takes and returns all parts, laid end to end along the dimension named above; an argument that names none is the same for every part. Nothing has to cross between parts.
All inputs are finite; a program needn't handle non-finite values.
Results may differ from a plain program's by a relative error of at most 0.0003.
Values sent between devices are 32-bit elements; how exact they have to be, the bound alone decides.
No kernel may reach another device: no remote copies, remote signals or barrier semaphores. Data moves between devices by JAX's collectives and lax.ppermute only.
A program may use at most 64 MiB of HBM per device.

v0:
```python
import functools

import jax
import jax.numpy as jnp
from jax import lax
from jax.experimental import pallas as pl
from jax.experimental.pallas import tpu as pltpu
from jax.sharding import PartitionSpec as P

HALF = 32
TAPS = 2 * HALF + 1
LOWER = 0.25
UPPER = 120.0
THETA = (LOWER + UPPER) / 2.0
DELTA = (UPPER - LOWER) / 2.0
SIGMA = THETA / DELTA
RHO = 1.0 / SIGMA
NEW_RHO = 1.0 / (2.0 * SIGMA - RHO)
BLOCK = 256
EDGE = 128
AXES = ("lat", "lon")

VMEM = pl.BlockSpec(memory_space=pltpu.VMEM)
SMEM = pl.BlockSpec(memory_space=pltpu.SMEM)
F32 = jnp.float32
BF16 = jnp.bfloat16


def place():
    lat = lax.axis_index("lat")
    return lat // 2, lax.rem(lat, 2), lax.axis_index("lon")


def shape(*dims, dtype=F32):
    return jax.ShapeDtypeStruct(dims, dtype)


def call(kernel, out_shape, args, specs=None, scratch=(), flops=0, name=None):
    nbytes = sum(a.size * a.dtype.itemsize for a in args)
    nbytes += sum(o.size * o.dtype.itemsize for o in out_shape)
    return pl.pallas_call(
        kernel,
        out_shape=out_shape,
        in_specs=specs or [VMEM] * len(args),
        out_specs=[VMEM] * len(out_shape),
        scratch_shapes=list(scratch),
        compiler_params=pltpu.CompilerParams(vmem_limit_bytes=24 * 2**20),
        cost_estimate=pl.CostEstimate(flops=flops, bytes_accessed=nbytes, transcendentals=0),
        name=name,
    )(*args)


def pack_kernel(guess_ref, land_ref, own_ref, core_ref, pair_ref, diag_ref):
    _, y, c = place()
    sea = land_ref[...].astype(F32)
    own_ref[...] = guess_ref[2 * c + y] * sea
    core_ref[...] = guess_ref[2 * (1 - c) + y] * sea
    pair_ref[...] = guess_ref[2 * c + (1 - y)] * sea
    diag_ref[...] = guess_ref[2 * (1 - c) + (1 - y)] * sea


def obs_kernel(obs_ref, precision_ref, counts_ref, keep_ref, send_ref):
    _, y, c = place()
    width = obs_ref.shape[2] // 2
    for day, ref in ((y, keep_ref), (1 - y, send_ref)):
        counts = counts_ref[day].astype(F32)
        for half, side in ((0, c), (1, 1 - c)):
            source = pl.ds(pl.multiple_of(side * width, width), width)
            target = pl.ds(half * width, width)
            ref[0, :, target] = obs_ref[day, :, source].astype(F32)
            ref[1, :, target] = counts * precision_ref[day, :, source].astype(F32)


def split(values):
    high = values.astype(BF16)
    return high, (values - high.astype(F32)).astype(BF16)


def banded(kern_ref, offset):
    forward = jnp.zeros(offset.shape, F32)
    adjoint = jnp.zeros(offset.shape, F32)
    for tap in range(TAPS):
        hit = offset == tap
        forward = jnp.where(hit, kern_ref[tap], forward)
        adjoint = jnp.where(hit, kern_ref[TAPS - 1 - tap], adjoint)
    return forward, adjoint


def matrix_kernel(rows, lat_ref, lon_ref, lat_fwd_ref, lat_adj_ref, lon_fwd_ref, lon_adj_ref):
    _, y, _ = place()
    dims = (2 * rows, 4 * rows)

    def where_row(block, inside):
        return rows * jnp.where(y == 0, block, 1 - block) + inside

    out = lax.broadcasted_iota(jnp.int32, dims, 0)
    col = lax.broadcasted_iota(jnp.int32, dims, 1)
    offset = where_row(col // rows - 1, col % rows) - where_row(out // rows, out % rows) + HALF
    for ref, matrix in zip((lat_fwd_ref, lat_adj_ref), banded(lat_ref, offset)):
        high, low = split(matrix)
        ref[: 2 * rows, : 4 * rows] = high
        ref[: 2 * rows, 4 * rows :] = high
        ref[2 * rows :, : 4 * rows] = low
        ref[2 * rows :, 4 * rows :] = jnp.zeros(dims, BF16)
    dims = (EDGE, EDGE)
    offset = lax.broadcasted_iota(jnp.int32, dims, 0) - lax.broadcasted_iota(jnp.int32, dims, 1)
    for ref in (lon_fwd_ref, lon_adj_ref):
        ref[...] = jnp.zeros(ref.shape, BF16)
    for distance in range(3):
        pair = banded(lon_ref, offset + EDGE * distance - (EDGE - HALF))
        for ref, matrix in zip((lon_fwd_ref, lon_adj_ref), pair):
            for part, piece in enumerate(split(matrix)):
                for column in range(BLOCK // EDGE):
                    row = EDGE * (column + distance)
                    ref[part, row : row + EDGE, EDGE * column : EDGE * (column + 1)] = piece


def coef_kernel(own_ref, core_ref, pair_ref, diag_ref, coef_ref, sea_ref, first_ref, second_ref):
    _, y, _ = place()
    rows, width = own_ref.shape[1:]
    own = jnp.concatenate([own_ref[0], core_ref[0]], axis=1) + 4.0
    pair = jnp.concatenate([pair_ref[0], diag_ref[0]], axis=1) + 4.0
    coef_ref[pl.ds(pl.multiple_of(rows * y, rows), rows), :] = own
    coef_ref[pl.ds(pl.multiple_of(rows * (1 - y), rows), rows), :] = pair
    sea_ref[:rows, :width] = own_ref[1]
    sea_ref[:rows, width:] = core_ref[1]
    sea_ref[rows:, :width] = pair_ref[1]
    sea_ref[rows:, width:] = diag_ref[1]
    first_ref[...] = jnp.where(y == 0, own[:8], own[rows - 8 :])
    second_ref[...] = jnp.where(y == 0, pair[rows - 8 :], pair[:8])


def load(refs):
    if len(refs) == 1:
        return refs[0][...]
    return jnp.concatenate([ref[...] for ref in refs], axis=1)


def lat_conv(blocks, matrix_ref):
    high, low = split(jnp.concatenate(blocks, axis=0))
    stacked = jnp.concatenate([high, low], axis=0)
    both = jnp.dot(matrix_ref[...], stacked, preferred_element_type=F32)
    half = both.shape[0] // 2
    return both[:half] + both[half:]


def lon_conv(field, matrix_ref):
    rows, length = field.shape
    count = length // BLOCK
    parts = []
    for part in split(field):
        wide = jnp.concatenate([part[:, -EDGE:], part, part[:, :EDGE]], axis=1)
        parts += [wide[:, BLOCK * i : BLOCK * (i + 1) + 2 * EDGE] for i in range(count)]
    coarse = jnp.dot(jnp.concatenate(parts, axis=0), matrix_ref[0], preferred_element_type=F32)
    fine = jnp.dot(
        jnp.concatenate(parts[:count], axis=0), matrix_ref[1], preferred_element_type=F32
    )
    out = coarse[: count * rows] + coarse[count * rows :] + fine
    return jnp.concatenate([out[rows * i : rows * (i + 1)] for i in range(count)], axis=1)


def misfit_kernel(halves, *refs):
    fields = [load(refs[halves * i : halves * (i + 1)]) for i in range(4)]
    keep_ref, sent_ref, lat_ref, fwd_ref, adj_ref, own_ref, pair_ref = refs[4 * halves :]
    seen = lon_conv(lat_conv(fields, lat_ref), fwd_ref)
    obs = jnp.concatenate([keep_ref[0], sent_ref[0]], axis=0)
    weight = jnp.concatenate([keep_ref[1], sent_ref[1]], axis=0)
    back = lon_conv(weight * (obs - seen), adj_ref)
    rows = own_ref.shape[0]
    own_ref[...] = back[:rows]
    pair_ref[...] = back[rows:]


def beside(center, above, below):
    width = center.shape[1]
    lateral = pltpu.roll(center, 1, 1) + pltpu.roll(center, width - 1, 1)
    return above + below + lateral


def prior_kernel(pairs, halves, *refs):
    second, own, pair, first = [load(refs[halves * i : halves * (i + 1)]) for i in range(4)]
    coef_ref, sea_ref, second_ref, first_ref, out_ref, ext, wide, inner = refs[4 * halves :]
    k, y, _ = place()
    rows, length = own.shape
    for where, values in (
        (jnp.where(y == 0, 0, 3), second),
        (jnp.where(y == 0, 1, 2), own),
        (jnp.where(y == 0, 2, 1), pair),
        (jnp.where(y == 0, 3, 0), first),
    ):
        ext[pl.ds(pl.multiple_of(rows * where, rows), rows), :] = values
    coef = coef_ref[...]
    wide[8 : 8 + 2 * rows, :] = coef
    wide[:8, :] = jnp.where(y == 0, second_ref[...], first_ref[...])
    wide[8 + 2 * rows :, :] = jnp.where(y == 0, first_ref[...], second_ref[...])
    low, count = rows - 8, 2 * rows + 16
    center = ext[low : low + count, :]
    around = beside(center, ext[low - 1 : low - 1 + count, :], ext[low + 1 : low + 1 + count, :])
    inner[...] = wide[...] * center - around
    north = jnp.where(k == 0, 0.0, 1.0)
    south = jnp.where(k == pairs - 1, 0.0, 1.0)
    inner[:8, :] = inner[:8, :] * north
    inner[8 + 2 * rows :, :] = inner[8 + 2 * rows :, :] * south
    center = inner[8 : 8 + 2 * rows, :]
    outer = coef * center - beside(center, inner[7 : 7 + 2 * rows, :], inner[9 : 9 + 2 * rows, :])
    ext[: 2 * rows, :] = outer
    out_ref[:rows, :] = ext[pl.ds(pl.multiple_of(rows * y, rows), rows), :]
    out_ref[rows:, :] = ext[pl.ds(pl.multiple_of(rows * (1 - y), rows), rows), :]
    out_ref[...] = out_ref[...] * sea_ref[...]


def update_kernel(halves, *refs):
    second, own, pair, first = [ref[...] for ref in refs[:4]]
    lat_ref, prior_ref, sea_ref = refs[4:7]
    back = lat_conv([second, own, pair, first], lat_ref)
    last = sea_ref[...] * back - prior_ref[...]
    rows, length = own.shape
    width = length // 2
    outs = refs[7 + 2 * halves :]
    outs[0][...] = last[:rows, :width]
    outs[1][...] = last[:rows, width:]
    outs[2][...] = last[rows:, :width]
    outs[3][...] = last[rows:, width:]
    if halves:
        outs[4][...] = load(refs[7 : 7 + halves]) + last[:rows] * (1.0 / THETA)
        outs[5][...] = load(refs[7 + halves : 7 + 2 * halves]) + last[rows:] * (1.0 / THETA)


def final_kernel(*refs):
    early, late = refs[:4], refs[4:8]
    guess_ref, land_ref, state_ref, last_ref = refs[8:]
    _, y, c = place()
    land = 1.0 - land_ref[...].astype(F32)
    days = (2 * c + y, 2 * (1 - c) + y, 2 * c + (1 - y), 2 * (1 - c) + (1 - y))
    for day, early_ref, late_ref in zip(days, early, late):
        guess = guess_ref[day]
        update = (early_ref[...] - land * guess) * (1.0 / THETA)
        state = guess + update
        last = late_ref[...] - land * state
        update = (NEW_RHO * RHO) * update + (2.0 * NEW_RHO / DELTA) * last
        state_ref[day] = state + update
        last_ref[day] = last


def body(
    pairs,
    first_guess,
    range_coef,
    land_sea,
    lat_kernel,
    lon_kernel,
    observations,
    obs_precision,
    track_counts,
):
    days, rows, width = first_guess.shape
    length = observations.shape[2]
    assert days == 4 and rows == HALF and length == 2 * width and length % BLOCK == 0
    places = [(k, y, c) for k in range(pairs) for y in range(2) for c in range(2)]

    def permute(array, move):
        number = {at: i for i, at in enumerate(places)}
        moves = [(number[at], number[move(*at)]) for at in places if move(*at) in number]
        return lax.ppermute(array, AXES, moves)

    core = lambda array: permute(array, lambda k, y, c: (k, y, 1 - c))
    pair = lambda array: permute(array, lambda k, y, c: (k, 1 - y, c))
    diag = lambda array: permute(array, lambda k, y, c: (k, 1 - y, 1 - c))
    first = lambda array: permute(array, lambda k, y, c: (k + 2 * y - 1, y, c))
    second = lambda array: permute(array, lambda k, y, c: (k + 1 - 2 * y, y, c))

    piece = shape(rows, width)
    band = shape(rows, length)
    own, to_core, to_pair, to_diag = call(
        pack_kernel, [piece] * 4, [first_guess, land_sea], name="pack"
    )
    by_pair, by_diag, by_core = pair(to_pair), diag(to_diag), core(to_core)
    keep, send = call(
        obs_kernel,
        [shape(2, rows, length)] * 2,
        [observations, obs_precision, track_counts[:, :, None]],
        name="observed",
    )
    lat_fwd, lat_adj, lon_fwd, lon_adj = call(
        functools.partial(matrix_kernel, rows),
        [shape(4 * rows, 8 * rows, dtype=BF16)] * 2
        + [shape(2, BLOCK + 2 * EDGE, BLOCK, dtype=BF16)] * 2,
        [lat_kernel, lon_kernel],
        [SMEM, SMEM],
        flops=4 * 65 * 2 * 70000,
        name="matrices",
    )
    maps = jnp.stack([range_coef, land_sea.astype(F32)])

    send, by_pair, by_diag = lax.optimization_barrier((send, by_pair, by_diag))
    v_first = [first(own), first(by_core)]
    v_second = [second(by_pair), second(by_diag)]
    sent = pair(send)
    maps, sent = lax.optimization_barrier((maps, sent))
    maps_pair = pair(maps)
    maps_core = core(maps)
    maps_diag = core(maps_pair)
    coef, sea, edge_first, edge_second = call(
        coef_kernel,
        [shape(2 * rows, length)] * 2 + [shape(8, length)] * 2,
        [maps, maps_core, maps_pair, maps_diag],
        name="maps",
    )
    edge_first, edge_second = first(edge_first), second(edge_second)

    v_own, v_pair = [own, by_core], [by_pair, by_diag]
    pieces = []
    conv = 2 * 3 * 2 * rows * length * 512
    for step in range(2):
        halves = len(v_own)
        fields = v_second + v_own + v_pair + v_first
        m_own, m_pair = call(
            functools.partial(misfit_kernel, halves),
            [band] * 2,
            fields + [keep, sent, lat_fwd, lon_fwd, lon_adj],
            flops=3 * conv,
            name="misfit",
        )
        m_first, m_second = first(m_own), second(m_pair)
        (prior,) = call(
            functools.partial(prior_kernel, pairs, halves),
            [shape(2 * rows, length)],
            fields + [coef, sea, edge_second, edge_first],
            scratch=[
                pltpu.VMEM((4 * rows, length), F32),
                pltpu.VMEM((2 * rows + 16, length), F32),
                pltpu.VMEM((2 * rows + 16, length), F32),
            ],
            flops=20 * 2 * rows * length,
            name="prior",
        )
        base = v_own + v_pair if step == 0 else []
        outs = call(
            functools.partial(update_kernel, len(base) // 2),
            [piece] * 4 + ([band] * 2 if base else []),
            [m_second, m_own, m_pair, m_first, lat_adj, prior, sea] + base,
            flops=conv,
            name="update",
        )
        pieces += [outs[0], core(outs[1]), pair(outs[2]), diag(outs[3])]
        if base:
            v_own, v_pair = [outs[4]], [outs[5]]
            v_first, v_second = [first(outs[4])], [second(outs[5])]
    state, last = call(
        final_kernel,
        [shape(days, rows, width)] * 2,
        pieces + [first_guess, land_sea],
        name="final",
    )
    return state, last


def solution(mesh):
    assert mesh.shape["lat"] % 2 == 0 and mesh.shape["lon"] == 2
    in_specs = (
        P(None, ("groups", "lat"), "lon"),
        P(("groups", "lat"), "lon"),
        P(("groups", "lat"), "lon"),
        P(),
        P(),
        P("lon", ("groups", "lat"), None),
        P("lon", ("groups", "lat"), None),
        P("lon", ("groups", "lat")),
    )
    out_specs = (P(None, ("groups", "lat"), "lon"), P(None, ("groups", "lat"), "lon"))
    return jax.shard_map(
        functools.partial(body, mesh.shape["lat"] // 2),
        mesh=mesh,
        in_specs=in_specs,
        out_specs=out_specs,
        check_vma=False,
    )
```

profile of v0, /device:TPU:0, one launch (start us, length us, event | category | flops | bytes accessed | tf_op | source)
XLA Modules:
  0.0 97.4 jit_solution(2794453478226108558)
XLA Ops:
  2.6 3.0 %collective-permute-start = (f32[32,1024]{1,0:T(8,128)S(1)}, f32[32,1024]{1,0:T(8,128)S(1)}, u32[]{:S(2)}, u32[]{:S(2)}) collective-permute-start(f32[32,1024]{1,0:T(8,128)S(1)} %get-tuple-element.36), channel_id=1, source_target_pairs={{0,2},{1,3},{2,0},{3,1},{4,6},{5,7},{6,4},{7,5},{8,10},{9,11},{10,... | collective-permute-start | bytes 393224 | tf_op jit(solution)/shard_map/ppermute | solution.py:264
  6.6 3.0 %collective-permute-done.refs_4_.refs_9_ = f32[32,1024]{1,0:T(8,128)S(1)} collective-permute-done((f32[32,1024]{1,0:T(8,128)S(1)}, f32[32,1024]{1,0:T(8,128)S(1)}, u32[]{:S(2)}, u32[]{:S(2)}) %collective-permute-start) | collective-permute-done | bytes 131104 | tf_op jit(solution)/shard_map/ppermute | solution.py:264
  9.6 1.9 %collective-permute-done.1.refs_5_.refs_10_ = f32[32,1024]{1,0:T(8,128)S(1)} collective-permute-done((f32[32,1024]{1,0:T(8,128)S(1)}, f32[32,1024]{1,0:T(8,128)S(1)}, u32[]{:S(2)}, u32[]{:S(2)}) %collective-permute-start.1) | collective-permute-done | bytes 131104 | tf_op jit(solution)/shard_map/ppermute | solution.py:264
  12.6 13.0 %collective-permute-done.7.refs_9_.refs_5_ = f32[2,32,2048]{2,1,0:T(8,128)S(1)} collective-permute-done((f32[2,32,2048]{2,1,0:T(8,128)S(1)}, f32[2,32,2048]{2,1,0:T(8,128)S(1)}, u32[]{:S(2)}, u32[]{:S(2)}) %collective-permute-start.7) | collective-permute-done | bytes 524320 | tf_op jit(solution)/shard_map/ppermute | solution.py:264
  25.6 1.7 %collective-permute-start.11 = (f32[2,32,1024]{2,1,0:T(8,128)S(1)}, f32[2,32,1024]{2,1,0:T(8,128)S(1)}, u32[]{:S(2)}, u32[]{:S(2)}) collective-permute-start(f32[2,32,1024]{2,1,0:T(8,128)S(1)} %pad_maximum_fusion.own_ref), channel_id=1, source_target_pairs={{0,2},{1,3},{2,0},{3,1},{4,6},{5,7},{6,4},{7,5},{8,10},{9,11},{10,... | collective-permute-start | bytes 786440 | tf_op jit(solution)/shard_map/ppermute | solution.py:264
  27.4 1.4 %collective-permute-start.5 = (f32[32,1024]{1,0:T(8,128)S(1)}, f32[32,1024]{1,0:T(8,128)S(1)}, u32[]{:S(2)}, u32[]{:S(2)}) collective-permute-start(f32[32,1024]{1,0:T(8,128)S(1)} %get-tuple-element.40.refs_2_.refs_7_), channel_id=1, source_target_pairs={{2,6},{3,7},{4,0},{5,1},{6,10},{7,11},{8,4},{9,5},{10,14},{11,15},... | collective-permute-start | bytes 393224 | tf_op jit(solution)/shard_map/ppermute | solution.py:264
  28.8 4.6 %collective-permute-start.2 = (f32[32,1024]{1,0:T(8,128)S(1)}, f32[32,1024]{1,0:T(8,128)S(1)}, u32[]{:S(2)}, u32[]{:S(2)}) collective-permute-start(f32[32,1024]{1,0:T(8,128)S(1)} %collective-permute-done.refs_4_.refs_9_), channel_id=1, source_target_pairs={{0,4},{1,5},{4,8},{5,9},{6,2},{7,3},{8,12},{9,13},{10,6},{11,7},{1... | collective-permute-start | bytes 393224 | tf_op jit(solution)/shard_map/ppermute | solution.py:264
  33.4 1.3 %collective-permute-start.6 = (f32[32,1024]{1,0:T(8,128)S(1)}, f32[32,1024]{1,0:T(8,128)S(1)}, u32[]{:S(2)}, u32[]{:S(2)}) collective-permute-start(f32[32,1024]{1,0:T(8,128)S(1)} %collective-permute-done.4.refs_3_.refs_8_), channel_id=1, source_target_pairs={{2,6},{3,7},{4,0},{5,1},{6,10},{7,11},{8,4},{9,5},{10,14},{11,15},... | collective-permute-start | bytes 393224 | tf_op jit(solution)/shard_map/ppermute | solution.py:264
  34.7 4.6 %collective-permute-start.3 = (f32[32,1024]{1,0:T(8,128)S(1)}, f32[32,1024]{1,0:T(8,128)S(1)}, u32[]{:S(2)}, u32[]{:S(2)}) collective-permute-start(f32[32,1024]{1,0:T(8,128)S(1)} %collective-permute-done.1.refs_5_.refs_10_), channel_id=1, source_target_pairs={{0,4},{1,5},{4,8},{5,9},{6,2},{7,3},{8,12},{9,13},{10,6},{11,7},{1... | collective-permute-start | bytes 393224 | tf_op jit(solution)/shard_map/ppermute | solution.py:264
  39.3 2.1 %matrices.1 = (bf16[128,256]{1,0:T(8,128)(2,1)S(1)}, bf16[128,256]{1,0:T(8,128)(2,1)S(1)}, bf16[2,512,256]{2,1,0:T(8,128)(2,1)S(1)}, bf16[2,512,256]{2,1,0:T(8,128)(2,1)S(1)}) custom-call(f32[65]{0:T(128)S(1)} %copy-done.6, f32[65]{0:T(128)S(1)} %copy-done.7), custom_call_target="tpu_custom_call" | custom-call | flops 36400000 | bytes 1180168 | tf_op jit(solution)/shard_map/matrices/pallas_call | solution.py:41
  42.0 2.1 %misfit.2 = (f32[32,2048]{1,0:T(8,128)S(1)}, f32[32,2048]{1,0:T(8,128)S(1)}) custom-call(f32[32,1024]{1,0:T(8,128)S(1)} %collective-permute-done.2.refs_0_, f32[32,1024]{1,0:T(8,128)S(1)} %collective-permute-done.3.refs_1_, f32[32,1024]{1,0:T(8,128)S(1)} %get-tuple-element.40.refs_2_.refs_7_, f32[32,1024]{1,0:T(8,128)S(1)} %collective-permute-done.4.refs_3_.refs_8_, ...), custom_call_target="tpu_custom_call" | custom-call | flops 1207959552 | bytes 3735552 | tf_op jit(solution)/shard_map/misfit/pallas_call | solution.py:41
  44.1 4.1 %collective-permute-start.8 = (f32[32,2048]{1,0:T(8,128)S(1)}, f32[32,2048]{1,0:T(8,128)S(1)}, u32[]{:S(2)}, u32[]{:S(2)}) collective-permute-start(f32[32,2048]{1,0:T(8,128)S(1)} %get-tuple-element.48.refs_2_), channel_id=1, source_target_pairs={{0,4},{1,5},{4,8},{5,9},{6,2},{7,3},{8,12},{9,13},{10,6},{11,7},{1... | collective-permute-start | bytes 786440 | tf_op jit(solution)/shard_map/ppermute | solution.py:264
  49.7 4.5 %collective-permute-start.13 = (f32[8,2048]{1,0:T(8,128)S(1)}, f32[8,2048]{1,0:T(8,128)S(1)}, u32[]{:S(2)}, u32[]{:S(2)}) collective-permute-start(f32[8,2048]{1,0:T(8,128)S(1)} %get-tuple-element.54), channel_id=1, source_target_pairs={{0,4},{1,5},{4,8},{5,9},{6,2},{7,3},{8,12},{9,13},{10,6},{11,7},{1... | collective-permute-start | bytes 196616 | tf_op jit(solution)/shard_map/ppermute | solution.py:264
  56.1 4.3 %collective-permute-done.14.refs_11_.refs_7_ = f32[8,2048]{1,0:T(8,128)S(1)} collective-permute-done((f32[8,2048]{1,0:T(8,128)S(1)}, f32[8,2048]{1,0:T(8,128)S(1)}, u32[]{:S(2)}, u32[]{:S(2)}) %collective-permute-start.14) | collective-permute-done | bytes 65568 | tf_op jit(solution)/shard_map/ppermute | solution.py:264
  61.9 3.5 %collective-permute-start.18 = (f32[32,2048]{1,0:T(8,128)S(1)}, f32[32,2048]{1,0:T(8,128)S(1)}, u32[]{:S(2)}, u32[]{:S(2)}) collective-permute-start(f32[32,2048]{1,0:T(8,128)S(1)} %get-tuple-element.60.refs_2_), channel_id=1, source_target_pairs={{0,4},{1,5},{4,8},{5,9},{6,2},{7,3},{8,12},{9,13},{10,6},{11,7},{1... | collective-permute-start | bytes 786440 | tf_op jit(solution)/shard_map/ppermute | solution.py:264
  66.7 2.6 %collective-permute-done.18.refs_0_ = f32[32,2048]{1,0:T(8,128)S(1)} collective-permute-done((f32[32,2048]{1,0:T(8,128)S(1)}, f32[32,2048]{1,0:T(8,128)S(1)}, u32[]{:S(2)}, u32[]{:S(2)}) %collective-permute-start.18) | collective-permute-done | bytes 262176 | tf_op jit(solution)/shard_map/ppermute | solution.py:264
  69.3 4.4 %collective-permute-done.19.refs_3_ = f32[32,2048]{1,0:T(8,128)S(1)} collective-permute-done((f32[32,2048]{1,0:T(8,128)S(1)}, f32[32,2048]{1,0:T(8,128)S(1)}, u32[]{:S(2)}, u32[]{:S(2)}) %collective-permute-start.19) | collective-permute-done | bytes 262176 | tf_op jit(solution)/shard_map/ppermute | solution.py:264
  73.7 2.1 %misfit.3 = (f32[32,2048]{1,0:T(8,128)S(1)}, f32[32,2048]{1,0:T(8,128)S(1)}) custom-call(f32[32,2048]{1,0:T(8,128)S(1)} %collective-permute-done.18.refs_0_, f32[32,2048]{1,0:T(8,128)S(1)} %get-tuple-element.61.refs_1_, f32[32,2048]{1,0:T(8,128)S(1)} %get-tuple-element.60.refs_2_, f32[32,2048]{1,0:T(8,128)S(1)} %collective-permute-done.19.refs_3_, ...), custom_call_target="tpu_custom_call" | custom-call | flops 1207959552 | bytes 3735552 | tf_op jit(solution)/shard_map/misfit/pallas_call | solution.py:41
  75.8 3.5 %collective-permute-start.20 = (f32[32,2048]{1,0:T(8,128)S(1)}, f32[32,2048]{1,0:T(8,128)S(1)}, u32[]{:S(2)}, u32[]{:S(2)}) collective-permute-start(f32[32,2048]{1,0:T(8,128)S(1)} %get-tuple-element.62.refs_2_), channel_id=1, source_target_pairs={{0,4},{1,5},{4,8},{5,9},{6,2},{7,3},{8,12},{9,13},{10,6},{11,7},{1... | collective-permute-start | bytes 786440 | tf_op jit(solution)/shard_map/ppermute | solution.py:264
  80.8 1.8 %collective-permute-start.17 = (f32[32,1024]{1,0:T(8,128)S(1)}, f32[32,1024]{1,0:T(8,128)S(1)}, u32[]{:S(2)}, u32[]{:S(2)}) collective-permute-start(f32[32,1024]{1,0:T(8,128)S(1)} %get-tuple-element.59), channel_id=1, source_target_pairs={{0,3},{1,2},{2,1},{3,0},{4,7},{5,6},{6,5},{7,4},{8,11},{9,10},{10,... | collective-permute-start | bytes 393224 | tf_op jit(solution)/shard_map/ppermute | solution.py:264
  83.8 3.8 %collective-permute-done.21.refs_3_ = f32[32,2048]{1,0:T(8,128)S(1)} collective-permute-done((f32[32,2048]{1,0:T(8,128)S(1)}, f32[32,2048]{1,0:T(8,128)S(1)}, u32[]{:S(2)}, u32[]{:S(2)}) %collective-permute-start.21) | collective-permute-done | bytes 262176 | tf_op jit(solution)/shard_map/ppermute | solution.py:264
  88.1 1.8 %collective-permute-start.24 = (f32[32,1024]{1,0:T(8,128)S(1)}, f32[32,1024]{1,0:T(8,128)S(1)}, u32[]{:S(2)}, u32[]{:S(2)}) collective-permute-start(f32[32,1024]{1,0:T(8,128)S(1)} %get-tuple-element.67), channel_id=1, source_target_pairs={{0,3},{1,2},{2,1},{3,0},{4,7},{5,6},{6,5},{7,4},{8,11},{9,10},{10,... | collective-permute-start | bytes 393224 | tf_op jit(solution)/shard_map/ppermute | solution.py:264
  89.9 4.5 %collective-permute-done.23.refs_6_ = f32[32,1024]{1,0:T(8,128)S(1)} collective-permute-done((f32[32,1024]{1,0:T(8,128)S(1)}, f32[32,1024]{1,0:T(8,128)S(1)}, u32[]{:S(2)}, u32[]{:S(2)}) %collective-permute-start.23) | collective-permute-done | bytes 131104 | tf_op jit(solution)/shard_map/ppermute | solution.py:264
  94.4 1.9 %collective-permute-done.24.refs_7_ = f32[32,1024]{1,0:T(8,128)S(1)} collective-permute-done((f32[32,1024]{1,0:T(8,128)S(1)}, f32[32,1024]{1,0:T(8,128)S(1)}, u32[]{:S(2)}, u32[]{:S(2)}) %collective-permute-start.24) | collective-permute-done | bytes 131104 | tf_op jit(solution)/shard_map/ppermute | solution.py:264
  (60 shorter events, 14.9 us)
Async XLA Ops:
  2.6 7.0 %collective-permute-start = (f32[32,1024]{1,0:T(8,128)S(1)}, f32[32,1024]{1,0:T(8,128)S(1)}, u32[]{:S(2)}, u32[]{:S(2)}) collective-permute-start(f32[32,1024]{1,0:T(8,128)S(1)} %get-tuple-element.36), channel_id=1, source_target_pairs={{0,2},{1,3},{2,0},{3,1},{4,6},{5,7},{6,4},{7,5},{8,10},{9,11},{10,... | collective-permute-start | bytes 393224 | tf_op jit(solution)/shard_map/ppermute | solution.py:264
  5.7 5.9 %collective-permute-start.1 = (f32[32,1024]{1,0:T(8,128)S(1)}, f32[32,1024]{1,0:T(8,128)S(1)}, u32[]{:S(2)}, u32[]{:S(2)}) collective-permute-start(f32[32,1024]{1,0:T(8,128)S(1)} %get-tuple-element.37), channel_id=1, source_target_pairs={{0,3},{1,2},{2,1},{3,0},{4,7},{5,6},{6,5},{7,4},{8,11},{9,10},{10,... | collective-permute-start | bytes 393224 | tf_op jit(solution)/shard_map/ppermute | solution.py:264
  11.5 14.1 %collective-permute-start.7 = (f32[2,32,2048]{2,1,0:T(8,128)S(1)}, f32[2,32,2048]{2,1,0:T(8,128)S(1)}, u32[]{:S(2)}, u32[]{:S(2)}) collective-permute-start(f32[2,32,2048]{2,1,0:T(8,128)S(1)} %get-tuple-element.43), channel_id=1, source_target_pairs={{0,2},{1,3},{2,0},{3,1},{4,6},{5,7},{6,4},{7,5},{8,10},{9,11},{10,... | collective-permute-start | bytes 1572872 | tf_op jit(solution)/shard_map/ppermute | solution.py:264
  25.6 15.8 %collective-permute-start.11 = (f32[2,32,1024]{2,1,0:T(8,128)S(1)}, f32[2,32,1024]{2,1,0:T(8,128)S(1)}, u32[]{:S(2)}, u32[]{:S(2)}) collective-permute-start(f32[2,32,1024]{2,1,0:T(8,128)S(1)} %pad_maximum_fusion.own_ref), channel_id=1, source_target_pairs={{0,2},{1,3},{2,0},{3,1},{4,6},{5,7},{6,4},{7,5},{8,10},{9,11},{10,... | collective-permute-start | bytes 786440 | tf_op jit(solution)/shard_map/ppermute | solution.py:264
  27.4 6.0 %collective-permute-start.4 = (f32[32,1024]{1,0:T(8,128)S(1)}, f32[32,1024]{1,0:T(8,128)S(1)}, u32[]{:S(2)}, u32[]{:S(2)}) collective-permute-start(f32[32,1024]{1,0:T(8,128)S(1)} %get-tuple-element.41), channel_id=1, source_target_pairs={{0,1},{1,0},{2,3},{3,2},{4,5},{5,4},{6,7},{7,6},{8,9},{9,8},{10,11... | collective-permute-start | bytes 393224 | tf_op jit(solution)/shard_map/ppermute | solution.py:264
  27.4 14.0 %collective-permute-start.5 = (f32[32,1024]{1,0:T(8,128)S(1)}, f32[32,1024]{1,0:T(8,128)S(1)}, u32[]{:S(2)}, u32[]{:S(2)}) collective-permute-start(f32[32,1024]{1,0:T(8,128)S(1)} %get-tuple-element.40.refs_2_.refs_7_), channel_id=1, source_target_pairs={{2,6},{3,7},{4,0},{5,1},{6,10},{7,11},{8,4},{9,5},{10,14},{11,15},... | collective-permute-start | bytes 393224 | tf_op jit(solution)/shard_map/ppermute | solution.py:264
  28.8 13.2 %collective-permute-start.2 = (f32[32,1024]{1,0:T(8,128)S(1)}, f32[32,1024]{1,0:T(8,128)S(1)}, u32[]{:S(2)}, u32[]{:S(2)}) collective-permute-start(f32[32,1024]{1,0:T(8,128)S(1)} %collective-permute-done.refs_4_.refs_9_), channel_id=1, source_target_pairs={{0,4},{1,5},{4,8},{5,9},{6,2},{7,3},{8,12},{9,13},{10,6},{11,7},{1... | collective-permute-start | bytes 393224 | tf_op jit(solution)/shard_map/ppermute | solution.py:264
  33.4 8.6 %collective-permute-start.6 = (f32[32,1024]{1,0:T(8,128)S(1)}, f32[32,1024]{1,0:T(8,128)S(1)}, u32[]{:S(2)}, u32[]{:S(2)}) collective-permute-start(f32[32,1024]{1,0:T(8,128)S(1)} %collective-permute-done.4.refs_3_.refs_8_), channel_id=1, source_target_pairs={{2,6},{3,7},{4,0},{5,1},{6,10},{7,11},{8,4},{9,5},{10,14},{11,15},... | collective-permute-start | bytes 393224 | tf_op jit(solution)/shard_map/ppermute | solution.py:264
  34.7 7.3 %collective-permute-start.3 = (f32[32,1024]{1,0:T(8,128)S(1)}, f32[32,1024]{1,0:T(8,128)S(1)}, u32[]{:S(2)}, u32[]{:S(2)}) collective-permute-start(f32[32,1024]{1,0:T(8,128)S(1)} %collective-permute-done.1.refs_5_.refs_10_), channel_id=1, source_target_pairs={{0,4},{1,5},{4,8},{5,9},{6,2},{7,3},{8,12},{9,13},{10,6},{11,7},{1... | collective-permute-start | bytes 393224 | tf_op jit(solution)/shard_map/ppermute | solution.py:264
  41.4 8.1 %collective-permute-start.10 = (f32[2,32,1024]{2,1,0:T(8,128)S(1)}, f32[2,32,1024]{2,1,0:T(8,128)S(1)}, u32[]{:S(2)}, u32[]{:S(2)}) collective-permute-start(f32[2,32,1024]{2,1,0:T(8,128)S(1)} %pad_maximum_fusion.own_ref), channel_id=1, source_target_pairs={{0,1},{1,0},{2,3},{3,2},{4,5},{5,4},{6,7},{7,6},{8,9},{9,8},{10,11... | collective-permute-start | bytes 786440 | tf_op jit(solution)/shard_map/ppermute | solution.py:264
  41.5 8.1 %collective-permute-start.12 = (f32[2,32,1024]{2,1,0:T(8,128)S(1)}, f32[2,32,1024]{2,1,0:T(8,128)S(1)}, u32[]{:S(2)}, u32[]{:S(2)}) collective-permute-start(f32[2,32,1024]{2,1,0:T(8,128)S(1)} %collective-permute-done.11.pair_ref), channel_id=1, source_target_pairs={{0,1},{1,0},{2,3},{3,2},{4,5},{5,4},{6,7},{7,6},{8,9},{9,8},{10,11... | collective-permute-start | bytes 786440 | tf_op jit(solution)/shard_map/ppermute | solution.py:264
  44.1 17.5 %collective-permute-start.8 = (f32[32,2048]{1,0:T(8,128)S(1)}, f32[32,2048]{1,0:T(8,128)S(1)}, u32[]{:S(2)}, u32[]{:S(2)}) collective-permute-start(f32[32,2048]{1,0:T(8,128)S(1)} %get-tuple-element.48.refs_2_), channel_id=1, source_target_pairs={{0,4},{1,5},{4,8},{5,9},{6,2},{7,3},{8,12},{9,13},{10,6},{11,7},{1... | collective-permute-start | bytes 786440 | tf_op jit(solution)/shard_map/ppermute | solution.py:264
  48.2 13.4 %collective-permute-start.9 = (f32[32,2048]{1,0:T(8,128)S(1)}, f32[32,2048]{1,0:T(8,128)S(1)}, u32[]{:S(2)}, u32[]{:S(2)}) collective-permute-start(f32[32,2048]{1,0:T(8,128)S(1)} %get-tuple-element.49.refs_1_), channel_id=1, source_target_pairs={{2,6},{3,7},{4,0},{5,1},{6,10},{7,11},{8,4},{9,5},{10,14},{11,15},... | collective-permute-start | bytes 786440 | tf_op jit(solution)/shard_map/ppermute | solution.py:264
  49.7 6.4 %collective-permute-start.13 = (f32[8,2048]{1,0:T(8,128)S(1)}, f32[8,2048]{1,0:T(8,128)S(1)}, u32[]{:S(2)}, u32[]{:S(2)}) collective-permute-start(f32[8,2048]{1,0:T(8,128)S(1)} %get-tuple-element.54), channel_id=1, source_target_pairs={{0,4},{1,5},{4,8},{5,9},{6,2},{7,3},{8,12},{9,13},{10,6},{11,7},{1... | collective-permute-start | bytes 196616 | tf_op jit(solution)/shard_map/ppermute | solution.py:264
  54.2 6.2 %collective-permute-start.14 = (f32[8,2048]{1,0:T(8,128)S(1)}, f32[8,2048]{1,0:T(8,128)S(1)}, u32[]{:S(2)}, u32[]{:S(2)}) collective-permute-start(f32[8,2048]{1,0:T(8,128)S(1)} %get-tuple-element.55), channel_id=1, source_target_pairs={{2,6},{3,7},{4,0},{5,1},{6,10},{7,11},{8,4},{9,5},{10,14},{11,15},... | collective-permute-start | bytes 196616 | tf_op jit(solution)/shard_map/ppermute | solution.py:264
  61.9 7.4 %collective-permute-start.18 = (f32[32,2048]{1,0:T(8,128)S(1)}, f32[32,2048]{1,0:T(8,128)S(1)}, u32[]{:S(2)}, u32[]{:S(2)}) collective-permute-start(f32[32,2048]{1,0:T(8,128)S(1)} %get-tuple-element.60.refs_2_), channel_id=1, source_target_pairs={{0,4},{1,5},{4,8},{5,9},{6,2},{7,3},{8,12},{9,13},{10,6},{11,7},{1... | collective-permute-start | bytes 786440 | tf_op jit(solution)/shard_map/ppermute | solution.py:264
  65.4 8.3 %collective-permute-start.19 = (f32[32,2048]{1,0:T(8,128)S(1)}, f32[32,2048]{1,0:T(8,128)S(1)}, u32[]{:S(2)}, u32[]{:S(2)}) collective-permute-start(f32[32,2048]{1,0:T(8,128)S(1)} %get-tuple-element.61.refs_1_), channel_id=1, source_target_pairs={{2,6},{3,7},{4,0},{5,1},{6,10},{7,11},{8,4},{9,5},{10,14},{11,15},... | collective-permute-start | bytes 786440 | tf_op jit(solution)/shard_map/ppermute | solution.py:264
  75.8 8.0 %collective-permute-start.20 = (f32[32,2048]{1,0:T(8,128)S(1)}, f32[32,2048]{1,0:T(8,128)S(1)}, u32[]{:S(2)}, u32[]{:S(2)}) collective-permute-start(f32[32,2048]{1,0:T(8,128)S(1)} %get-tuple-element.62.refs_2_), channel_id=1, source_target_pairs={{0,4},{1,5},{4,8},{5,9},{6,2},{7,3},{8,12},{9,13},{10,6},{11,7},{1... | collective-permute-start | bytes 786440 | tf_op jit(solution)/shard_map/ppermute | solution.py:264
  79.3 8.3 %collective-permute-start.21 = (f32[32,2048]{1,0:T(8,128)S(1)}, f32[32,2048]{1,0:T(8,128)S(1)}, u32[]{:S(2)}, u32[]{:S(2)}) collective-permute-start(f32[32,2048]{1,0:T(8,128)S(1)} %get-tuple-element.63.refs_1_), channel_id=1, source_target_pairs={{2,6},{3,7},{4,0},{5,1},{6,10},{7,11},{8,4},{9,5},{10,14},{11,15},... | collective-permute-start | bytes 786440 | tf_op jit(solution)/shard_map/ppermute | solution.py:264
  80.6 7.4 %collective-permute-start.15 = (f32[32,1024]{1,0:T(8,128)S(1)}, f32[32,1024]{1,0:T(8,128)S(1)}, u32[]{:S(2)}, u32[]{:S(2)}) collective-permute-start(f32[32,1024]{1,0:T(8,128)S(1)} %get-tuple-element.57), channel_id=1, source_target_pairs={{0,1},{1,0},{2,3},{3,2},{4,5},{5,4},{6,7},{7,6},{8,9},{9,8},{10,11... | collective-permute-start | bytes 393224 | tf_op jit(solution)/shard_map/ppermute | solution.py:264
  80.7 9.2 %collective-permute-start.16 = (f32[32,1024]{1,0:T(8,128)S(1)}, f32[32,1024]{1,0:T(8,128)S(1)}, u32[]{:S(2)}, u32[]{:S(2)}) collective-permute-start(f32[32,1024]{1,0:T(8,128)S(1)} %get-tuple-element.58), channel_id=1, source_target_pairs={{0,2},{1,3},{2,0},{3,1},{4,6},{5,7},{6,4},{7,5},{8,10},{9,11},{10,... | collective-permute-start | bytes 393224 | tf_op jit(solution)/shard_map/ppermute | solution.py:264
  80.8 9.1 %collective-permute-start.17 = (f32[32,1024]{1,0:T(8,128)S(1)}, f32[32,1024]{1,0:T(8,128)S(1)}, u32[]{:S(2)}, u32[]{:S(2)}) collective-permute-start(f32[32,1024]{1,0:T(8,128)S(1)} %get-tuple-element.59), channel_id=1, source_target_pairs={{0,3},{1,2},{2,1},{3,0},{4,7},{5,6},{6,5},{7,4},{8,11},{9,10},{10,... | collective-permute-start | bytes 393224 | tf_op jit(solution)/shard_map/ppermute | solution.py:264
  88.0 6.4 %collective-permute-start.23 = (f32[32,1024]{1,0:T(8,128)S(1)}, f32[32,1024]{1,0:T(8,128)S(1)}, u32[]{:S(2)}, u32[]{:S(2)}) collective-permute-start(f32[32,1024]{1,0:T(8,128)S(1)} %get-tuple-element.66), channel_id=1, source_target_pairs={{0,2},{1,3},{2,0},{3,1},{4,6},{5,7},{6,4},{7,5},{8,10},{9,11},{10,... | collective-permute-start | bytes 393224 | tf_op jit(solution)/shard_map/ppermute | solution.py:264
  88.1 8.2 %collective-permute-start.24 = (f32[32,1024]{1,0:T(8,128)S(1)}, f32[32,1024]{1,0:T(8,128)S(1)}, u32[]{:S(2)}, u32[]{:S(2)}) collective-permute-start(f32[32,1024]{1,0:T(8,128)S(1)} %get-tuple-element.67), channel_id=1, source_target_pairs={{0,3},{1,2},{2,1},{3,0},{4,7},{5,6},{6,5},{7,4},{8,11},{9,10},{10,... | collective-permute-start | bytes 393224 | tf_op jit(solution)/shard_map/ppermute | solution.py:264
  (11 other events, 55.7 us)
where the time goes:
time: 97.9 us; the launch traced here: 97.4 us
  starting transfers between devices  42.9 us (44%)
  waiting for transfers between devices  40 us (41%)
  Pallas kernels  10.8 us (11%)
  local copies, waits for them, and re-layouts  2.74 us (3%)
  between operations  0.98 us (1%)
    ppermute x25, starting transfers between devices, permute(): return lax.ppermute(array, AXES, moves)  42.9 us
    ppermute x25, waiting for transfers between devices, permute(): return lax.ppermute(array, AXES, moves)  40 us
    pallas_call x11, Pallas kernels, call(): pl.pallas_call(kernel, out_shape=out_shape, in_specs=specs or [VMEM] * le...  10.8 us
    unnamed x20, local copies, waits for them, and re-layouts  2.65 us
  transfers between devices with their start and end apart: 25, of which 10 were waited for; matrix products, arithmetic and copies ran while one was open for 0% of the time, Pallas kernels for 7%

commit v1 on v0

v1 whole, which is shorter than its diff:
```python
import functools

import jax
import jax.numpy as jnp
from jax import lax
from jax.experimental import pallas as pl
from jax.experimental.pallas import tpu as pltpu
from jax.sharding import PartitionSpec as P

HALF = 32
TAPS = 2 * HALF + 1
LOWER = 0.25
UPPER = 120.0
THETA = (LOWER + UPPER) / 2.0
DELTA = (UPPER - LOWER) / 2.0
SIGMA = THETA / DELTA
RHO = 1.0 / SIGMA
NEW_RHO = 1.0 / (2.0 * SIGMA - RHO)
BLOCK = 256
EDGE = 128
ADJOINT_COST = 2 * 10**10
PACK_VMEM = 62 * 2**20
AXES = ("lat", "lon")

VMEM = pl.BlockSpec(memory_space=pltpu.VMEM)
SMEM = pl.BlockSpec(memory_space=pltpu.SMEM)
HBM = pl.BlockSpec(memory_space=pltpu.HBM)
F32 = jnp.float32
BF16 = jnp.bfloat16


def place():
    lat = lax.axis_index("lat")
    return lat // 2, lax.rem(lat, 2), lax.axis_index("lon")


def open_sides(pairs):
    k, _, _ = place()
    north, south = jnp.where(k == 0, 0.0, 1.0), jnp.where(k == pairs - 1, 0.0, 1.0)
    even = lax.rem(k, 2) == 0
    return jnp.where(even, north, south), jnp.where(even, south, north)


def odd_even(own, pair):
    k, y, _ = place()
    straight = lax.rem(k + y, 2) == 0
    return jnp.where(straight, own, pair), jnp.where(straight, pair, own)


def shape(*dims, dtype=F32):
    return jax.ShapeDtypeStruct(dims, dtype)


def call(
    kernel, out_shape, args, specs=None, outs=None, scratch=(), flops=0, vmem=24 * 2**20, name=None
):
    nbytes = sum(a.size * a.dtype.itemsize for a in args)
    nbytes += sum(o.size * o.dtype.itemsize for o in out_shape)
    return pl.pallas_call(
        kernel,
        out_shape=out_shape,
        in_specs=specs or [VMEM] * len(args),
        out_specs=outs or [VMEM] * len(out_shape),
        scratch_shapes=list(scratch),
        compiler_params=pltpu.CompilerParams(vmem_limit_bytes=vmem),
        cost_estimate=pl.CostEstimate(flops=flops, bytes_accessed=nbytes, transcendentals=0),
        name=name,
    )(*args)


def pack_kernel(guess_ref, land_ref, coef_ref, own_ref, core_ref, pair_ref, diag_ref, *scratch):
    guess, land, coef, packed, sems = scratch
    _, y, c = place()
    days = (2 * c + (1 - y), 2 * (1 - c) + (1 - y), 2 * (1 - c) + y, 2 * c + y)
    rows, width = land.shape
    start = pl.multiple_of((rows - 8) * y, 8)
    copies = [
        pltpu.make_async_copy(land_ref, land, sems.at[0]),
        pltpu.make_async_copy(coef_ref.at[pl.ds(start, 8), :], coef, sems.at[1]),
    ]
    for i, day in enumerate(days):
        copies.append(pltpu.make_async_copy(guess_ref.at[day], guess.at[i], sems.at[2 + i]))
    for copy in copies:
        copy.start()
    copies[0].wait()
    copies[1].wait()
    edge = jnp.where(y == 0, coef[:1, :], coef[7:, :])
    edge = jnp.concatenate([edge[:, i : i + 128] for i in range(0, width, 128)], axis=0)
    outs = []
    for i, ref in enumerate((pair_ref, diag_ref, core_ref, own_ref)):
        copies[2 + i].wait()
        for group in range(rows // 8):
            part = slice(8 * group, 8 * group + 8)
            sea = land[part, :].astype(F32)
            packed[i, :, width * group : width * (group + 1)] = guess[i, part, :] * sea
        packed[i, :, width * (rows // 8) :] = edge
        outs.append(pltpu.make_async_copy(packed.at[i], ref, sems.at[6 + i]))
        outs[-1].start()
    for out in outs:
        out.wait()


def order_kernel(own_ref, core_ref, pair_ref, diag_ref, odd_ref, even_ref):
    size = own_ref.shape[1]
    for i, (own, pair) in enumerate(((own_ref, pair_ref), (core_ref, diag_ref))):
        odd, even = odd_even(own[...], pair[...])
        odd_ref[:, size * i : size * (i + 1)] = odd
        even_ref[:, size * i : size * (i + 1)] = even


def obs_kernel(obs_ref, precision_ref, counts_ref, keep_ref, send_ref):
    _, y, c = place()
    width = obs_ref.shape[2] // 2
    for day, ref in ((y, keep_ref), (1 - y, send_ref)):
        counts = counts_ref[day].astype(F32)
        for half, side in ((0, c), (1, 1 - c)):
            source = pl.ds(pl.multiple_of(side * width, width), width)
            target = pl.ds(half * width, width)
            ref[0, :, target] = obs_ref[day, :, source].astype(F32)
            ref[1, :, target] = counts * precision_ref[day, :, source].astype(F32)


def split(values):
    high = values.astype(BF16)
    return high, (values - high.astype(F32)).astype(BF16)


def banded(kern_ref, offset):
    forward = jnp.zeros(offset.shape, F32)
    adjoint = jnp.zeros(offset.shape, F32)
    for tap in range(TAPS):
        hit = offset == tap
        forward = jnp.where(hit, kern_ref[tap], forward)
        adjoint = jnp.where(hit, kern_ref[TAPS - 1 - tap], adjoint)
    return forward, adjoint


def matrix_kernel(pairs, rows, lat_ref, lon_ref, lat_fwd_ref, lat_adj_ref, lon_fwd_ref, lon_adj_ref):
    k, y, _ = place()
    dims = (2 * rows, 4 * rows)

    even = lax.rem(k, 2) == 0
    out = lax.broadcasted_iota(jnp.int32, dims, 0)
    col = lax.broadcasted_iota(jnp.int32, dims, 1)
    target = rows * jnp.where(y == 0, out // rows, 1 - out // rows) + out % rows
    source = rows * jnp.where(even, col // rows - 1, 2 - col // rows) + col % rows
    offset = source - target + HALF
    odd_open, even_open = open_sides(pairs)
    inside = jnp.where(col < 3 * rows, 1.0, even_open)
    inside = jnp.where(col < rows, odd_open, inside)
    for ref, matrix in zip((lat_fwd_ref, lat_adj_ref), banded(lat_ref, offset)):
        high, low = split(matrix * inside)
        ref[: 2 * rows, : 4 * rows] = high
        ref[: 2 * rows, 4 * rows :] = high
        ref[2 * rows :, : 4 * rows] = low
        ref[2 * rows :, 4 * rows :] = jnp.zeros(dims, BF16)
    dims = (EDGE, EDGE)
    offset = lax.broadcasted_iota(jnp.int32, dims, 0) - lax.broadcasted_iota(jnp.int32, dims, 1)
    for ref in (lon_fwd_ref, lon_adj_ref):
        ref[...] = jnp.zeros(ref.shape, BF16)
    for distance in range(3):
        pair = banded(lon_ref, offset + EDGE * distance - (EDGE - HALF))
        for ref, matrix in zip((lon_fwd_ref, lon_adj_ref), pair):
            for part, piece in enumerate(split(matrix)):
                for column in range(BLOCK // EDGE):
                    row = EDGE * (column + distance)
                    ref[part, row : row + EDGE, EDGE * column : EDGE * (column + 1)] = piece


def load(ref):
    if ref.shape[0] > 8:
        return ref[...]
    size, groups = ref.shape[1] // 2, HALF // 8
    width = (size - 128) // groups
    return jnp.concatenate(
        [
            jnp.concatenate(
                [ref[:, size * half + width * i : size * half + width * (i + 1)] for half in range(2)],
                axis=1,
            )
            for i in range(groups)
        ],
        axis=0,
    )


def edge_row(ref):
    size = ref.shape[1] // 2
    tiles = [ref[:, size * half - 128 : size * half] for half in (1, 2)]
    return jnp.concatenate([tile[i : i + 1, :] for tile in tiles for i in range(8)], axis=1)


def lat_conv(blocks, matrix_ref):
    high, low = split(jnp.concatenate(blocks, axis=0))
    stacked = jnp.concatenate([high, low], axis=0)
    both = jnp.dot(matrix_ref[...], stacked, preferred_element_type=F32)
    half = both.shape[0] // 2
    return both[:half] + both[half:]


def lon_conv(field, matrix_ref):
    rows, length = field.shape
    count = length // BLOCK
    parts = []
    for part in split(field):
        wide = jnp.concatenate([part[:, -EDGE:], part, part[:, :EDGE]], axis=1)
        parts += [wide[:, BLOCK * i : BLOCK * (i + 1) + 2 * EDGE] for i in range(count)]
    coarse = jnp.dot(jnp.concatenate(parts, axis=0), matrix_ref[0], preferred_element_type=F32)
    fine = jnp.dot(
        jnp.concatenate(parts[:count], axis=0), matrix_ref[1], preferred_element_type=F32
    )
    out = coarse[: count * rows] + coarse[count * rows :] + fine
    return jnp.concatenate([out[rows * i : rows * (i + 1)] for i in range(count)], axis=1)


def seen_kernel(*refs):
    fields = [load(ref) for ref in refs[:4]]
    lat_ref, fwd_ref, seen_ref = refs[4:]
    seen_ref[...] = lon_conv(lat_conv(fields, lat_ref), fwd_ref)


def misfit_kernel(seen_ref, keep_ref, sent_ref, adj_ref, odd_ref, even_ref):
    obs = jnp.concatenate([keep_ref[0], sent_ref[0]], axis=0)
    weight = jnp.concatenate([keep_ref[1], sent_ref[1]], axis=0)
    spread = lon_conv(weight * (obs - seen_ref[...]), adj_ref)
    rows = odd_ref.shape[0]
    odd_ref[...], even_ref[...] = odd_even(spread[:rows], spread[rows:])


def beside(center, above, below):
    width = center.shape[1]
    lateral = pltpu.roll(center, 1, 1) + pltpu.roll(center, width - 1, 1)
    return above + below + lateral


def prior_kernel(pairs, *refs):
    fields = [load(ref) for ref in refs[:4]]
    odd_edge, even_edge = edge_row(refs[4]), edge_row(refs[5])
    map_refs = refs[6:10]
    out_ref, ext, wide, inner = refs[10:]
    k, y, _ = place()
    rows, length = fields[0].shape
    even = lax.rem(k, 2) == 0
    odd_open, even_open = open_sides(pairs)
    fields[0] = fields[0] * odd_open
    fields[3] = fields[3] * even_open
    for block, field in enumerate(fields):
        where = rows * jnp.where(even, block, 3 - block)
        ext[pl.ds(pl.multiple_of(where, rows), rows), :] = field
    for block, (left, right) in enumerate((map_refs[:2], map_refs[2:])):
        where = pl.multiple_of(8 + rows * jnp.where(y == 0, block, 1 - block), 8)
        coef = jnp.concatenate([left[0], right[0]], axis=1) + 4.0
        wide[pl.ds(where, rows), :] = coef
    north = jnp.where(even, odd_edge, even_edge) + 4.0
    south = jnp.where(even, even_edge, odd_edge) + 4.0
    wide[:8, :] = jnp.broadcast_to(north, (8, length))
    wide[8 + 2 * rows :, :] = jnp.broadcast_to(south, (8, length))
    low, count = rows - 8, 2 * rows + 16
    center = ext[low : low + count, :]
    around = beside(center, ext[low - 1 : low - 1 + count, :], ext[low + 1 : low + 1 + count, :])
    inner[...] = wide[...] * center - around
    inner[:8, :] = inner[:8, :] * jnp.where(k == 0, 0.0, 1.0)
    inner[8 + 2 * rows :, :] = inner[8 + 2 * rows :, :] * jnp.where(k == pairs - 1, 0.0, 1.0)
    center = inner[8 : 8 + 2 * rows, :]
    around = beside(center, inner[7 : 7 + 2 * rows, :], inner[9 : 9 + 2 * rows, :])
    ext[: 2 * rows, :] = wide[8 : 8 + 2 * rows, :] * center - around
    out_ref[:rows, :] = ext[pl.ds(pl.multiple_of(rows * y, rows), rows), :]
    out_ref[rows:, :] = ext[pl.ds(pl.multiple_of(rows * (1 - y), rows), rows), :]


def adjoint_kernel(*refs):
    refs[5][...] = lat_conv([ref[...] for ref in refs[:4]], refs[4])


def update_kernel(final, *refs):
    back_ref, prior_ref, left, right, pair_left, pair_right = refs[:6]
    last = back_ref[...] - prior_ref[...]
    rows, length = last.shape[0] // 2, last.shape[1]
    width = length // 2
    last_own = last[:rows] * jnp.concatenate([left[1], right[1]], axis=1)
    last_pair = last[rows:] * jnp.concatenate([pair_left[1], pair_right[1]], axis=1)
    outs = refs[-4:] if final else refs[-6:]
    outs[0][...] = last_own[:, :width]
    outs[1][...] = last_own[:, width:]
    outs[2][...] = last_pair[:, :width]
    outs[3][...] = last_pair[:, width:]
    if not final:
        odd, even = odd_even(last_own, last_pair)
        outs[4][...] = load(refs[6]) + odd * (1.0 / THETA)
        outs[5][...] = load(refs[7]) + even * (1.0 / THETA)


def final_kernel(*refs):
    early, late = refs[:4], refs[4:8]
    guess_ref, land_ref, state_ref, last_ref = refs[8:]
    _, y, c = place()
    land = 1.0 - land_ref[...].astype(F32)
    days = (2 * c + y, 2 * (1 - c) + y, 2 * c + (1 - y), 2 * (1 - c) + (1 - y))
    for day, early_ref, late_ref in zip(days, early, late):
        guess = guess_ref[day]
        update = (early_ref[...] - land * guess) * (1.0 / THETA)
        state = guess + update
        last = late_ref[...] - land * state
        update = (NEW_RHO * RHO) * update + (2.0 * NEW_RHO / DELTA) * last
        state_ref[day] = state + update
        last_ref[day] = last


def body(
    pairs,
    first_guess,
    range_coef,
    land_sea,
    lat_kernel,
    lon_kernel,
    observations,
    obs_precision,
    track_counts,
):
    days, rows, width = first_guess.shape
    length = observations.shape[2]
    assert days == 4 and rows == HALF and length == 2 * width and length % BLOCK == 0
    assert width == 8 * 128
    places = [(k, y, c) for k in range(pairs) for y in range(2) for c in range(2)]

    def permute(array, move):
        moves = [(i, places.index(move(*at))) for i, at in enumerate(places)]
        return lax.ppermute(array, AXES, moves)

    def swap(k, y, c, parity):
        target = k + 1 if k % 2 == parity else k - 1
        return (target, y, c) if 0 <= target < pairs else (k, y, 1 - c)

    core = lambda array: permute(array, lambda k, y, c: (k, y, 1 - c))
    pair = lambda array: permute(array, lambda k, y, c: (k, 1 - y, c))
    diag = lambda array: permute(array, lambda k, y, c: (k, 1 - y, 1 - c))
    odd = lambda array: permute(array, lambda k, y, c: swap(k, y, c, 1))
    even = lambda array: permute(array, lambda k, y, c: swap(k, y, c, 0))

    piece = shape(rows, width)
    packed = shape(8, rows // 8 * width + 128)
    band = shape(rows, length)
    own, to_core, to_pair, to_diag = call(
        pack_kernel,
        [packed] * 4,
        [first_guess, land_sea, range_coef],
        [HBM] * 3,
        scratch=[
            pltpu.VMEM((4, rows, width), F32),
            pltpu.VMEM((rows, width), jnp.int32),
            pltpu.VMEM((8, width), F32),
            pltpu.VMEM((4,) + packed.shape, F32),
            pltpu.SemaphoreType.DMA((10,)),
        ],
        outs=[HBM] * 4,
        vmem=PACK_VMEM,
        name="pack",
    )
    by_pair, by_diag = pair(to_pair), diag(to_diag)
    keep, send = call(
        obs_kernel,
        [shape(2, rows, length)] * 2,
        [observations, obs_precision, track_counts[:, :, None]],
        name="observed",
    )
    lat_fwd, lat_adj, lon_fwd, lon_adj = call(
        functools.partial(matrix_kernel, pairs, rows),
        [shape(4 * rows, 8 * rows, dtype=BF16)] * 2
        + [shape(2, BLOCK + 2 * EDGE, BLOCK, dtype=BF16)] * 2,
        [lat_kernel, lon_kernel],
        [SMEM, SMEM],
        flops=4 * 65 * 2 * 70000,
        name="matrices",
    )
    to_core, lat_fwd = lax.optimization_barrier((to_core, lat_fwd))
    by_core = core(to_core)
    maps = jnp.stack([range_coef, land_sea.astype(F32)])

    send, by_pair, by_diag = lax.optimization_barrier((send, by_pair, by_diag))
    v_odd, v_even = call(
        order_kernel,
        [shape(8, 2 * packed.shape[1])] * 2,
        [own, by_core, by_pair, by_diag],
        name="order",
    )
    fields = [odd(v_odd), v_odd, v_even, even(v_even)]
    edges = [fields[0], fields[3]]
    sent = pair(send)
    conv = 2 * 3 * 2 * rows * length * 512
    maps_core = core(maps)

    pieces = []
    for step in range(2):
        (seen,) = call(
            seen_kernel,
            [shape(2 * rows, length)],
            fields + [lat_fwd, lon_fwd],
            flops=2 * conv,
            name="seen",
        )
        m_odd, m_even = call(
            misfit_kernel, [band] * 2, [seen, keep, sent, lon_adj], flops=conv, name="misfit"
        )
        if not step:
            maps, m_odd, m_even = lax.optimization_barrier((maps, m_odd, m_even))
            maps_pair = pair(maps)
            maps = [maps, maps_core, maps_pair, core(maps_pair)]
        (back,) = call(
            adjoint_kernel,
            [shape(2 * rows, length)],
            [odd(m_odd), m_odd, m_even, even(m_even), lat_adj],
            flops=ADJOINT_COST,
            name="adjoint",
        )
        (prior,) = call(
            functools.partial(prior_kernel, pairs),
            [shape(2 * rows, length)],
            fields + edges + maps,
            scratch=[
                pltpu.VMEM((4 * rows, length), F32),
                pltpu.VMEM((2 * rows + 16, length), F32),
                pltpu.VMEM((2 * rows + 16, length), F32),
            ],
            name="prior",
        )
        outs = call(
            functools.partial(update_kernel, step == 1),
            [piece] * 4 + ([] if step else [band] * 2),
            [back, prior] + maps + ([] if step else [v_odd, v_even]),
            name="update",
        )
        pieces += [outs[0], core(outs[1]), pair(outs[2]), diag(outs[3])]
        if not step:
            fields = [odd(outs[4]), outs[4], outs[5], even(outs[5])]
    state, last = call(
        final_kernel,
        [shape(days, rows, width)] * 2,
        pieces + [first_guess, land_sea],
        name="final",
    )
    return state, last


def solution(mesh):
    assert mesh.shape["lat"] % 2 == 0 and mesh.shape["lon"] == 2
    in_specs = (
        P(None, ("groups", "lat"), "lon"),
        P(("groups", "lat"), "lon"),
        P(("groups", "lat"), "lon"),
        P(),
        P(),
        P("lon", ("groups", "lat"), None),
        P("lon", ("groups", "lat"), None),
        P("lon", ("groups", "lat")),
    )
    out_specs = (P(None, ("groups", "lat"), "lon"), P(None, ("groups", "lat"), "lon"))
    return jax.shard_map(
        functools.partial(body, mesh.shape["lat"] // 2),
        mesh=mesh,
        in_specs=in_specs,
        out_specs=out_specs,
        check_vma=False,
    )
```

time: 97.9 us -> 68.4 us (0.70)
  starting transfers between devices: 42.9 us -> 21.6 us
  waiting for transfers between devices: 40 us -> 33.7 us
  local copies, waits for them, and re-layouts: 2.74 us -> 0.56 us
    ppermute x25 -> x21, starting transfers between devices: 42.9 us -> 21.6 us  [permute(): return lax.ppermute(array, AXES, moves)]
    ppermute x25 -> x21, waiting for transfers between devices: 40 us -> 33.7 us  [permute(): return lax.ppermute(array, AXES, moves)]
    unnamed x20, local copies, waits for them, and re-layouts: 2.65 us -> 0.47 us
    pallas_call x11 -> x15, Pallas kernels: 10.8 us -> 11.5 us  [call(): pl.pallas_call(kernel, out_shape=out_shape, in_specs=specs or [VMEM] * le...]
  transfers between devices with their start and end apart: 25 -> 21, of which waited for: 10 -> 10; matrix products, arithmetic and copies ran while one was open for 0% -> 0% of each run, Pallas kernels for 7% -> 7%
where the time goes in v1:
time: 68.4 us; the launch traced here: 68.3 us
  waiting for transfers between devices  33.7 us (49%)
  starting transfers between devices  21.6 us (32%)
  Pallas kernels  11.5 us (17%)
  between operations  0.89 us (1%)
    ppermute x21, waiting for transfers between devices, permute(): return lax.ppermute(array, AXES, moves)  33.7 us
    ppermute x21, starting transfers between devices, permute(): return lax.ppermute(array, AXES, moves)  21.6 us
    pallas_call x15, Pallas kernels, call(): pl.pallas_call(kernel, out_shape=out_shape, in_specs=specs or [VMEM] * le...  11.5 us
  transfers between devices with their start and end apart: 21, of which 10 were waited for; matrix products, arithmetic and copies ran while one was open for 0% of the time, Pallas kernels for 7%

profile of v1, /device:TPU:0, one launch (start us, length us, event | category | flops | bytes accessed | tf_op | source)
XLA Modules:
  0.0 68.3 jit_solution(7397405093433702753)
XLA Ops:
  0.6 2.0 %pack.1 = (f32[8,4224]{1,0:T(8,128)}, f32[8,4224]{1,0:T(8,128)}, f32[8,4224]{1,0:T(8,128)}, f32[8,4224]{1,0:T(8,128)}) custom-call(f32[4,32,1024]{2,1,0:T(8,128)} %refs_8_.1, s32[32,1024]{1,0:T(8,128)} %refs_9_.1, f32[32,1024]{1,0:T(8,128)} %coef_ref.1), custom_call_target="tpu_custom_call" | custom-call | bytes 1327104 | tf_op jit(solution)/shard_map/pack/pallas_call | solution.py:59
  2.7 3.0 %collective-permute-start.1 = (f32[8,4224]{1,0:T(8,128)}, f32[8,4224]{1,0:T(8,128)S(1)}, u32[]{:S(2)}, u32[]{:S(2)}) collective-permute-start(f32[8,4224]{1,0:T(8,128)} %get-tuple-element.41), channel_id=1, source_target_pairs={{0,2},{1,3},{2,0},{3,1},{4,6},{5,7},{6,4},{7,5},{8,10},{9,11},{10,... | collective-permute-start | bytes 405512 | tf_op jit(solution)/shard_map/ppermute | solution.py:328
  5.7 2.1 %matrices.1 = (bf16[128,256]{1,0:T(8,128)(2,1)S(1)}, bf16[128,256]{1,0:T(8,128)(2,1)S(1)}, bf16[2,512,256]{2,1,0:T(8,128)(2,1)S(1)}, bf16[2,512,256]{2,1,0:T(8,128)(2,1)S(1)}) custom-call(f32[65]{0:T(128)S(1)} %copy-done.5, f32[65]{0:T(128)S(1)} %copy-done.6), custom_call_target="tpu_custom_call" | custom-call | flops 36400000 | bytes 1180168 | tf_op jit(solution)/shard_map/matrices/pallas_call | solution.py:59
  8.8 1.3 %collective-permute-done.1.pair_ref = f32[8,4224]{1,0:T(8,128)S(1)} collective-permute-done((f32[8,4224]{1,0:T(8,128)}, f32[8,4224]{1,0:T(8,128)S(1)}, u32[]{:S(2)}, u32[]{:S(2)}) %collective-permute-start.1) | collective-permute-done | bytes 135200 | tf_op jit(solution)/shard_map/ppermute | solution.py:328
  10.0 1.8 %collective-permute-done.2.diag_ref = f32[8,4224]{1,0:T(8,128)S(1)} collective-permute-done((f32[8,4224]{1,0:T(8,128)}, f32[8,4224]{1,0:T(8,128)S(1)}, u32[]{:S(2)}, u32[]{:S(2)}) %collective-permute-start.2) | collective-permute-done | bytes 135200 | tf_op jit(solution)/shard_map/ppermute | solution.py:328
  11.9 1.1 %collective-permute-start.5 = (f32[2,32,2048]{2,1,0:T(8,128)S(1)}, f32[2,32,2048]{2,1,0:T(8,128)S(1)}, u32[]{:S(2)}, u32[]{:S(2)}) collective-permute-start(f32[2,32,2048]{2,1,0:T(8,128)S(1)} %get-tuple-element.50), channel_id=1, source_target_pairs={{0,2},{1,3},{2,0},{3,1},{4,6},{5,7},{6,4},{7,5},{8,10},{9,11},{10,... | collective-permute-start | bytes 1572872 | tf_op jit(solution)/shard_map/ppermute | solution.py:328
  13.8 2.5 %collective-permute-start.4 = (f32[8,8448]{1,0:T(8,128)S(1)}, f32[8,8448]{1,0:T(8,128)S(1)}, u32[]{:S(2)}, u32[]{:S(2)}) collective-permute-start(f32[8,8448]{1,0:T(8,128)S(1)} %get-tuple-element.46.refs_2_.refs_7_), channel_id=1, source_target_pairs={{0,4},{1,5},{2,6},{3,7},{4,0},{5,1},{6,2},{7,3},{8,12},{9,13},{10,... | collective-permute-start | bytes 811016 | tf_op jit(solution)/shard_map/ppermute | solution.py:328
  16.4 7.0 %collective-permute-done.4.refs_3_.refs_5_ = f32[8,8448]{1,0:T(8,128)S(1)} collective-permute-done((f32[8,8448]{1,0:T(8,128)S(1)}, f32[8,8448]{1,0:T(8,128)S(1)}, u32[]{:S(2)}, u32[]{:S(2)}) %collective-permute-start.4) | collective-permute-done | bytes 270368 | tf_op jit(solution)/shard_map/ppermute | solution.py:328
  24.2 1.9 %collective-permute-done.5.sent_ref = f32[2,32,2048]{2,1,0:T(8,128)S(1)} collective-permute-done((f32[2,32,2048]{2,1,0:T(8,128)S(1)}, f32[2,32,2048]{2,1,0:T(8,128)S(1)}, u32[]{:S(2)}, u32[]{:S(2)}) %collective-permute-start.5) | collective-permute-done | bytes 524320 | tf_op jit(solution)/shard_map/ppermute | solution.py:328
  26.6 1.8 %collective-permute-start.9 = (f32[2,32,1024]{2,1,0:T(8,128)S(1)}, f32[2,32,1024]{2,1,0:T(8,128)S(1)}, u32[]{:S(2)}, u32[]{:S(2)}) collective-permute-start(f32[2,32,1024]{2,1,0:T(8,128)S(1)} %pad_maximum_fusion.refs_6_.refs_2_), channel_id=1, source_target_pairs={{0,2},{1,3},{2,0},{3,1},{4,6},{5,7},{6,4},{7,5},{8,10},{9,11},{10,... | collective-permute-start | bytes 786440 | tf_op jit(solution)/shard_map/ppermute | solution.py:328
  28.4 3.1 %collective-permute-start.7 = (f32[32,2048]{1,0:T(8,128)S(1)}, f32[32,2048]{1,0:T(8,128)S(1)}, u32[]{:S(2)}, u32[]{:S(2)}) collective-permute-start(f32[32,2048]{1,0:T(8,128)S(1)} %get-tuple-element.55.refs_2_), channel_id=1, source_target_pairs={{0,4},{1,5},{2,6},{3,7},{4,0},{5,1},{6,2},{7,3},{8,12},{9,13},{10,... | collective-permute-start | bytes 786440 | tf_op jit(solution)/shard_map/ppermute | solution.py:328
  31.6 3.4 %collective-permute-done.9.refs_8_.refs_4_ = f32[2,32,1024]{2,1,0:T(8,128)S(1)} collective-permute-done((f32[2,32,1024]{2,1,0:T(8,128)S(1)}, f32[2,32,1024]{2,1,0:T(8,128)S(1)}, u32[]{:S(2)}, u32[]{:S(2)}) %collective-permute-start.9) | collective-permute-done | bytes 262176 | tf_op jit(solution)/shard_map/ppermute | solution.py:328
  35.0 2.6 %collective-permute-done.7.refs_3_ = f32[32,2048]{1,0:T(8,128)S(1)} collective-permute-done((f32[32,2048]{1,0:T(8,128)S(1)}, f32[32,2048]{1,0:T(8,128)S(1)}, u32[]{:S(2)}, u32[]{:S(2)}) %collective-permute-start.7) | collective-permute-done | bytes 262176 | tf_op jit(solution)/shard_map/ppermute | solution.py:328
  38.0 1.2 %prior.2.refs_1_ = f32[64,2048]{1,0:T(8,128)S(1)} custom-call(f32[8,8448]{1,0:T(8,128)S(1)} %collective-permute-done.3.refs_0_.refs_4_, f32[8,8448]{1,0:T(8,128)S(1)} %get-tuple-element.45.refs_1_.refs_6_, f32[8,8448]{1,0:T(8,128)S(1)} %get-tuple-element.46.refs_2_.refs_7_, f32[8,8448]{1,0:T(8,128)S(1)} %collective-permute-done.4.refs_3_.refs_5_, ...), custom_call_target="tpu_custom_call" | custom-call | bytes 3194880 | tf_op jit(solution)/shard_map/prior/pallas_call | solution.py:59
  39.4 2.5 %collective-permute-start.15 = (f32[32,2048]{1,0:T(8,128)S(1)}, f32[32,2048]{1,0:T(8,128)S(1)}, u32[]{:S(2)}, u32[]{:S(2)}) collective-permute-start(f32[32,2048]{1,0:T(8,128)S(1)} %get-tuple-element.63.refs_2_), channel_id=1, source_target_pairs={{0,4},{1,5},{2,6},{3,7},{4,0},{5,1},{6,2},{7,3},{8,12},{9,13},{10,... | collective-permute-start | bytes 786440 | tf_op jit(solution)/shard_map/ppermute | solution.py:328
  41.9 6.2 %collective-permute-done.15.refs_3_ = f32[32,2048]{1,0:T(8,128)S(1)} collective-permute-done((f32[32,2048]{1,0:T(8,128)S(1)}, f32[32,2048]{1,0:T(8,128)S(1)}, u32[]{:S(2)}, u32[]{:S(2)}) %collective-permute-start.15) | collective-permute-done | bytes 262176 | tf_op jit(solution)/shard_map/ppermute | solution.py:328
  49.6 2.5 %collective-permute-start.17 = (f32[32,2048]{1,0:T(8,128)S(1)}, f32[32,2048]{1,0:T(8,128)S(1)}, u32[]{:S(2)}, u32[]{:S(2)}) collective-permute-start(f32[32,2048]{1,0:T(8,128)S(1)} %get-tuple-element.65.refs_2_), channel_id=1, source_target_pairs={{0,4},{1,5},{2,6},{3,7},{4,0},{5,1},{6,2},{7,3},{8,12},{9,13},{10,... | collective-permute-start | bytes 786440 | tf_op jit(solution)/shard_map/ppermute | solution.py:328
  52.9 1.1 %collective-permute-start.13 = (f32[32,1024]{1,0:T(8,128)S(1)}, f32[32,1024]{1,0:T(8,128)S(1)}, u32[]{:S(2)}, u32[]{:S(2)}) collective-permute-start(f32[32,1024]{1,0:T(8,128)S(1)} %get-tuple-element.61), channel_id=1, source_target_pairs={{0,3},{1,2},{2,1},{3,0},{4,7},{5,6},{6,5},{7,4},{8,11},{9,10},{10,... | collective-permute-start | bytes 393224 | tf_op jit(solution)/shard_map/ppermute | solution.py:328
  54.0 1.2 %prior.3.refs_1_ = f32[64,2048]{1,0:T(8,128)S(1)} custom-call(f32[32,2048]{1,0:T(8,128)S(1)} %collective-permute-done.14.refs_0_, f32[32,2048]{1,0:T(8,128)S(1)} %get-tuple-element.62.refs_1_, f32[32,2048]{1,0:T(8,128)S(1)} %get-tuple-element.63.refs_2_, f32[32,2048]{1,0:T(8,128)S(1)} %collective-permute-done.15.refs_3_, ...), custom_call_target="tpu_custom_call" | custom-call | bytes 3162112 | tf_op jit(solution)/shard_map/prior/pallas_call | solution.py:59
  55.2 3.2 %collective-permute-done.17.refs_3_ = f32[32,2048]{1,0:T(8,128)S(1)} collective-permute-done((f32[32,2048]{1,0:T(8,128)S(1)}, f32[32,2048]{1,0:T(8,128)S(1)}, u32[]{:S(2)}, u32[]{:S(2)}) %collective-permute-start.17) | collective-permute-done | bytes 262176 | tf_op jit(solution)/shard_map/ppermute | solution.py:328
  58.8 1.2 %collective-permute-start.19 = (f32[32,1024]{1,0:T(8,128)S(1)}, f32[32,1024]{1,0:T(8,128)S(1)}, u32[]{:S(2)}, u32[]{:S(2)}) collective-permute-start(f32[32,1024]{1,0:T(8,128)S(1)} %get-tuple-element.68), channel_id=1, source_target_pairs={{0,2},{1,3},{2,0},{3,1},{4,6},{5,7},{6,4},{7,5},{8,10},{9,11},{10,... | collective-permute-start | bytes 393224 | tf_op jit(solution)/shard_map/ppermute | solution.py:328
  60.7 4.5 %collective-permute-done.19.refs_6_ = f32[32,1024]{1,0:T(8,128)S(1)} collective-permute-done((f32[32,1024]{1,0:T(8,128)S(1)}, f32[32,1024]{1,0:T(8,128)S(1)}, u32[]{:S(2)}, u32[]{:S(2)}) %collective-permute-start.19) | collective-permute-done | bytes 131104 | tf_op jit(solution)/shard_map/ppermute | solution.py:328
  65.2 1.9 %collective-permute-done.20.refs_7_ = f32[32,1024]{1,0:T(8,128)S(1)} collective-permute-done((f32[32,1024]{1,0:T(8,128)S(1)}, f32[32,1024]{1,0:T(8,128)S(1)}, u32[]{:S(2)}, u32[]{:S(2)}) %collective-permute-start.20) | collective-permute-done | bytes 131104 | tf_op jit(solution)/shard_map/ppermute | solution.py:328
  67.1 1.2 %final.1 = (f32[4,32,1024]{2,1,0:T(8,128)}, f32[4,32,1024]{2,1,0:T(8,128)}) custom-call(f32[32,1024]{1,0:T(8,128)S(1)} %get-tuple-element.58.refs_0_, f32[32,1024]{1,0:T(8,128)S(1)} %collective-permute-done.11.refs_1_, f32[32,1024]{1,0:T(8,128)S(1)} %collective-permute-done.12.refs_2_, f32[32,1024]{1,0:T(8,128)S(1)} %collective-permute-done.13.refs_3_, ...), custom_call_target="tpu_custom_call" | custom-call | bytes 2752512 | tf_op jit(solution)/shard_map/final/pallas_call | solution.py:59
  (56 shorter events, 7.2 us)
Async XLA Ops:
  0.6 8.0 %copy-start.2 = (bf16[2,32,2048]{2,1,0:T(8,128)(2,1)S(1)}, bf16[2,32,2048]{2,1,0:T(8,128)(2,1)}, u32[]{:S(2)}) copy-start(bf16[2,32,2048]{2,1,0:T(8,128)(2,1)} %obs_ref.1) | copy-start | bytes 786436
  0.6 8.0 %copy-start.3 = (bf16[2,32,2048]{2,1,0:T(8,128)(2,1)S(1)}, bf16[2,32,2048]{2,1,0:T(8,128)(2,1)}, u32[]{:S(2)}) copy-start(bf16[2,32,2048]{2,1,0:T(8,128)(2,1)} %precision_ref.1) | copy-start | bytes 786436
  2.7 7.4 %collective-permute-start.1 = (f32[8,4224]{1,0:T(8,128)}, f32[8,4224]{1,0:T(8,128)S(1)}, u32[]{:S(2)}, u32[]{:S(2)}) collective-permute-start(f32[8,4224]{1,0:T(8,128)} %get-tuple-element.41), channel_id=1, source_target_pairs={{0,2},{1,3},{2,0},{3,1},{4,6},{5,7},{6,4},{7,5},{8,10},{9,11},{10,... | collective-permute-start | bytes 405512 | tf_op jit(solution)/shard_map/ppermute | solution.py:328
  5.7 6.2 %collective-permute-start.2 = (f32[8,4224]{1,0:T(8,128)}, f32[8,4224]{1,0:T(8,128)S(1)}, u32[]{:S(2)}, u32[]{:S(2)}) collective-permute-start(f32[8,4224]{1,0:T(8,128)} %get-tuple-element.42), channel_id=1, source_target_pairs={{0,3},{1,2},{2,1},{3,0},{4,7},{5,6},{6,5},{7,4},{8,11},{9,10},{10,... | collective-permute-start | bytes 405512 | tf_op jit(solution)/shard_map/ppermute | solution.py:328
  7.9 5.1 %collective-permute-start = (f32[8,4224]{1,0:T(8,128)S(1)}, f32[8,4224]{1,0:T(8,128)S(1)}, u32[]{:S(2)}, u32[]{:S(2)}) collective-permute-start(f32[8,4224]{1,0:T(8,128)S(1)} %copy-done.9), channel_id=1, source_target_pairs={{0,1},{1,0},{2,3},{3,2},{4,5},{5,4},{6,7},{7,6},{8,9},{9,8},{10,11... | collective-permute-start | bytes 405512 | tf_op jit(solution)/shard_map/ppermute | solution.py:328
  11.9 14.2 %collective-permute-start.5 = (f32[2,32,2048]{2,1,0:T(8,128)S(1)}, f32[2,32,2048]{2,1,0:T(8,128)S(1)}, u32[]{:S(2)}, u32[]{:S(2)}) collective-permute-start(f32[2,32,2048]{2,1,0:T(8,128)S(1)} %get-tuple-element.50), channel_id=1, source_target_pairs={{0,2},{1,3},{2,0},{3,1},{4,6},{5,7},{6,4},{7,5},{8,10},{9,11},{10,... | collective-permute-start | bytes 1572872 | tf_op jit(solution)/shard_map/ppermute | solution.py:328
  13.1 3.3 %collective-permute-start.3 = (f32[8,8448]{1,0:T(8,128)S(1)}, f32[8,8448]{1,0:T(8,128)S(1)}, u32[]{:S(2)}, u32[]{:S(2)}) collective-permute-start(f32[8,8448]{1,0:T(8,128)S(1)} %get-tuple-element.45.refs_1_.refs_6_), channel_id=1, source_target_pairs={{0,1},{1,0},{2,3},{3,2},{4,8},{5,9},{6,10},{7,11},{8,4},{9,5},{10,... | collective-permute-start | bytes 811016 | tf_op jit(solution)/shard_map/ppermute | solution.py:328
  13.8 9.5 %collective-permute-start.4 = (f32[8,8448]{1,0:T(8,128)S(1)}, f32[8,8448]{1,0:T(8,128)S(1)}, u32[]{:S(2)}, u32[]{:S(2)}) collective-permute-start(f32[8,8448]{1,0:T(8,128)S(1)} %get-tuple-element.46.refs_2_.refs_7_), channel_id=1, source_target_pairs={{0,4},{1,5},{2,6},{3,7},{4,0},{5,1},{6,2},{7,3},{8,12},{9,13},{10,... | collective-permute-start | bytes 811016 | tf_op jit(solution)/shard_map/ppermute | solution.py:328
  26.6 8.4 %collective-permute-start.9 = (f32[2,32,1024]{2,1,0:T(8,128)S(1)}, f32[2,32,1024]{2,1,0:T(8,128)S(1)}, u32[]{:S(2)}, u32[]{:S(2)}) collective-permute-start(f32[2,32,1024]{2,1,0:T(8,128)S(1)} %pad_maximum_fusion.refs_6_.refs_2_), channel_id=1, source_target_pairs={{0,2},{1,3},{2,0},{3,1},{4,6},{5,7},{6,4},{7,5},{8,10},{9,11},{10,... | collective-permute-start | bytes 786440 | tf_op jit(solution)/shard_map/ppermute | solution.py:328
  28.4 6.6 %collective-permute-start.6 = (f32[32,2048]{1,0:T(8,128)S(1)}, f32[32,2048]{1,0:T(8,128)S(1)}, u32[]{:S(2)}, u32[]{:S(2)}) collective-permute-start(f32[32,2048]{1,0:T(8,128)S(1)} %get-tuple-element.54.refs_1_), channel_id=1, source_target_pairs={{0,1},{1,0},{2,3},{3,2},{4,8},{5,9},{6,10},{7,11},{8,4},{9,5},{10,... | collective-permute-start | bytes 786440 | tf_op jit(solution)/shard_map/ppermute | solution.py:328
  28.4 9.2 %collective-permute-start.7 = (f32[32,2048]{1,0:T(8,128)S(1)}, f32[32,2048]{1,0:T(8,128)S(1)}, u32[]{:S(2)}, u32[]{:S(2)}) collective-permute-start(f32[32,2048]{1,0:T(8,128)S(1)} %get-tuple-element.55.refs_2_), channel_id=1, source_target_pairs={{0,4},{1,5},{2,6},{3,7},{4,0},{5,1},{6,2},{7,3},{8,12},{9,13},{10,... | collective-permute-start | bytes 786440 | tf_op jit(solution)/shard_map/ppermute | solution.py:328
  31.6 6.3 %collective-permute-start.8 = (f32[2,32,1024]{2,1,0:T(8,128)S(1)}, f32[2,32,1024]{2,1,0:T(8,128)S(1)}, u32[]{:S(2)}, u32[]{:S(2)}) collective-permute-start(f32[2,32,1024]{2,1,0:T(8,128)S(1)} %pad_maximum_fusion.refs_6_.refs_2_), channel_id=1, source_target_pairs={{0,1},{1,0},{2,3},{3,2},{4,5},{5,4},{6,7},{7,6},{8,9},{9,8},{10,11... | collective-permute-start | bytes 786440 | tf_op jit(solution)/shard_map/ppermute | solution.py:328
  35.0 2.9 %collective-permute-start.10 = (f32[2,32,1024]{2,1,0:T(8,128)S(1)}, f32[2,32,1024]{2,1,0:T(8,128)S(1)}, u32[]{:S(2)}, u32[]{:S(2)}) collective-permute-start(f32[2,32,1024]{2,1,0:T(8,128)S(1)} %collective-permute-done.9.refs_8_.refs_4_), channel_id=1, source_target_pairs={{0,1},{1,0},{2,3},{3,2},{4,5},{5,4},{6,7},{7,6},{8,9},{9,8},{10,11... | collective-permute-start | bytes 786440 | tf_op jit(solution)/shard_map/ppermute | solution.py:328
  39.3 2.6 %collective-permute-start.14 = (f32[32,2048]{1,0:T(8,128)S(1)}, f32[32,2048]{1,0:T(8,128)S(1)}, u32[]{:S(2)}, u32[]{:S(2)}) collective-permute-start(f32[32,2048]{1,0:T(8,128)S(1)} %get-tuple-element.62.refs_1_), channel_id=1, source_target_pairs={{0,1},{1,0},{2,3},{3,2},{4,8},{5,9},{6,10},{7,11},{8,4},{9,5},{10,... | collective-permute-start | bytes 786440 | tf_op jit(solution)/shard_map/ppermute | solution.py:328
  39.4 8.7 %collective-permute-start.15 = (f32[32,2048]{1,0:T(8,128)S(1)}, f32[32,2048]{1,0:T(8,128)S(1)}, u32[]{:S(2)}, u32[]{:S(2)}) collective-permute-start(f32[32,2048]{1,0:T(8,128)S(1)} %get-tuple-element.63.refs_2_), channel_id=1, source_target_pairs={{0,4},{1,5},{2,6},{3,7},{4,0},{5,1},{6,2},{7,3},{8,12},{9,13},{10,... | collective-permute-start | bytes 786440 | tf_op jit(solution)/shard_map/ppermute | solution.py:328
  49.5 5.6 %collective-permute-start.16 = (f32[32,2048]{1,0:T(8,128)S(1)}, f32[32,2048]{1,0:T(8,128)S(1)}, u32[]{:S(2)}, u32[]{:S(2)}) collective-permute-start(f32[32,2048]{1,0:T(8,128)S(1)} %get-tuple-element.64.refs_1_), channel_id=1, source_target_pairs={{0,1},{1,0},{2,3},{3,2},{4,8},{5,9},{6,10},{7,11},{8,4},{9,5},{10,... | collective-permute-start | bytes 786440 | tf_op jit(solution)/shard_map/ppermute | solution.py:328
  49.6 8.7 %collective-permute-start.17 = (f32[32,2048]{1,0:T(8,128)S(1)}, f32[32,2048]{1,0:T(8,128)S(1)}, u32[]{:S(2)}, u32[]{:S(2)}) collective-permute-start(f32[32,2048]{1,0:T(8,128)S(1)} %get-tuple-element.65.refs_2_), channel_id=1, source_target_pairs={{0,4},{1,5},{2,6},{3,7},{4,0},{5,1},{6,2},{7,3},{8,12},{9,13},{10,... | collective-permute-start | bytes 786440 | tf_op jit(solution)/shard_map/ppermute | solution.py:328
  52.1 7.9 %collective-permute-start.11 = (f32[32,1024]{1,0:T(8,128)S(1)}, f32[32,1024]{1,0:T(8,128)S(1)}, u32[]{:S(2)}, u32[]{:S(2)}) collective-permute-start(f32[32,1024]{1,0:T(8,128)S(1)} %get-tuple-element.59), channel_id=1, source_target_pairs={{0,1},{1,0},{2,3},{3,2},{4,5},{5,4},{6,7},{7,6},{8,9},{9,8},{10,11... | collective-permute-start | bytes 393224 | tf_op jit(solution)/shard_map/ppermute | solution.py:328
  52.1 8.6 %collective-permute-start.12 = (f32[32,1024]{1,0:T(8,128)S(1)}, f32[32,1024]{1,0:T(8,128)S(1)}, u32[]{:S(2)}, u32[]{:S(2)}) collective-permute-start(f32[32,1024]{1,0:T(8,128)S(1)} %get-tuple-element.60), channel_id=1, source_target_pairs={{0,2},{1,3},{2,0},{3,1},{4,6},{5,7},{6,4},{7,5},{8,10},{9,11},{10,... | collective-permute-start | bytes 393224 | tf_op jit(solution)/shard_map/ppermute | solution.py:328
  52.9 7.8 %collective-permute-start.13 = (f32[32,1024]{1,0:T(8,128)S(1)}, f32[32,1024]{1,0:T(8,128)S(1)}, u32[]{:S(2)}, u32[]{:S(2)}) collective-permute-start(f32[32,1024]{1,0:T(8,128)S(1)} %get-tuple-element.61), channel_id=1, source_target_pairs={{0,3},{1,2},{2,1},{3,0},{4,7},{5,6},{6,5},{7,4},{8,11},{9,10},{10,... | collective-permute-start | bytes 393224 | tf_op jit(solution)/shard_map/ppermute | solution.py:328
  58.7 8.4 %copy-start = (f32[4,32,1024]{2,1,0:T(8,128)S(1)}, f32[4,32,1024]{2,1,0:T(8,128)}, u32[]{:S(2)}) copy-start(f32[4,32,1024]{2,1,0:T(8,128)} %refs_8_.1) | copy-start | bytes 1572868
  58.8 2.0 %collective-permute-start.18 = (f32[32,1024]{1,0:T(8,128)S(1)}, f32[32,1024]{1,0:T(8,128)S(1)}, u32[]{:S(2)}, u32[]{:S(2)}) collective-permute-start(f32[32,1024]{1,0:T(8,128)S(1)} %get-tuple-element.67), channel_id=1, source_target_pairs={{0,1},{1,0},{2,3},{3,2},{4,5},{5,4},{6,7},{7,6},{8,9},{9,8},{10,11... | collective-permute-start | bytes 393224 | tf_op jit(solution)/shard_map/ppermute | solution.py:328
  58.8 6.4 %collective-permute-start.19 = (f32[32,1024]{1,0:T(8,128)S(1)}, f32[32,1024]{1,0:T(8,128)S(1)}, u32[]{:S(2)}, u32[]{:S(2)}) collective-permute-start(f32[32,1024]{1,0:T(8,128)S(1)} %get-tuple-element.68), channel_id=1, source_target_pairs={{0,2},{1,3},{2,0},{3,1},{4,6},{5,7},{6,4},{7,5},{8,10},{9,11},{10,... | collective-permute-start | bytes 393224 | tf_op jit(solution)/shard_map/ppermute | solution.py:328
  60.0 7.1 %collective-permute-start.20 = (f32[32,1024]{1,0:T(8,128)S(1)}, f32[32,1024]{1,0:T(8,128)S(1)}, u32[]{:S(2)}, u32[]{:S(2)}) collective-permute-start(f32[32,1024]{1,0:T(8,128)S(1)} %get-tuple-element.69), channel_id=1, source_target_pairs={{0,3},{1,2},{2,1},{3,0},{4,7},{5,6},{6,5},{7,4},{8,11},{9,10},{10,... | collective-permute-start | bytes 393224 | tf_op jit(solution)/shard_map/ppermute | solution.py:328
  (7 other events, 22.1 us)

commit v2 on v1

--- a/solution.py
+++ b/solution.py
@@ -18,6 +18,7 @@
 NEW_RHO = 1.0 / (2.0 * SIGMA - RHO)
 BLOCK = 256
 EDGE = 128
+LEFT_COST = 5 * 10**9
 ADJOINT_COST = 2 * 10**10
 PACK_VMEM = 62 * 2**20
 AXES = ("lat", "lon")
@@ -52,20 +53,20 @@
 
 
 def call(
-    kernel, out_shape, args, specs=None, outs=None, scratch=(), flops=0, vmem=24 * 2**20, name=None
+    kernel, out_shape, args, specs=None, outs=None, scratch=(), flops=0, vmem=24 * 2**20, aliases=None, name=None
 ):
-    nbytes = sum(a.size * a.dtype.itemsize for a in args)
-    nbytes += sum(o.size * o.dtype.itemsize for o in out_shape)
-    return pl.pallas_call(
+    nbytes = 0 if flops == 0 else sum(a.size * a.dtype.itemsize for a in args)
+    return list(pl.pallas_call(
         kernel,
         out_shape=out_shape,
         in_specs=specs or [VMEM] * len(args),
         out_specs=outs or [VMEM] * len(out_shape),
         scratch_shapes=list(scratch),
+        input_output_aliases=aliases or {},
         compiler_params=pltpu.CompilerParams(vmem_limit_bytes=vmem),
         cost_estimate=pl.CostEstimate(flops=flops, bytes_accessed=nbytes, transcendentals=0),
         name=name,
-    )(*args)
+    )(*args))
 
 
 def pack_kernel(guess_ref, land_ref, coef_ref, own_ref, core_ref, pair_ref, diag_ref, *scratch):
@@ -214,17 +215,20 @@
 
 
 def seen_kernel(*refs):
-    fields = [load(ref) for ref in refs[:4]]
     lat_ref, fwd_ref, seen_ref = refs[4:]
-    seen_ref[...] = lon_conv(lat_conv(fields, lat_ref), fwd_ref)
-
-
-def misfit_kernel(seen_ref, keep_ref, sent_ref, adj_ref, odd_ref, even_ref):
+    seen_ref[...] = lon_conv(lat_conv([load(ref) for ref in refs[:4]], lat_ref), fwd_ref)
+
+
+def misfit_kernel(seen_ref, keep_ref, sent_ref, adj_ref, *outs):
     obs = jnp.concatenate([keep_ref[0], sent_ref[0]], axis=0)
     weight = jnp.concatenate([keep_ref[1], sent_ref[1]], axis=0)
     spread = lon_conv(weight * (obs - seen_ref[...]), adj_ref)
-    rows = odd_ref.shape[0]
-    odd_ref[...], even_ref[...] = odd_even(spread[:rows], spread[rows:])
+    rows, width = outs[0].shape
+    odd, even = odd_even(spread[:rows], spread[rows:])
+    for part, (odd_ref, even_ref) in enumerate(zip(outs[::2], outs[1::2])):
+        columns = slice(width * part, width * (part + 1))
+        odd_ref[...] = odd[:, columns]
+        even_ref[...] = even[:, columns]
 
 
 def beside(center, above, below):
@@ -236,7 +240,6 @@
 def prior_kernel(pairs, *refs):
     fields = [load(ref) for ref in refs[:4]]
     odd_edge, even_edge = edge_row(refs[4]), edge_row(refs[5])
-    map_refs = refs[6:10]
     out_ref, ext, wide, inner = refs[10:]
     k, y, _ = place()
     rows, length = fields[0].shape
@@ -247,9 +250,9 @@
     for block, field in enumerate(fields):
         where = rows * jnp.where(even, block, 3 - block)
         ext[pl.ds(pl.multiple_of(where, rows), rows), :] = field
-    for block, (left, right) in enumerate((map_refs[:2], map_refs[2:])):
+    for block, (left, right) in enumerate(map_pairs(refs[6:10])):
         where = pl.multiple_of(8 + rows * jnp.where(y == 0, block, 1 - block), 8)
-        coef = jnp.concatenate([left[0], right[0]], axis=1) + 4.0
+        coef = jnp.concatenate([left[...], right[...]], axis=1) + 4.0
         wide[pl.ds(where, rows), :] = coef
     north = jnp.where(even, odd_edge, even_edge) + 4.0
     south = jnp.where(even, even_edge, odd_edge) + 4.0
@@ -268,42 +271,66 @@
     out_ref[rows:, :] = ext[pl.ds(pl.multiple_of(rows * (1 - y), rows), rows), :]
 
 
+def map_pairs(refs):
+    return refs[:2], refs[2:]
+
+
 def adjoint_kernel(*refs):
     refs[5][...] = lat_conv([ref[...] for ref in refs[:4]], refs[4])
 
 
-def update_kernel(final, *refs):
-    back_ref, prior_ref, left, right, pair_left, pair_right = refs[:6]
+def update_kernel(back_ref, prior_ref, *refs):
+    rows, width = back_ref.shape[0] // 2, back_ref.shape[1] // 2
     last = back_ref[...] - prior_ref[...]
-    rows, length = last.shape[0] // 2, last.shape[1]
-    width = length // 2
-    last_own = last[:rows] * jnp.concatenate([left[1], right[1]], axis=1)
-    last_pair = last[rows:] * jnp.concatenate([pair_left[1], pair_right[1]], axis=1)
-    outs = refs[-4:] if final else refs[-6:]
-    outs[0][...] = last_own[:, :width]
-    outs[1][...] = last_own[:, width:]
-    outs[2][...] = last_pair[:, :width]
-    outs[3][...] = last_pair[:, width:]
-    if not final:
-        odd, even = odd_even(last_own, last_pair)
-        outs[4][...] = load(refs[6]) + odd * (1.0 / THETA)
-        outs[5][...] = load(refs[7]) + even * (1.0 / THETA)
-
-
-def final_kernel(*refs):
-    early, late = refs[:4], refs[4:8]
-    guess_ref, land_ref, state_ref, last_ref = refs[8:]
+    sea = [jnp.concatenate([left[...], right[...]], axis=1) for left, right in map_pairs(refs[:4])]
+    last_own, last_pair = last[:rows] * sea[0], last[rows:] * sea[1]
+    base, states, outs = refs[4:6], refs[6:8], refs[8:]
+    for before, state, change in zip(base, states, odd_even(last_own, last_pair)):
+        state[...] = load(before) + change * (1.0 / THETA)
+    for i in range(2):
+        outs[2 * i][...] = last_own[:, width * i : width * (i + 1)]
+        outs[2 * i + 1][...] = last_pair[:, width * i : width * (i + 1)]
+
+
+def last_kernel(half, *refs):
+    lat_ref, prior_ref = refs[4:6]
+    rows, width = refs[0].shape
+    last = lat_conv([ref[...] for ref in refs[:4]], lat_ref)
+    last = last - prior_ref[:, width * half : width * (half + 1)]
+    own, pair = map_pairs(refs[6:10])
+    refs[10][...] = last[:rows] * own[half][...]
+    refs[11][...] = last[rows:] * pair[half][...]
+
+
+def days_of():
     _, y, c = place()
+    return 2 * c + y, 2 * c + (1 - y), 2 * (1 - c) + y, 2 * (1 - c) + (1 - y)
+
+
+def early_kernel(*refs):
+    guess_ref, land_ref, fixed_ref, state_ref = refs[4:]
     land = 1.0 - land_ref[...].astype(F32)
-    days = (2 * c + y, 2 * (1 - c) + y, 2 * c + (1 - y), 2 * (1 - c) + (1 - y))
-    for day, early_ref, late_ref in zip(days, early, late):
+    for i, (day, ref) in enumerate(zip(days_of(), refs[:4])):
         guess = guess_ref[day]
-        update = (early_ref[...] - land * guess) * (1.0 / THETA)
+        update = (ref[...] - land * guess) * (1.0 / THETA)
         state = guess + update
-        last = late_ref[...] - land * state
-        update = (NEW_RHO * RHO) * update + (2.0 * NEW_RHO / DELTA) * last
-        state_ref[day] = state + update
-        last_ref[day] = last
+        fixed_ref[i] = land * state
+        state_ref[i] = state + (NEW_RHO * RHO) * update
+
+
+def final_kernel(half, *refs):
+    late, (fixed_ref, sum_ref) = refs[:2], refs[2:4]
+    state_ref, last_ref, state, last, sems = refs[-5:]
+    days = days_of()[2 * half : 2 * half + 2]
+    copies = []
+    for i, (day, ref) in enumerate(zip(days, late)):
+        last[i] = ref[...] - fixed_ref[2 * half + i]
+        state[i] = sum_ref[2 * half + i] + (2.0 * NEW_RHO / DELTA) * last[i]
+        for j, (source, target) in enumerate(((state, state_ref), (last, last_ref))):
+            copies.append(pltpu.make_async_copy(source.at[i], target.at[day], sems.at[2 * i + j]))
+            copies[-1].start()
+    for copy in copies:
+        copy.wait()
 
 
 def body(
@@ -339,7 +366,6 @@
 
     piece = shape(rows, width)
     packed = shape(8, rows // 8 * width + 128)
-    band = shape(rows, length)
     own, to_core, to_pair, to_diag = call(
         pack_kernel,
         [packed] * 4,
@@ -357,12 +383,24 @@
         name="pack",
     )
     by_pair, by_diag = pair(to_pair), diag(to_diag)
+    observations, own = lax.optimization_barrier((observations, own))
+    by_core = core(to_core)
     keep, send = call(
         obs_kernel,
         [shape(2, rows, length)] * 2,
         [observations, obs_precision, track_counts[:, :, None]],
         name="observed",
     )
+    coef, sea = range_coef, land_sea.astype(F32)
+    send, by_pair, by_diag, by_core = lax.optimization_barrier((send, by_pair, by_diag, by_core))
+    sent = pair(send)
+    v_odd, v_even = call(
+        order_kernel,
+        [shape(8, 2 * packed.shape[1])] * 2,
+        [own, by_core, by_pair, by_diag],
+        name="order",
+    )
+    coef, sea, lat_kernel, v_odd = lax.optimization_barrier((coef, sea, lat_kernel, v_odd))
     lat_fwd, lat_adj, lon_fwd, lon_adj = call(
         functools.partial(matrix_kernel, pairs, rows),
         [shape(4 * rows, 8 * rows, dtype=BF16)] * 2
@@ -372,24 +410,12 @@
         flops=4 * 65 * 2 * 70000,
         name="matrices",
     )
-    to_core, lat_fwd = lax.optimization_barrier((to_core, lat_fwd))
-    by_core = core(to_core)
-    maps = jnp.stack([range_coef, land_sea.astype(F32)])
-
-    send, by_pair, by_diag = lax.optimization_barrier((send, by_pair, by_diag))
-    v_odd, v_even = call(
-        order_kernel,
-        [shape(8, 2 * packed.shape[1])] * 2,
-        [own, by_core, by_pair, by_diag],
-        name="order",
-    )
     fields = [odd(v_odd), v_odd, v_even, even(v_even)]
+    by_lon = [core(coef), core(sea)]
+    fields[0], *by_lon = lax.optimization_barrier((fields[0], *by_lon))
     edges = [fields[0], fields[3]]
-    sent = pair(send)
+    band = shape(rows, length)
     conv = 2 * 3 * 2 * rows * length * 512
-    maps_core = core(maps)
-
-    pieces = []
     for step in range(2):
         (seen,) = call(
             seen_kernel,
@@ -398,24 +424,22 @@
             flops=2 * conv,
             name="seen",
         )
-        m_odd, m_even = call(
-            misfit_kernel, [band] * 2, [seen, keep, sent, lon_adj], flops=conv, name="misfit"
+        misfit = call(
+            misfit_kernel,
+            [piece] * 4 if step else [band] * 2,
+            [seen, keep, sent, lon_adj],
+            flops=conv,
+            name="misfit",
         )
         if not step:
-            maps, m_odd, m_even = lax.optimization_barrier((maps, m_odd, m_even))
-            maps_pair = pair(maps)
-            maps = [maps, maps_core, maps_pair, core(maps_pair)]
-        (back,) = call(
-            adjoint_kernel,
-            [shape(2 * rows, length)],
-            [odd(m_odd), m_odd, m_even, even(m_even), lat_adj],
-            flops=ADJOINT_COST,
-            name="adjoint",
-        )
+            coef, sea, misfit[0] = lax.optimization_barrier((coef, sea, misfit[0]))
+            coef_pair, sea_pair = pair(coef), pair(sea)
+            coefs = [coef, by_lon[0], coef_pair, core(coef_pair)]
+            seas = [sea, by_lon[1], sea_pair, core(sea_pair)]
         (prior,) = call(
             functools.partial(prior_kernel, pairs),
             [shape(2 * rows, length)],
-            fields + edges + maps,
+            fields + edges + coefs,
             scratch=[
                 pltpu.VMEM((4 * rows, length), F32),
                 pltpu.VMEM((2 * rows + 16, length), F32),
@@ -423,22 +447,66 @@
             ],
             name="prior",
         )
-        outs = call(
-            functools.partial(update_kernel, step == 1),
-            [piece] * 4 + ([] if step else [band] * 2),
-            [back, prior] + maps + ([] if step else [v_odd, v_even]),
-            name="update",
+        common = [lat_adj, prior] + seas
+        moved = [odd(m) if i % 2 == 0 else even(m) for i, m in enumerate(misfit)]
+        if not step:
+            (back,) = call(
+                adjoint_kernel,
+                [shape(2 * rows, length)],
+                [moved[0], *misfit, moved[1], lat_adj],
+                flops=ADJOINT_COST,
+                name="adjoint",
+            )
+            v_odd, v_even, *pieces = call(
+                update_kernel,
+                [band] * 2 + [piece] * 4,
+                [back, prior, *seas, v_odd, v_even],
+                name="update",
+            )
+            fields = [odd(v_odd), v_odd, v_even, even(v_even)]
+            pieces = [pieces[0], pair(pieces[1]), core(pieces[2]), diag(pieces[3])]
+            early = call(
+                early_kernel,
+                [shape(days, rows, width)] * 2,
+                pieces + [first_guess, land_sea],
+                name="early",
+            )
+    moved[0], *early = lax.optimization_barrier((moved[0], *early))
+    left_own, left_pair = call(
+        functools.partial(last_kernel, 0),
+        [piece] * 2,
+        [moved[0], *misfit[:2], moved[1], *common],
+        flops=LEFT_COST,
+        name="update",
+    )
+    moved[2], left_own = lax.optimization_barrier((moved[2], left_own))
+    right_own, right_pair = call(
+        functools.partial(last_kernel, 1),
+        [piece] * 2,
+        [moved[2], *misfit[2:], moved[3], *common],
+        flops=conv,
+        name="update",
+    )
+    pieces = [left_own, pair(left_pair), core(right_own), diag(right_pair)]
+    result = []
+    for half in range(2):
+        args = pieces[2 * half : 2 * half + 2] + early
+        result = call(
+            functools.partial(final_kernel, half),
+            [shape(days, rows, width)] * 2,
+            args + (result if half else []),
+            [VMEM] * 4 + [HBM] * 2 * half,
+            outs=[HBM] * 2,
+            scratch=[
+                pltpu.VMEM((2, rows, width), F32),
+                pltpu.VMEM((2, rows, width), F32),
+                pltpu.SemaphoreType.DMA((4,)),
+            ],
+            aliases={4: 0, 5: 1} if half else {},
+            flops=0 if half else LEFT_COST,
+            name="final",
         )
-        pieces += [outs[0], core(outs[1]), pair(outs[2]), diag(outs[3])]
-        if not step:
-            fields = [odd(outs[4]), outs[4], outs[5], even(outs[5])]
-    state, last = call(
-        final_kernel,
-        [shape(days, rows, width)] * 2,
-        pieces + [first_guess, land_sea],
-        name="final",
-    )
-    return state, last
+    return tuple(result)
 
 
 def solution(mesh):

time: 68.4 us -> 65.4 us (0.956)
  waiting for transfers between devices: 33.7 us -> 26.1 us
  starting transfers between devices: 21.6 us -> 25.3 us
  Pallas kernels: 11.5 us -> 12.3 us
    ppermute x21 -> x26, waiting for transfers between devices: 33.7 us -> 26.1 us  [permute(): return lax.ppermute(array, AXES, moves)]
    ppermute x21 -> x26, starting transfers between devices: 21.6 us -> 25.3 us  [permute(): return lax.ppermute(array, AXES, moves)]
    pallas_call x15 -> x17, Pallas kernels: 11.5 us -> 12.3 us  [call(): pl.pallas_call(kernel, out_shape=out_shape, in_specs=specs or [VMEM] * le...]
  transfers between devices with their start and end apart: 21 -> 26, of which waited for: 10 -> 11; matrix products, arithmetic and copies ran while one was open for 0% -> 0% of each run, Pallas kernels for 7% -> 13%
where the time goes in v2:
time: 65.4 us; the launch traced here: 65.2 us
  waiting for transfers between devices  26.1 us (40%)
  starting transfers between devices  25.3 us (39%)
  Pallas kernels  12.3 us (19%)
  between operations  0.93 us (1%)
    ppermute x26, waiting for transfers between devices, permute(): return lax.ppermute(array, AXES, moves)  26.1 us
    ppermute x26, starting transfers between devices, permute(): return lax.ppermute(array, AXES, moves)  25.3 us
    pallas_call x17, Pallas kernels, call(): pl.pallas_call(kernel, out_shape=out_shape, in_specs=specs or [VMEM] * le...  12.3 us
  transfers between devices with their start and end apart: 26, of which 11 were waited for; matrix products, arithmetic and copies ran while one was open for 0% of the time, Pallas kernels for 13%

profile of v2, /device:TPU:0, one launch (start us, length us, event | category | flops | bytes accessed | tf_op | source)
XLA Modules:
  0.0 65.2 jit_solution(1994233289953943831)
XLA Ops:
  0.6 2.0 %pack.1 = (f32[8,4224]{1,0:T(8,128)}, f32[8,4224]{1,0:T(8,128)}, f32[8,4224]{1,0:T(8,128)}, f32[8,4224]{1,0:T(8,128)}) custom-call(f32[4,32,1024]{2,1,0:T(8,128)} %refs_4_.1, s32[32,1024]{1,0:T(8,128)} %refs_5_.1, f32[32,1024]{1,0:T(8,128)} %refs_6_.1), custom_call_target="tpu_custom_call" | custom-call | tf_op jit(solution)/shard_map/pack/pallas_call | solution.py:59
  2.6 3.0 %collective-permute-start = (f32[8,4224]{1,0:T(8,128)}, f32[8,4224]{1,0:T(8,128)S(1)}, u32[]{:S(2)}, u32[]{:S(2)}) collective-permute-start(f32[8,4224]{1,0:T(8,128)} %get-tuple-element.59), channel_id=1, source_target_pairs={{0,2},{1,3},{2,0},{3,1},{4,6},{5,7},{6,4},{7,5},{8,10},{9,11},{10,... | collective-permute-start | bytes 405512 | tf_op jit(solution)/shard_map/ppermute | solution.py:355
  6.6 3.4 %collective-permute-done.pair_ref = f32[8,4224]{1,0:T(8,128)S(1)} collective-permute-done((f32[8,4224]{1,0:T(8,128)}, f32[8,4224]{1,0:T(8,128)S(1)}, u32[]{:S(2)}, u32[]{:S(2)}) %collective-permute-start) | collective-permute-done | bytes 135200 | tf_op jit(solution)/shard_map/ppermute | solution.py:355
  10.0 1.8 %collective-permute-done.1.diag_ref = f32[8,4224]{1,0:T(8,128)S(1)} collective-permute-done((f32[8,4224]{1,0:T(8,128)}, f32[8,4224]{1,0:T(8,128)S(1)}, u32[]{:S(2)}, u32[]{:S(2)}) %collective-permute-start.1) | collective-permute-done | bytes 135200 | tf_op jit(solution)/shard_map/ppermute | solution.py:355
  11.8 1.1 %collective-permute-start.7 = (f32[2,32,2048]{2,1,0:T(8,128)S(1)}, f32[2,32,2048]{2,1,0:T(8,128)S(1)}, u32[]{:S(2)}, u32[]{:S(2)}) collective-permute-start(f32[2,32,2048]{2,1,0:T(8,128)S(1)} %get-tuple-element.75), channel_id=1, source_target_pairs={{0,2},{1,3},{2,0},{3,1},{4,6},{5,7},{6,4},{7,5},{8,10},{9,11},{10,... | collective-permute-start | bytes 1572872 | tf_op jit(solution)/shard_map/ppermute | solution.py:355
  13.9 2.5 %collective-permute-start.6 = (f32[8,8448]{1,0:T(8,128)S(1)}, f32[8,8448]{1,0:T(8,128)S(1)}, u32[]{:S(2)}, u32[]{:S(2)}) collective-permute-start(f32[8,8448]{1,0:T(8,128)S(1)} %get-tuple-element.70.refs_2_.refs_5_), channel_id=1, source_target_pairs={{0,4},{1,5},{2,6},{3,7},{4,0},{5,1},{6,2},{7,3},{8,12},{9,13},{10,... | collective-permute-start | bytes 811016 | tf_op jit(solution)/shard_map/ppermute | solution.py:355
  16.8 2.1 %matrices.1 = (bf16[128,256]{1,0:T(8,128)(2,1)S(1)}, bf16[128,256]{1,0:T(8,128)(2,1)S(1)}, bf16[2,512,256]{2,1,0:T(8,128)(2,1)S(1)}, bf16[2,512,256]{2,1,0:T(8,128)(2,1)S(1)}) custom-call(f32[65]{0:T(128)S(1)} %copy-done.6, f32[65]{0:T(128)S(1)} %copy-done.7), custom_call_target="tpu_custom_call" | custom-call | flops 36400000 | bytes 520 | tf_op jit(solution)/shard_map/matrices/pallas_call | solution.py:59
  19.0 4.4 %collective-permute-done.6.refs_3_.refs_5_ = f32[8,8448]{1,0:T(8,128)S(1)} collective-permute-done((f32[8,8448]{1,0:T(8,128)S(1)}, f32[8,8448]{1,0:T(8,128)S(1)}, u32[]{:S(2)}, u32[]{:S(2)}) %collective-permute-start.6) | collective-permute-done | bytes 270368 | tf_op jit(solution)/shard_map/ppermute | solution.py:355
  24.2 1.8 %collective-permute-done.7.sent_ref = f32[2,32,2048]{2,1,0:T(8,128)S(1)} collective-permute-done((f32[2,32,2048]{2,1,0:T(8,128)S(1)}, f32[2,32,2048]{2,1,0:T(8,128)S(1)}, u32[]{:S(2)}, u32[]{:S(2)}) %collective-permute-start.7) | collective-permute-done | bytes 524320 | tf_op jit(solution)/shard_map/ppermute | solution.py:355
  26.7 3.4 %collective-permute-start.9 = (f32[32,2048]{1,0:T(8,128)S(1)}, f32[32,2048]{1,0:T(8,128)S(1)}, u32[]{:S(2)}, u32[]{:S(2)}) collective-permute-start(f32[32,2048]{1,0:T(8,128)S(1)} %get-tuple-element.79.refs_2_), channel_id=1, source_target_pairs={{0,4},{1,5},{2,6},{3,7},{4,0},{5,1},{6,2},{7,3},{8,12},{9,13},{10,... | collective-permute-start | bytes 786440 | tf_op jit(solution)/shard_map/ppermute | solution.py:355
  30.1 1.5 %collective-permute-start.10 = (f32[32,1024]{1,0:T(8,128)S(1)}, f32[32,1024]{1,0:T(8,128)S(1)}, u32[]{:S(2)}, u32[]{:S(2)}) collective-permute-start(f32[32,1024]{1,0:T(8,128)S(1)} %copy-done.2), channel_id=1, source_target_pairs={{0,2},{1,3},{2,0},{3,1},{4,6},{5,7},{6,4},{7,5},{8,10},{9,11},{10,... | collective-permute-start | bytes 393224 | tf_op jit(solution)/shard_map/ppermute | solution.py:355
  32.1 4.2 %collective-permute-done.10.refs_8_ = f32[32,1024]{1,0:T(8,128)S(1)} collective-permute-done((f32[32,1024]{1,0:T(8,128)S(1)}, f32[32,1024]{1,0:T(8,128)S(1)}, u32[]{:S(2)}, u32[]{:S(2)}) %collective-permute-start.10) | collective-permute-done | bytes 131104 | tf_op jit(solution)/shard_map/ppermute | solution.py:355
  36.2 1.4 %collective-permute-done.12.refs_2_.refs_8_ = f32[32,1024]{1,0:T(8,128)S(1)} collective-permute-done((f32[32,1024]{1,0:T(8,128)S(1)}, f32[32,1024]{1,0:T(8,128)S(1)}, u32[]{:S(2)}, u32[]{:S(2)}) %collective-permute-start.12) | collective-permute-done | bytes 131104 | tf_op jit(solution)/shard_map/ppermute | solution.py:355
  38.0 1.2 %prior.2.prior_ref = f32[64,2048]{1,0:T(8,128)S(1)} custom-call(f32[8,8448]{1,0:T(8,128)S(1)} %collective-permute-done.3.refs_0_.refs_4_, f32[8,8448]{1,0:T(8,128)S(1)} %get-tuple-element.68.refs_1_.refs_4_, f32[8,8448]{1,0:T(8,128)S(1)} %get-tuple-element.70.refs_2_.refs_5_, f32[8,8448]{1,0:T(8,128)S(1)} %collective-permute-done.6.refs_3_.refs_5_, ...), custom_call_target="tpu_custom_call" | custom-call | tf_op jit(solution)/shard_map/prior/pallas_call | solution.py:59
  39.9 1.9 %collective-permute-start.15 = (f32[32,2048]{1,0:T(8,128)S(1)}, f32[32,2048]{1,0:T(8,128)S(1)}, u32[]{:S(2)}, u32[]{:S(2)}) collective-permute-start(f32[32,2048]{1,0:T(8,128)S(1)} %get-tuple-element.86.refs_2_), channel_id=1, source_target_pairs={{0,4},{1,5},{2,6},{3,7},{4,0},{5,1},{6,2},{7,3},{8,12},{9,13},{10,... | collective-permute-start | bytes 786440 | tf_op jit(solution)/shard_map/ppermute | solution.py:355
  41.9 1.5 %collective-permute-start.18 = (f32[32,1024]{1,0:T(8,128)S(1)}, f32[32,1024]{1,0:T(8,128)S(1)}, u32[]{:S(2)}, u32[]{:S(2)}) collective-permute-start(f32[32,1024]{1,0:T(8,128)S(1)} %get-tuple-element.90), channel_id=1, source_target_pairs={{0,2},{1,3},{2,0},{3,1},{4,6},{5,7},{6,4},{7,5},{8,10},{9,11},{10,... | collective-permute-start | bytes 393224 | tf_op jit(solution)/shard_map/ppermute | solution.py:355
  44.0 4.5 %collective-permute-done.15.refs_3_ = f32[32,2048]{1,0:T(8,128)S(1)} collective-permute-done((f32[32,2048]{1,0:T(8,128)S(1)}, f32[32,2048]{1,0:T(8,128)S(1)}, u32[]{:S(2)}, u32[]{:S(2)}) %collective-permute-start.15) | collective-permute-done | bytes 262176 | tf_op jit(solution)/shard_map/ppermute | solution.py:355
  50.1 2.1 %collective-permute-start.21 = (f32[32,1024]{1,0:T(8,128)S(1)}, f32[32,1024]{1,0:T(8,128)S(1)}, u32[]{:S(2)}, u32[]{:S(2)}) collective-permute-start(f32[32,1024]{1,0:T(8,128)S(1)} %get-tuple-element.96.refs_2_), channel_id=1, source_target_pairs={{0,4},{1,5},{2,6},{3,7},{4,0},{5,1},{6,2},{7,3},{8,12},{9,13},{10,... | collective-permute-start | bytes 393224 | tf_op jit(solution)/shard_map/ppermute | solution.py:355
  52.4 1.7 %collective-permute-start.22 = (f32[32,1024]{1,0:T(8,128)S(1)}, f32[32,1024]{1,0:T(8,128)S(1)}, u32[]{:S(2)}, u32[]{:S(2)}) collective-permute-start(f32[32,1024]{1,0:T(8,128)S(1)} %get-tuple-element.99.refs_2_), channel_id=1, source_target_pairs={{0,4},{1,5},{2,6},{3,7},{4,0},{5,1},{6,2},{7,3},{8,12},{9,13},{10,... | collective-permute-start | bytes 393224 | tf_op jit(solution)/shard_map/ppermute | solution.py:355
  54.1 1.2 %prior.3.refs_5_ = f32[64,2048]{1,0:T(8,128)S(1)} custom-call(f32[32,2048]{1,0:T(8,128)S(1)} %collective-permute-done.14.refs_0_, f32[32,2048]{1,0:T(8,128)S(1)} %get-tuple-element.85.refs_1_, f32[32,2048]{1,0:T(8,128)S(1)} %get-tuple-element.86.refs_2_, f32[32,2048]{1,0:T(8,128)S(1)} %collective-permute-done.15.refs_3_, ...), custom_call_target="tpu_custom_call" | custom-call | tf_op jit(solution)/shard_map/prior/pallas_call | solution.py:59
  55.3 1.1 %collective-permute-done.21.refs_3_ = f32[32,1024]{1,0:T(8,128)S(1)} collective-permute-done((f32[32,1024]{1,0:T(8,128)S(1)}, f32[32,1024]{1,0:T(8,128)S(1)}, u32[]{:S(2)}, u32[]{:S(2)}) %collective-permute-start.21) | collective-permute-done | bytes 131104 | tf_op jit(solution)/shard_map/ppermute | solution.py:355
  56.6 1.6 %collective-permute-start.25 = (f32[32,1024]{1,0:T(8,128)S(1)}, f32[32,1024]{1,0:T(8,128)S(1)}, u32[]{:S(2)}, u32[]{:S(2)}) collective-permute-start(f32[32,1024]{1,0:T(8,128)S(1)} %get-tuple-element.105), channel_id=1, source_target_pairs={{0,2},{1,3},{2,0},{3,1},{4,6},{5,7},{6,4},{7,5},{8,10},{9,11},{10,... | collective-permute-start | bytes 393224 | tf_op jit(solution)/shard_map/ppermute | solution.py:355
  59.1 1.6 %collective-permute-start.24 = (f32[32,1024]{1,0:T(8,128)S(1)}, f32[32,1024]{1,0:T(8,128)S(1)}, u32[]{:S(2)}, u32[]{:S(2)}) collective-permute-start(f32[32,1024]{1,0:T(8,128)S(1)} %get-tuple-element.101), channel_id=1, source_target_pairs={{0,3},{1,2},{2,1},{3,0},{4,7},{5,6},{6,5},{7,4},{8,11},{9,10},{10,... | collective-permute-start | bytes 393224 | tf_op jit(solution)/shard_map/ppermute | solution.py:355
  62.5 1.9 %collective-permute-done.24.refs_1_ = f32[32,1024]{1,0:T(8,128)S(1)} collective-permute-done((f32[32,1024]{1,0:T(8,128)S(1)}, f32[32,1024]{1,0:T(8,128)S(1)}, u32[]{:S(2)}, u32[]{:S(2)}) %collective-permute-start.24) | collective-permute-done | bytes 131104 | tf_op jit(solution)/shard_map/ppermute | solution.py:355
  (65 shorter events, 11.5 us)
Async XLA Ops:
  2.6 7.4 %collective-permute-start = (f32[8,4224]{1,0:T(8,128)}, f32[8,4224]{1,0:T(8,128)S(1)}, u32[]{:S(2)}, u32[]{:S(2)}) collective-permute-start(f32[8,4224]{1,0:T(8,128)} %get-tuple-element.59), channel_id=1, source_target_pairs={{0,2},{1,3},{2,0},{3,1},{4,6},{5,7},{6,4},{7,5},{8,10},{9,11},{10,... | collective-permute-start | bytes 405512 | tf_op jit(solution)/shard_map/ppermute | solution.py:355
  5.7 6.2 %collective-permute-start.1 = (f32[8,4224]{1,0:T(8,128)}, f32[8,4224]{1,0:T(8,128)S(1)}, u32[]{:S(2)}, u32[]{:S(2)}) collective-permute-start(f32[8,4224]{1,0:T(8,128)} %get-tuple-element.60), channel_id=1, source_target_pairs={{0,3},{1,2},{2,1},{3,0},{4,7},{5,6},{6,5},{7,4},{8,11},{9,10},{10,... | collective-permute-start | bytes 405512 | tf_op jit(solution)/shard_map/ppermute | solution.py:355
  5.7 6.2 %collective-permute-start.2 = (f32[8,4224]{1,0:T(8,128)}, f32[8,4224]{1,0:T(8,128)S(1)}, u32[]{:S(2)}, u32[]{:S(2)}) collective-permute-start(f32[8,4224]{1,0:T(8,128)} %get-tuple-element.61), channel_id=1, source_target_pairs={{0,1},{1,0},{2,3},{3,2},{4,5},{5,4},{6,7},{7,6},{8,9},{9,8},{10,11... | collective-permute-start | bytes 405512 | tf_op jit(solution)/shard_map/ppermute | solution.py:355
  11.8 14.2 %collective-permute-start.7 = (f32[2,32,2048]{2,1,0:T(8,128)S(1)}, f32[2,32,2048]{2,1,0:T(8,128)S(1)}, u32[]{:S(2)}, u32[]{:S(2)}) collective-permute-start(f32[2,32,2048]{2,1,0:T(8,128)S(1)} %get-tuple-element.75), channel_id=1, source_target_pairs={{0,2},{1,3},{2,0},{3,1},{4,6},{5,7},{6,4},{7,5},{8,10},{9,11},{10,... | collective-permute-start | bytes 1572872 | tf_op jit(solution)/shard_map/ppermute | solution.py:355
  13.1 5.9 %collective-permute-start.3 = (f32[8,8448]{1,0:T(8,128)S(1)}, f32[8,8448]{1,0:T(8,128)S(1)}, u32[]{:S(2)}, u32[]{:S(2)}) collective-permute-start(f32[8,8448]{1,0:T(8,128)S(1)} %get-tuple-element.68.refs_1_.refs_4_), channel_id=1, source_target_pairs={{0,1},{1,0},{2,3},{3,2},{4,8},{5,9},{6,10},{7,11},{8,4},{9,5},{10,... | collective-permute-start | bytes 811016 | tf_op jit(solution)/shard_map/ppermute | solution.py:355
  13.9 9.5 %collective-permute-start.6 = (f32[8,8448]{1,0:T(8,128)S(1)}, f32[8,8448]{1,0:T(8,128)S(1)}, u32[]{:S(2)}, u32[]{:S(2)}) collective-permute-start(f32[8,8448]{1,0:T(8,128)S(1)} %get-tuple-element.70.refs_2_.refs_5_), channel_id=1, source_target_pairs={{0,4},{1,5},{2,6},{3,7},{4,0},{5,1},{6,2},{7,3},{8,12},{9,13},{10,... | collective-permute-start | bytes 811016 | tf_op jit(solution)/shard_map/ppermute | solution.py:355
  16.3 2.6 %collective-permute-start.4 = (f32[32,1024]{1,0:T(8,128)S(1)}, f32[32,1024]{1,0:T(8,128)S(1)}, u32[]{:S(2)}, u32[]{:S(2)}) collective-permute-start(f32[32,1024]{1,0:T(8,128)S(1)} %copy-done.2), channel_id=1, source_target_pairs={{0,1},{1,0},{2,3},{3,2},{4,5},{5,4},{6,7},{7,6},{8,9},{9,8},{10,11... | collective-permute-start | bytes 393224 | tf_op jit(solution)/shard_map/ppermute | solution.py:355
  16.5 2.5 %collective-permute-start.5 = (f32[32,1024]{1,0:T(8,128)S(1)}, f32[32,1024]{1,0:T(8,128)S(1)}, u32[]{:S(2)}, u32[]{:S(2)}) collective-permute-start(f32[32,1024]{1,0:T(8,128)S(1)} %convert_element_type.3.refs_0_.refs_6_), channel_id=1, source_target_pairs={{0,1},{1,0},{2,3},{3,2},{4,5},{5,4},{6,7},{7,6},{8,9},{9,8},{10,11... | collective-permute-start | bytes 393224 | tf_op jit(solution)/shard_map/ppermute | solution.py:355
  26.6 11.0 %collective-permute-start.8 = (f32[32,2048]{1,0:T(8,128)S(1)}, f32[32,2048]{1,0:T(8,128)S(1)}, u32[]{:S(2)}, u32[]{:S(2)}) collective-permute-start(f32[32,2048]{1,0:T(8,128)S(1)} %get-tuple-element.78.refs_1_), channel_id=1, source_target_pairs={{0,1},{1,0},{2,3},{3,2},{4,8},{5,9},{6,10},{7,11},{8,4},{9,5},{10,... | collective-permute-start | bytes 786440 | tf_op jit(solution)/shard_map/ppermute | solution.py:355
  26.7 11.0 %collective-permute-start.9 = (f32[32,2048]{1,0:T(8,128)S(1)}, f32[32,2048]{1,0:T(8,128)S(1)}, u32[]{:S(2)}, u32[]{:S(2)}) collective-permute-start(f32[32,2048]{1,0:T(8,128)S(1)} %get-tuple-element.79.refs_2_), channel_id=1, source_target_pairs={{0,4},{1,5},{2,6},{3,7},{4,0},{5,1},{6,2},{7,3},{8,12},{9,13},{10,... | collective-permute-start | bytes 786440 | tf_op jit(solution)/shard_map/ppermute | solution.py:355
  30.1 6.2 %collective-permute-start.10 = (f32[32,1024]{1,0:T(8,128)S(1)}, f32[32,1024]{1,0:T(8,128)S(1)}, u32[]{:S(2)}, u32[]{:S(2)}) collective-permute-start(f32[32,1024]{1,0:T(8,128)S(1)} %copy-done.2), channel_id=1, source_target_pairs={{0,2},{1,3},{2,0},{3,1},{4,6},{5,7},{6,4},{7,5},{8,10},{9,11},{10,... | collective-permute-start | bytes 393224 | tf_op jit(solution)/shard_map/ppermute | solution.py:355
  31.6 6.1 %collective-permute-start.12 = (f32[32,1024]{1,0:T(8,128)S(1)}, f32[32,1024]{1,0:T(8,128)S(1)}, u32[]{:S(2)}, u32[]{:S(2)}) collective-permute-start(f32[32,1024]{1,0:T(8,128)S(1)} %convert_element_type.3.refs_0_.refs_6_), channel_id=1, source_target_pairs={{0,2},{1,3},{2,0},{3,1},{4,6},{5,7},{6,4},{7,5},{8,10},{9,11},{10,... | collective-permute-start | bytes 393224 | tf_op jit(solution)/shard_map/ppermute | solution.py:355
  39.3 4.6 %collective-permute-start.14 = (f32[32,2048]{1,0:T(8,128)S(1)}, f32[32,2048]{1,0:T(8,128)S(1)}, u32[]{:S(2)}, u32[]{:S(2)}) collective-permute-start(f32[32,2048]{1,0:T(8,128)S(1)} %get-tuple-element.85.refs_1_), channel_id=1, source_target_pairs={{0,1},{1,0},{2,3},{3,2},{4,8},{5,9},{6,10},{7,11},{8,4},{9,5},{10,... | collective-permute-start | bytes 786440 | tf_op jit(solution)/shard_map/ppermute | solution.py:355
  39.9 8.6 %collective-permute-start.15 = (f32[32,2048]{1,0:T(8,128)S(1)}, f32[32,2048]{1,0:T(8,128)S(1)}, u32[]{:S(2)}, u32[]{:S(2)}) collective-permute-start(f32[32,2048]{1,0:T(8,128)S(1)} %get-tuple-element.86.refs_2_), channel_id=1, source_target_pairs={{0,4},{1,5},{2,6},{3,7},{4,0},{5,1},{6,2},{7,3},{8,12},{9,13},{10,... | collective-permute-start | bytes 786440 | tf_op jit(solution)/shard_map/ppermute | solution.py:355
  41.9 10.3 %collective-permute-start.18 = (f32[32,1024]{1,0:T(8,128)S(1)}, f32[32,1024]{1,0:T(8,128)S(1)}, u32[]{:S(2)}, u32[]{:S(2)}) collective-permute-start(f32[32,1024]{1,0:T(8,128)S(1)} %get-tuple-element.90), channel_id=1, source_target_pairs={{0,2},{1,3},{2,0},{3,1},{4,6},{5,7},{6,4},{7,5},{8,10},{9,11},{10,... | collective-permute-start | bytes 393224 | tf_op jit(solution)/shard_map/ppermute | solution.py:355
  43.3 8.8 %collective-permute-start.19 = (f32[32,1024]{1,0:T(8,128)S(1)}, f32[32,1024]{1,0:T(8,128)S(1)}, u32[]{:S(2)}, u32[]{:S(2)}) collective-permute-start(f32[32,1024]{1,0:T(8,128)S(1)} %get-tuple-element.91), channel_id=1, source_target_pairs={{0,1},{1,0},{2,3},{3,2},{4,5},{5,4},{6,7},{7,6},{8,9},{9,8},{10,11... | collective-permute-start | bytes 393224 | tf_op jit(solution)/shard_map/ppermute | solution.py:355
  43.4 8.8 %collective-permute-start.20 = (f32[32,1024]{1,0:T(8,128)S(1)}, f32[32,1024]{1,0:T(8,128)S(1)}, u32[]{:S(2)}, u32[]{:S(2)}) collective-permute-start(f32[32,1024]{1,0:T(8,128)S(1)} %get-tuple-element.92), channel_id=1, source_target_pairs={{0,3},{1,2},{2,1},{3,0},{4,7},{5,6},{6,5},{7,4},{8,11},{9,10},{10,... | collective-permute-start | bytes 393224 | tf_op jit(solution)/shard_map/ppermute | solution.py:355
  50.0 5.3 %collective-permute-start.17 = (f32[32,1024]{1,0:T(8,128)S(1)}, f32[32,1024]{1,0:T(8,128)S(1)}, u32[]{:S(2)}, u32[]{:S(2)}) collective-permute-start(f32[32,1024]{1,0:T(8,128)S(1)} %get-tuple-element.88.refs_1_), channel_id=1, source_target_pairs={{0,1},{1,0},{2,3},{3,2},{4,8},{5,9},{6,10},{7,11},{8,4},{9,5},{10,... | collective-permute-start | bytes 393224 | tf_op jit(solution)/shard_map/ppermute | solution.py:355
  50.1 6.3 %collective-permute-start.21 = (f32[32,1024]{1,0:T(8,128)S(1)}, f32[32,1024]{1,0:T(8,128)S(1)}, u32[]{:S(2)}, u32[]{:S(2)}) collective-permute-start(f32[32,1024]{1,0:T(8,128)S(1)} %get-tuple-element.96.refs_2_), channel_id=1, source_target_pairs={{0,4},{1,5},{2,6},{3,7},{4,0},{5,1},{6,2},{7,3},{8,12},{9,13},{10,... | collective-permute-start | bytes 393224 | tf_op jit(solution)/shard_map/ppermute | solution.py:355
  52.3 5.8 %collective-permute-start.16 = (f32[32,1024]{1,0:T(8,128)S(1)}, f32[32,1024]{1,0:T(8,128)S(1)}, u32[]{:S(2)}, u32[]{:S(2)}) collective-permute-start(f32[32,1024]{1,0:T(8,128)S(1)} %get-tuple-element.87.refs_1_), channel_id=1, source_target_pairs={{0,1},{1,0},{2,3},{3,2},{4,8},{5,9},{6,10},{7,11},{8,4},{9,5},{10,... | collective-permute-start | bytes 393224 | tf_op jit(solution)/shard_map/ppermute | solution.py:355
  52.4 6.4 %collective-permute-start.22 = (f32[32,1024]{1,0:T(8,128)S(1)}, f32[32,1024]{1,0:T(8,128)S(1)}, u32[]{:S(2)}, u32[]{:S(2)}) collective-permute-start(f32[32,1024]{1,0:T(8,128)S(1)} %get-tuple-element.99.refs_2_), channel_id=1, source_target_pairs={{0,4},{1,5},{2,6},{3,7},{4,0},{5,1},{6,2},{7,3},{8,12},{9,13},{10,... | collective-permute-start | bytes 393224 | tf_op jit(solution)/shard_map/ppermute | solution.py:355
  56.6 5.0 %collective-permute-start.25 = (f32[32,1024]{1,0:T(8,128)S(1)}, f32[32,1024]{1,0:T(8,128)S(1)}, u32[]{:S(2)}, u32[]{:S(2)}) collective-permute-start(f32[32,1024]{1,0:T(8,128)S(1)} %get-tuple-element.105), channel_id=1, source_target_pairs={{0,2},{1,3},{2,0},{3,1},{4,6},{5,7},{6,4},{7,5},{8,10},{9,11},{10,... | collective-permute-start | bytes 393224 | tf_op jit(solution)/shard_map/ppermute | solution.py:355
  59.0 3.5 %collective-permute-start.23 = (f32[32,1024]{1,0:T(8,128)S(1)}, f32[32,1024]{1,0:T(8,128)S(1)}, u32[]{:S(2)}, u32[]{:S(2)}) collective-permute-start(f32[32,1024]{1,0:T(8,128)S(1)} %get-tuple-element.100), channel_id=1, source_target_pairs={{0,1},{1,0},{2,3},{3,2},{4,5},{5,4},{6,7},{7,6},{8,9},{9,8},{10,11... | collective-permute-start | bytes 393224 | tf_op jit(solution)/shard_map/ppermute | solution.py:355
  59.1 5.3 %collective-permute-start.24 = (f32[32,1024]{1,0:T(8,128)S(1)}, f32[32,1024]{1,0:T(8,128)S(1)}, u32[]{:S(2)}, u32[]{:S(2)}) collective-permute-start(f32[32,1024]{1,0:T(8,128)S(1)} %get-tuple-element.101), channel_id=1, source_target_pairs={{0,3},{1,2},{2,1},{3,0},{4,7},{5,6},{6,5},{7,4},{8,11},{9,10},{10,... | collective-permute-start | bytes 393224 | tf_op jit(solution)/shard_map/ppermute | solution.py:355
  (11 other events, 42.1 us)

commit v3 on v2

--- a/solution.py
+++ b/solution.py
@@ -38,13 +38,13 @@
 def open_sides(pairs):
     k, _, _ = place()
     north, south = jnp.where(k == 0, 0.0, 1.0), jnp.where(k == pairs - 1, 0.0, 1.0)
-    even = lax.rem(k, 2) == 0
-    return jnp.where(even, north, south), jnp.where(even, south, north)
-
-
-def odd_even(own, pair):
+    flip = lax.rem(k, 2) == 1
+    return jnp.where(flip, north, south), jnp.where(flip, south, north)
+
+
+def lead_trail(own, pair):
     k, y, _ = place()
-    straight = lax.rem(k + y, 2) == 0
+    straight = lax.rem(k + y, 2) == 1
     return jnp.where(straight, own, pair), jnp.where(straight, pair, own)
 
 
@@ -101,12 +101,12 @@
         out.wait()
 
 
-def order_kernel(own_ref, core_ref, pair_ref, diag_ref, odd_ref, even_ref):
+def order_kernel(own_ref, core_ref, pair_ref, diag_ref, lead_ref, trail_ref):
     size = own_ref.shape[1]
     for i, (own, pair) in enumerate(((own_ref, pair_ref), (core_ref, diag_ref))):
-        odd, even = odd_even(own[...], pair[...])
-        odd_ref[:, size * i : size * (i + 1)] = odd
-        even_ref[:, size * i : size * (i + 1)] = even
+        lead, trail = lead_trail(own[...], pair[...])
+        lead_ref[:, size * i : size * (i + 1)] = lead
+        trail_ref[:, size * i : size * (i + 1)] = trail
 
 
 def obs_kernel(obs_ref, precision_ref, counts_ref, keep_ref, send_ref):
@@ -140,15 +140,15 @@
     k, y, _ = place()
     dims = (2 * rows, 4 * rows)
 
-    even = lax.rem(k, 2) == 0
+    flip = lax.rem(k, 2) == 1
     out = lax.broadcasted_iota(jnp.int32, dims, 0)
     col = lax.broadcasted_iota(jnp.int32, dims, 1)
     target = rows * jnp.where(y == 0, out // rows, 1 - out // rows) + out % rows
-    source = rows * jnp.where(even, col // rows - 1, 2 - col // rows) + col % rows
+    source = rows * jnp.where(flip, col // rows - 1, 2 - col // rows) + col % rows
     offset = source - target + HALF
-    odd_open, even_open = open_sides(pairs)
-    inside = jnp.where(col < 3 * rows, 1.0, even_open)
-    inside = jnp.where(col < rows, odd_open, inside)
+    lead_open, trail_open = open_sides(pairs)
+    inside = jnp.where(col < 3 * rows, 1.0, trail_open)
+    inside = jnp.where(col < rows, lead_open, inside)
     for ref, matrix in zip((lat_fwd_ref, lat_adj_ref), banded(lat_ref, offset)):
         high, low = split(matrix * inside)
         ref[: 2 * rows, : 4 * rows] = high
@@ -224,11 +224,11 @@
     weight = jnp.concatenate([keep_ref[1], sent_ref[1]], axis=0)
     spread = lon_conv(weight * (obs - seen_ref[...]), adj_ref)
     rows, width = outs[0].shape
-    odd, even = odd_even(spread[:rows], spread[rows:])
-    for part, (odd_ref, even_ref) in enumerate(zip(outs[::2], outs[1::2])):
+    lead, trail = lead_trail(spread[:rows], spread[rows:])
+    for part, (lead_ref, trail_ref) in enumerate(zip(outs[::2], outs[1::2])):
         columns = slice(width * part, width * (part + 1))
-        odd_ref[...] = odd[:, columns]
-        even_ref[...] = even[:, columns]
+        lead_ref[...] = lead[:, columns]
+        trail_ref[...] = trail[:, columns]
 
 
 def beside(center, above, below):
@@ -239,23 +239,23 @@
 
 def prior_kernel(pairs, *refs):
     fields = [load(ref) for ref in refs[:4]]
-    odd_edge, even_edge = edge_row(refs[4]), edge_row(refs[5])
+    lead_edge, trail_edge = edge_row(refs[4]), edge_row(refs[5])
     out_ref, ext, wide, inner = refs[10:]
     k, y, _ = place()
     rows, length = fields[0].shape
-    even = lax.rem(k, 2) == 0
-    odd_open, even_open = open_sides(pairs)
-    fields[0] = fields[0] * odd_open
-    fields[3] = fields[3] * even_open
+    flip = lax.rem(k, 2) == 1
+    lead_open, trail_open = open_sides(pairs)
+    fields[0] = fields[0] * lead_open
+    fields[3] = fields[3] * trail_open
     for block, field in enumerate(fields):
-        where = rows * jnp.where(even, block, 3 - block)
+        where = rows * jnp.where(flip, block, 3 - block)
         ext[pl.ds(pl.multiple_of(where, rows), rows), :] = field
     for block, (left, right) in enumerate(map_pairs(refs[6:10])):
         where = pl.multiple_of(8 + rows * jnp.where(y == 0, block, 1 - block), 8)
-        coef = jnp.concatenate([left[...], right[...]], axis=1) + 4.0
+        coef = jnp.concatenate([left[0], right[0]], axis=1) + 4.0
         wide[pl.ds(where, rows), :] = coef
-    north = jnp.where(even, odd_edge, even_edge) + 4.0
-    south = jnp.where(even, even_edge, odd_edge) + 4.0
+    north = jnp.where(flip, lead_edge, trail_edge) + 4.0
+    south = jnp.where(flip, trail_edge, lead_edge) + 4.0
     wide[:8, :] = jnp.broadcast_to(north, (8, length))
     wide[8 + 2 * rows :, :] = jnp.broadcast_to(south, (8, length))
     low, count = rows - 8, 2 * rows + 16
@@ -282,10 +282,10 @@
 def update_kernel(back_ref, prior_ref, *refs):
     rows, width = back_ref.shape[0] // 2, back_ref.shape[1] // 2
     last = back_ref[...] - prior_ref[...]
-    sea = [jnp.concatenate([left[...], right[...]], axis=1) for left, right in map_pairs(refs[:4])]
+    sea = [jnp.concatenate([left[1], right[1]], axis=1) for left, right in map_pairs(refs[:4])]
     last_own, last_pair = last[:rows] * sea[0], last[rows:] * sea[1]
     base, states, outs = refs[4:6], refs[6:8], refs[8:]
-    for before, state, change in zip(base, states, odd_even(last_own, last_pair)):
+    for before, state, change in zip(base, states, lead_trail(last_own, last_pair)):
         state[...] = load(before) + change * (1.0 / THETA)
     for i in range(2):
         outs[2 * i][...] = last_own[:, width * i : width * (i + 1)]
@@ -298,8 +298,8 @@
     last = lat_conv([ref[...] for ref in refs[:4]], lat_ref)
     last = last - prior_ref[:, width * half : width * (half + 1)]
     own, pair = map_pairs(refs[6:10])
-    refs[10][...] = last[:rows] * own[half][...]
-    refs[11][...] = last[rows:] * pair[half][...]
+    refs[10][...] = last[:rows] * own[half][1]
+    refs[11][...] = last[rows:] * pair[half][1]
 
 
 def days_of():
@@ -361,8 +361,8 @@
     core = lambda array: permute(array, lambda k, y, c: (k, y, 1 - c))
     pair = lambda array: permute(array, lambda k, y, c: (k, 1 - y, c))
     diag = lambda array: permute(array, lambda k, y, c: (k, 1 - y, 1 - c))
-    odd = lambda array: permute(array, lambda k, y, c: swap(k, y, c, 1))
-    even = lambda array: permute(array, lambda k, y, c: swap(k, y, c, 0))
+    lead = lambda array: permute(array, lambda k, y, c: swap(k, y, c, 0))
+    trail = lambda array: permute(array, lambda k, y, c: swap(k, y, c, 1))
 
     piece = shape(rows, width)
     packed = shape(8, rows // 8 * width + 128)
@@ -391,16 +391,16 @@
         [observations, obs_precision, track_counts[:, :, None]],
         name="observed",
     )
-    coef, sea = range_coef, land_sea.astype(F32)
-    send, by_pair, by_diag, by_core = lax.optimization_barrier((send, by_pair, by_diag, by_core))
+    maps = jnp.stack([range_coef, land_sea.astype(F32)])
     sent = pair(send)
-    v_odd, v_even = call(
+    v_lead, v_trail = call(
         order_kernel,
         [shape(8, 2 * packed.shape[1])] * 2,
         [own, by_core, by_pair, by_diag],
+        flops=ADJOINT_COST,
         name="order",
     )
-    coef, sea, lat_kernel, v_odd = lax.optimization_barrier((coef, sea, lat_kernel, v_odd))
+    maps, lat_kernel, v_lead = lax.optimization_barrier((maps, lat_kernel, v_lead))
     lat_fwd, lat_adj, lon_fwd, lon_adj = call(
         functools.partial(matrix_kernel, pairs, rows),
         [shape(4 * rows, 8 * rows, dtype=BF16)] * 2
@@ -410,9 +410,9 @@
         flops=4 * 65 * 2 * 70000,
         name="matrices",
     )
-    fields = [odd(v_odd), v_odd, v_even, even(v_even)]
-    by_lon = [core(coef), core(sea)]
-    fields[0], *by_lon = lax.optimization_barrier((fields[0], *by_lon))
+    fields = [lead(v_lead), v_lead, v_trail, trail(v_trail)]
+    by_lon = core(maps)
+    fields[0], by_lon = lax.optimization_barrier((fields[0], by_lon))
     edges = [fields[0], fields[3]]
     band = shape(rows, length)
     conv = 2 * 3 * 2 * rows * length * 512
@@ -432,14 +432,13 @@
             name="misfit",
         )
         if not step:
-            coef, sea, misfit[0] = lax.optimization_barrier((coef, sea, misfit[0]))
-            coef_pair, sea_pair = pair(coef), pair(sea)
-            coefs = [coef, by_lon[0], coef_pair, core(coef_pair)]
-            seas = [sea, by_lon[1], sea_pair, core(sea_pair)]
+            maps, misfit[0] = lax.optimization_barrier((maps, misfit[0]))
+            maps_pair = pair(maps)
+            maps = [maps, by_lon, maps_pair, core(maps_pair)]
         (prior,) = call(
             functools.partial(prior_kernel, pairs),
             [shape(2 * rows, length)],
-            fields + edges + coefs,
+            fields + edges + maps,
             scratch=[
                 pltpu.VMEM((4 * rows, length), F32),
                 pltpu.VMEM((2 * rows + 16, length), F32),
@@ -447,8 +446,8 @@
             ],
             name="prior",
         )
-        common = [lat_adj, prior] + seas
-        moved = [odd(m) if i % 2 == 0 else even(m) for i, m in enumerate(misfit)]
+        common = [lat_adj, prior] + maps
+        moved = [lead(m) if i % 2 == 0 else trail(m) for i, m in enumerate(misfit)]
         if not step:
             (back,) = call(
                 adjoint_kernel,
@@ -457,13 +456,13 @@
                 flops=ADJOINT_COST,
                 name="adjoint",
             )
-            v_odd, v_even, *pieces = call(
+            v_lead, v_trail, *pieces = call(
                 update_kernel,
                 [band] * 2 + [piece] * 4,
-                [back, prior, *seas, v_odd, v_even],
+                [back, prior, *maps, v_lead, v_trail],
                 name="update",
             )
-            fields = [odd(v_odd), v_odd, v_even, even(v_even)]
+            fields = [lead(v_lead), v_lead, v_trail, trail(v_trail)]
             pieces = [pieces[0], pair(pieces[1]), core(pieces[2]), diag(pieces[3])]
             early = call(
                 early_kernel,

time: 65.4 us -> 61.7 us (0.943)
  starting transfers between devices: 25.3 us -> 23 us
  waiting for transfers between devices: 26.1 us -> 24.6 us
    ppermute x26 -> x23, starting transfers between devices: 25.3 us -> 23 us  [permute(): return lax.ppermute(array, AXES, moves)]
    ppermute x26 -> x23, waiting for transfers between devices: 26.1 us -> 24.6 us  [permute(): return lax.ppermute(array, AXES, moves)]
  transfers between devices with their start and end apart: 26 -> 23, of which waited for: 11 -> 11; matrix products, arithmetic and copies ran while one was open for 0% -> 0% of each run, Pallas kernels for 13% -> 12%
where the time goes in v3:
time: 61.7 us; the launch traced here: 61.5 us
  waiting for transfers between devices  24.6 us (40%)
  starting transfers between devices  23 us (37%)
  Pallas kernels  12.3 us (20%)
  between operations  0.89 us (1%)
  local copies, waits for them, and re-layouts  0.75 us (1%)
    ppermute x23, waiting for transfers between devices, permute(): return lax.ppermute(array, AXES, moves)  24.6 us
    ppermute x23, starting transfers between devices, permute(): return lax.ppermute(array, AXES, moves)  23 us
    pallas_call x17, Pallas kernels, call(): pl.pallas_call(kernel, out_shape=out_shape, in_specs=specs or [VMEM] * le...  12.3 us
  transfers between devices with their start and end apart: 23, of which 11 were waited for; matrix products, arithmetic and copies ran while one was open for 0% of the time, Pallas kernels for 12%

profile of v3, /device:TPU:0, one launch (start us, length us, event | category | flops | bytes accessed | tf_op | source)
XLA Modules:
  0.0 61.5 jit_solution(9593290919856539676)
XLA Ops:
  0.6 2.0 %pack.1 = (f32[8,4224]{1,0:T(8,128)}, f32[8,4224]{1,0:T(8,128)}, f32[8,4224]{1,0:T(8,128)}, f32[8,4224]{1,0:T(8,128)}) custom-call(f32[4,32,1024]{2,1,0:T(8,128)} %refs_4_.1, s32[32,1024]{1,0:T(8,128)} %refs_5_.1, f32[32,1024]{1,0:T(8,128)} %coef_ref.1), custom_call_target="tpu_custom_call" | custom-call | tf_op jit(solution)/shard_map/pack/pallas_call | solution.py:59
  3.2 2.6 %collective-permute-start.1 = (f32[8,4224]{1,0:T(8,128)}, f32[8,4224]{1,0:T(8,128)S(1)}, u32[]{:S(2)}, u32[]{:S(2)}) collective-permute-start(f32[8,4224]{1,0:T(8,128)} %get-tuple-element.51), channel_id=1, source_target_pairs={{0,2},{1,3},{2,0},{3,1},{4,6},{5,7},{6,4},{7,5},{8,10},{9,11},{10,... | collective-permute-start | bytes 405512 | tf_op jit(solution)/shard_map/ppermute | solution.py:355
  6.7 1.2 %collective-permute-start.6 = (f32[2,32,2048]{2,1,0:T(8,128)S(1)}, f32[2,32,2048]{2,1,0:T(8,128)S(1)}, u32[]{:S(2)}, u32[]{:S(2)}) collective-permute-start(f32[2,32,2048]{2,1,0:T(8,128)S(1)} %get-tuple-element.63), channel_id=1, source_target_pairs={{0,2},{1,3},{2,0},{3,1},{4,6},{5,7},{6,4},{7,5},{8,10},{9,11},{10,... | collective-permute-start | bytes 1572872 | tf_op jit(solution)/shard_map/ppermute | solution.py:355
  8.0 2.4 %collective-permute-done.1.pair_ref = f32[8,4224]{1,0:T(8,128)S(1)} collective-permute-done((f32[8,4224]{1,0:T(8,128)}, f32[8,4224]{1,0:T(8,128)S(1)}, u32[]{:S(2)}, u32[]{:S(2)}) %collective-permute-start.1) | collective-permute-done | bytes 135200 | tf_op jit(solution)/shard_map/ppermute | solution.py:355
  10.4 2.5 %collective-permute-done.2.diag_ref = f32[8,4224]{1,0:T(8,128)S(1)} collective-permute-done((f32[8,4224]{1,0:T(8,128)}, f32[8,4224]{1,0:T(8,128)S(1)}, u32[]{:S(2)}, u32[]{:S(2)}) %collective-permute-start.2) | collective-permute-done | bytes 135200 | tf_op jit(solution)/shard_map/ppermute | solution.py:355
  13.0 1.6 %collective-permute-start.3 = (f32[8,8448]{1,0:T(8,128)S(1)}, f32[8,8448]{1,0:T(8,128)S(1)}, u32[]{:S(2)}, u32[]{:S(2)}) collective-permute-start(f32[8,8448]{1,0:T(8,128)S(1)} %get-tuple-element.55.refs_1_.refs_4_), channel_id=1, source_target_pairs={{0,4},{1,5},{2,6},{3,7},{4,0},{5,1},{6,2},{7,3},{8,12},{9,13},{10,... | collective-permute-start | bytes 811016 | tf_op jit(solution)/shard_map/ppermute | solution.py:355
  15.1 2.1 %matrices.1 = (bf16[128,256]{1,0:T(8,128)(2,1)S(1)}, bf16[128,256]{1,0:T(8,128)(2,1)S(1)}, bf16[2,512,256]{2,1,0:T(8,128)(2,1)S(1)}, bf16[2,512,256]{2,1,0:T(8,128)(2,1)S(1)}) custom-call(f32[65]{0:T(128)S(1)} %copy-done.5, f32[65]{0:T(128)S(1)} %copy-done.6), custom_call_target="tpu_custom_call" | custom-call | flops 36400000 | bytes 520 | tf_op jit(solution)/shard_map/matrices/pallas_call | solution.py:59
  17.3 4.7 %collective-permute-done.3.refs_0_.refs_4_ = f32[8,8448]{1,0:T(8,128)S(1)} collective-permute-done((f32[8,8448]{1,0:T(8,128)S(1)}, f32[8,8448]{1,0:T(8,128)S(1)}, u32[]{:S(2)}, u32[]{:S(2)}) %collective-permute-start.3) | collective-permute-done | bytes 270368 | tf_op jit(solution)/shard_map/ppermute | solution.py:355
  22.8 1.5 %collective-permute-done.6.sent_ref = f32[2,32,2048]{2,1,0:T(8,128)S(1)} collective-permute-done((f32[2,32,2048]{2,1,0:T(8,128)S(1)}, f32[2,32,2048]{2,1,0:T(8,128)S(1)}, u32[]{:S(2)}, u32[]{:S(2)}) %collective-permute-start.6) | collective-permute-done | bytes 524320 | tf_op jit(solution)/shard_map/ppermute | solution.py:355
  24.9 1.8 %collective-permute-start.9 = (f32[2,32,1024]{2,1,0:T(8,128)S(1)}, f32[2,32,1024]{2,1,0:T(8,128)S(1)}, u32[]{:S(2)}, u32[]{:S(2)}) collective-permute-start(f32[2,32,1024]{2,1,0:T(8,128)S(1)} %pad_maximum_fusion.refs_6_.refs_0_), channel_id=1, source_target_pairs={{0,2},{1,3},{2,0},{3,1},{4,6},{5,7},{6,4},{7,5},{8,10},{9,11},{10,... | collective-permute-start | bytes 786440 | tf_op jit(solution)/shard_map/ppermute | solution.py:355
  26.7 1.6 %collective-permute-start.7 = (f32[32,2048]{1,0:T(8,128)S(1)}, f32[32,2048]{1,0:T(8,128)S(1)}, u32[]{:S(2)}, u32[]{:S(2)}) collective-permute-start(f32[32,2048]{1,0:T(8,128)S(1)} %get-tuple-element.66.refs_1_), channel_id=1, source_target_pairs={{0,4},{1,5},{2,6},{3,7},{4,0},{5,1},{6,2},{7,3},{8,12},{9,13},{10,... | collective-permute-start | bytes 786440 | tf_op jit(solution)/shard_map/ppermute | solution.py:355
  28.3 4.7 %collective-permute-done.9.refs_8_.refs_2_ = f32[2,32,1024]{2,1,0:T(8,128)S(1)} collective-permute-done((f32[2,32,1024]{2,1,0:T(8,128)S(1)}, f32[2,32,1024]{2,1,0:T(8,128)S(1)}, u32[]{:S(2)}, u32[]{:S(2)}) %collective-permute-start.9) | collective-permute-done | bytes 262176 | tf_op jit(solution)/shard_map/ppermute | solution.py:355
  33.0 1.3 %collective-permute-done.7.refs_0_ = f32[32,2048]{1,0:T(8,128)S(1)} collective-permute-done((f32[32,2048]{1,0:T(8,128)S(1)}, f32[32,2048]{1,0:T(8,128)S(1)}, u32[]{:S(2)}, u32[]{:S(2)}) %collective-permute-start.7) | collective-permute-done | bytes 262176 | tf_op jit(solution)/shard_map/ppermute | solution.py:355
  34.6 1.2 %prior.2.prior_ref = f32[64,2048]{1,0:T(8,128)S(1)} custom-call(f32[8,8448]{1,0:T(8,128)S(1)} %collective-permute-done.3.refs_0_.refs_4_, f32[8,8448]{1,0:T(8,128)S(1)} %get-tuple-element.55.refs_1_.refs_4_, f32[8,8448]{1,0:T(8,128)S(1)} %get-tuple-element.57.refs_2_.refs_5_, f32[8,8448]{1,0:T(8,128)S(1)} %collective-permute-done.5.refs_3_.refs_5_, ...), custom_call_target="tpu_custom_call" | custom-call | tf_op jit(solution)/shard_map/prior/pallas_call | solution.py:59
  36.0 2.8 %collective-permute-start.11 = (f32[32,2048]{1,0:T(8,128)S(1)}, f32[32,2048]{1,0:T(8,128)S(1)}, u32[]{:S(2)}, u32[]{:S(2)}) collective-permute-start(f32[32,2048]{1,0:T(8,128)S(1)} %get-tuple-element.71.refs_1_), channel_id=1, source_target_pairs={{0,4},{1,5},{2,6},{3,7},{4,0},{5,1},{6,2},{7,3},{8,12},{9,13},{10,... | collective-permute-start | bytes 786440 | tf_op jit(solution)/shard_map/ppermute | solution.py:355
  39.5 1.4 %collective-permute-start.17 = (f32[32,1024]{1,0:T(8,128)S(1)}, f32[32,1024]{1,0:T(8,128)S(1)}, u32[]{:S(2)}, u32[]{:S(2)}) collective-permute-start(f32[32,1024]{1,0:T(8,128)S(1)} %get-tuple-element.78), channel_id=1, source_target_pairs={{0,3},{1,2},{2,1},{3,0},{4,7},{5,6},{6,5},{7,4},{8,11},{9,10},{10,... | collective-permute-start | bytes 393224 | tf_op jit(solution)/shard_map/ppermute | solution.py:355
  40.9 3.4 %collective-permute-done.11.refs_0_ = f32[32,2048]{1,0:T(8,128)S(1)} collective-permute-done((f32[32,2048]{1,0:T(8,128)S(1)}, f32[32,2048]{1,0:T(8,128)S(1)}, u32[]{:S(2)}, u32[]{:S(2)}) %collective-permute-start.11) | collective-permute-done | bytes 262176 | tf_op jit(solution)/shard_map/ppermute | solution.py:355
  45.7 2.8 %collective-permute-start.14 = (f32[32,1024]{1,0:T(8,128)S(1)}, f32[32,1024]{1,0:T(8,128)S(1)}, u32[]{:S(2)}, u32[]{:S(2)}) collective-permute-start(f32[32,1024]{1,0:T(8,128)S(1)} %get-tuple-element.74.refs_1_), channel_id=1, source_target_pairs={{0,4},{1,5},{2,6},{3,7},{4,0},{5,1},{6,2},{7,3},{8,12},{9,13},{10,... | collective-permute-start | bytes 393224 | tf_op jit(solution)/shard_map/ppermute | solution.py:355
  48.8 2.1 %collective-permute-start.13 = (f32[32,1024]{1,0:T(8,128)S(1)}, f32[32,1024]{1,0:T(8,128)S(1)}, u32[]{:S(2)}, u32[]{:S(2)}) collective-permute-start(f32[32,1024]{1,0:T(8,128)S(1)} %get-tuple-element.73.refs_1_), channel_id=1, source_target_pairs={{0,4},{1,5},{2,6},{3,7},{4,0},{5,1},{6,2},{7,3},{8,12},{9,13},{10,... | collective-permute-start | bytes 393224 | tf_op jit(solution)/shard_map/ppermute | solution.py:355
  50.8 1.2 %prior.3.refs_5_ = f32[64,2048]{1,0:T(8,128)S(1)} custom-call(f32[32,2048]{1,0:T(8,128)S(1)} %collective-permute-done.11.refs_0_, f32[32,2048]{1,0:T(8,128)S(1)} %get-tuple-element.71.refs_1_, f32[32,2048]{1,0:T(8,128)S(1)} %get-tuple-element.72.refs_2_, f32[32,2048]{1,0:T(8,128)S(1)} %collective-permute-done.12.refs_3_, ...), custom_call_target="tpu_custom_call" | custom-call | tf_op jit(solution)/shard_map/prior/pallas_call | solution.py:59
  52.6 1.6 %collective-permute-start.22 = (f32[32,1024]{1,0:T(8,128)S(1)}, f32[32,1024]{1,0:T(8,128)S(1)}, u32[]{:S(2)}, u32[]{:S(2)}) collective-permute-start(f32[32,1024]{1,0:T(8,128)S(1)} %get-tuple-element.91), channel_id=1, source_target_pairs={{0,2},{1,3},{2,0},{3,1},{4,6},{5,7},{6,4},{7,5},{8,10},{9,11},{10,... | collective-permute-start | bytes 393224 | tf_op jit(solution)/shard_map/ppermute | solution.py:355
  55.0 1.6 %collective-permute-start.21 = (f32[32,1024]{1,0:T(8,128)S(1)}, f32[32,1024]{1,0:T(8,128)S(1)}, u32[]{:S(2)}, u32[]{:S(2)}) collective-permute-start(f32[32,1024]{1,0:T(8,128)S(1)} %get-tuple-element.87), channel_id=1, source_target_pairs={{0,3},{1,2},{2,1},{3,0},{4,7},{5,6},{6,5},{7,4},{8,11},{9,10},{10,... | collective-permute-start | bytes 393224 | tf_op jit(solution)/shard_map/ppermute | solution.py:355
  56.7 1.7 %collective-permute-done.22.refs_1_ = f32[32,1024]{1,0:T(8,128)S(1)} collective-permute-done((f32[32,1024]{1,0:T(8,128)S(1)}, f32[32,1024]{1,0:T(8,128)S(1)}, u32[]{:S(2)}, u32[]{:S(2)}) %collective-permute-start.22) | collective-permute-done | bytes 131104 | tf_op jit(solution)/shard_map/ppermute | solution.py:355
  59.2 1.4 %collective-permute-done.21.refs_1_ = f32[32,1024]{1,0:T(8,128)S(1)} collective-permute-done((f32[32,1024]{1,0:T(8,128)S(1)}, f32[32,1024]{1,0:T(8,128)S(1)}, u32[]{:S(2)}, u32[]{:S(2)}) %collective-permute-start.21) | collective-permute-done | bytes 131104 | tf_op jit(solution)/shard_map/ppermute | solution.py:355
  (60 shorter events, 9.4 us)
Async XLA Ops:
  0.6 5.9 %copy-start.2 = (bf16[2,32,2048]{2,1,0:T(8,128)(2,1)S(1)}, bf16[2,32,2048]{2,1,0:T(8,128)(2,1)}, u32[]{:S(2)}) copy-start(bf16[2,32,2048]{2,1,0:T(8,128)(2,1)} %obs_ref) | copy-start | bytes 786436
  2.6 5.3 %collective-permute-start = (f32[8,4224]{1,0:T(8,128)}, f32[8,4224]{1,0:T(8,128)S(1)}, u32[]{:S(2)}, u32[]{:S(2)}) collective-permute-start(f32[8,4224]{1,0:T(8,128)} %get-tuple-element.50), channel_id=1, source_target_pairs={{0,1},{1,0},{2,3},{3,2},{4,5},{5,4},{6,7},{7,6},{8,9},{9,8},{10,11... | collective-permute-start | bytes 405512 | tf_op jit(solution)/shard_map/ppermute | solution.py:355
  3.2 7.2 %collective-permute-start.1 = (f32[8,4224]{1,0:T(8,128)}, f32[8,4224]{1,0:T(8,128)S(1)}, u32[]{:S(2)}, u32[]{:S(2)}) collective-permute-start(f32[8,4224]{1,0:T(8,128)} %get-tuple-element.51), channel_id=1, source_target_pairs={{0,2},{1,3},{2,0},{3,1},{4,6},{5,7},{6,4},{7,5},{8,10},{9,11},{10,... | collective-permute-start | bytes 405512 | tf_op jit(solution)/shard_map/ppermute | solution.py:355
  5.8 7.1 %collective-permute-start.2 = (f32[8,4224]{1,0:T(8,128)}, f32[8,4224]{1,0:T(8,128)S(1)}, u32[]{:S(2)}, u32[]{:S(2)}) collective-permute-start(f32[8,4224]{1,0:T(8,128)} %get-tuple-element.52), channel_id=1, source_target_pairs={{0,3},{1,2},{2,1},{3,0},{4,7},{5,6},{6,5},{7,4},{8,11},{9,10},{10,... | collective-permute-start | bytes 405512 | tf_op jit(solution)/shard_map/ppermute | solution.py:355
  6.7 17.6 %collective-permute-start.6 = (f32[2,32,2048]{2,1,0:T(8,128)S(1)}, f32[2,32,2048]{2,1,0:T(8,128)S(1)}, u32[]{:S(2)}, u32[]{:S(2)}) collective-permute-start(f32[2,32,2048]{2,1,0:T(8,128)S(1)} %get-tuple-element.63), channel_id=1, source_target_pairs={{0,2},{1,3},{2,0},{3,1},{4,6},{5,7},{6,4},{7,5},{8,10},{9,11},{10,... | collective-permute-start | bytes 1572872 | tf_op jit(solution)/shard_map/ppermute | solution.py:355
  13.0 9.0 %collective-permute-start.3 = (f32[8,8448]{1,0:T(8,128)S(1)}, f32[8,8448]{1,0:T(8,128)S(1)}, u32[]{:S(2)}, u32[]{:S(2)}) collective-permute-start(f32[8,8448]{1,0:T(8,128)S(1)} %get-tuple-element.55.refs_1_.refs_4_), channel_id=1, source_target_pairs={{0,4},{1,5},{2,6},{3,7},{4,0},{5,1},{6,2},{7,3},{8,12},{9,13},{10,... | collective-permute-start | bytes 811016 | tf_op jit(solution)/shard_map/ppermute | solution.py:355
  14.6 7.3 %collective-permute-start.5 = (f32[8,8448]{1,0:T(8,128)S(1)}, f32[8,8448]{1,0:T(8,128)S(1)}, u32[]{:S(2)}, u32[]{:S(2)}) collective-permute-start(f32[8,8448]{1,0:T(8,128)S(1)} %get-tuple-element.57.refs_2_.refs_5_), channel_id=1, source_target_pairs={{0,1},{1,0},{2,3},{3,2},{4,8},{5,9},{6,10},{7,11},{8,4},{9,5},{10,... | collective-permute-start | bytes 811016 | tf_op jit(solution)/shard_map/ppermute | solution.py:355
  15.0 2.2 %collective-permute-start.4 = (f32[2,32,1024]{2,1,0:T(8,128)S(1)}, f32[2,32,1024]{2,1,0:T(8,128)S(1)}, u32[]{:S(2)}, u32[]{:S(2)}) collective-permute-start(f32[2,32,1024]{2,1,0:T(8,128)S(1)} %pad_maximum_fusion.refs_6_.refs_0_), channel_id=1, source_target_pairs={{0,1},{1,0},{2,3},{3,2},{4,5},{5,4},{6,7},{7,6},{8,9},{9,8},{10,11... | collective-permute-start | bytes 786440 | tf_op jit(solution)/shard_map/ppermute | solution.py:355
  24.9 8.1 %collective-permute-start.9 = (f32[2,32,1024]{2,1,0:T(8,128)S(1)}, f32[2,32,1024]{2,1,0:T(8,128)S(1)}, u32[]{:S(2)}, u32[]{:S(2)}) collective-permute-start(f32[2,32,1024]{2,1,0:T(8,128)S(1)} %pad_maximum_fusion.refs_6_.refs_0_), channel_id=1, source_target_pairs={{0,2},{1,3},{2,0},{3,1},{4,6},{5,7},{6,4},{7,5},{8,10},{9,11},{10,... | collective-permute-start | bytes 786440 | tf_op jit(solution)/shard_map/ppermute | solution.py:355
  26.7 7.6 %collective-permute-start.7 = (f32[32,2048]{1,0:T(8,128)S(1)}, f32[32,2048]{1,0:T(8,128)S(1)}, u32[]{:S(2)}, u32[]{:S(2)}) collective-permute-start(f32[32,2048]{1,0:T(8,128)S(1)} %get-tuple-element.66.refs_1_), channel_id=1, source_target_pairs={{0,4},{1,5},{2,6},{3,7},{4,0},{5,1},{6,2},{7,3},{8,12},{9,13},{10,... | collective-permute-start | bytes 786440 | tf_op jit(solution)/shard_map/ppermute | solution.py:355
  28.3 6.0 %collective-permute-start.8 = (f32[32,2048]{1,0:T(8,128)S(1)}, f32[32,2048]{1,0:T(8,128)S(1)}, u32[]{:S(2)}, u32[]{:S(2)}) collective-permute-start(f32[32,2048]{1,0:T(8,128)S(1)} %get-tuple-element.67.refs_2_), channel_id=1, source_target_pairs={{0,1},{1,0},{2,3},{3,2},{4,8},{5,9},{6,10},{7,11},{8,4},{9,5},{10,... | collective-permute-start | bytes 786440 | tf_op jit(solution)/shard_map/ppermute | solution.py:355
  33.0 1.6 %collective-permute-start.10 = (f32[2,32,1024]{2,1,0:T(8,128)S(1)}, f32[2,32,1024]{2,1,0:T(8,128)S(1)}, u32[]{:S(2)}, u32[]{:S(2)}) collective-permute-start(f32[2,32,1024]{2,1,0:T(8,128)S(1)} %collective-permute-done.9.refs_8_.refs_2_), channel_id=1, source_target_pairs={{0,1},{1,0},{2,3},{3,2},{4,5},{5,4},{6,7},{7,6},{8,9},{9,8},{10,11... | collective-permute-start | bytes 786440 | tf_op jit(solution)/shard_map/ppermute | solution.py:355
  36.0 8.3 %collective-permute-start.11 = (f32[32,2048]{1,0:T(8,128)S(1)}, f32[32,2048]{1,0:T(8,128)S(1)}, u32[]{:S(2)}, u32[]{:S(2)}) collective-permute-start(f32[32,2048]{1,0:T(8,128)S(1)} %get-tuple-element.71.refs_1_), channel_id=1, source_target_pairs={{0,4},{1,5},{2,6},{3,7},{4,0},{5,1},{6,2},{7,3},{8,12},{9,13},{10,... | collective-permute-start | bytes 786440 | tf_op jit(solution)/shard_map/ppermute | solution.py:355
  38.7 5.6 %collective-permute-start.12 = (f32[32,2048]{1,0:T(8,128)S(1)}, f32[32,2048]{1,0:T(8,128)S(1)}, u32[]{:S(2)}, u32[]{:S(2)}) collective-permute-start(f32[32,2048]{1,0:T(8,128)S(1)} %get-tuple-element.72.refs_2_), channel_id=1, source_target_pairs={{0,1},{1,0},{2,3},{3,2},{4,8},{5,9},{6,10},{7,11},{8,4},{9,5},{10,... | collective-permute-start | bytes 786440 | tf_op jit(solution)/shard_map/ppermute | solution.py:355
  38.7 9.8 %collective-permute-start.15 = (f32[32,1024]{1,0:T(8,128)S(1)}, f32[32,1024]{1,0:T(8,128)S(1)}, u32[]{:S(2)}, u32[]{:S(2)}) collective-permute-start(f32[32,1024]{1,0:T(8,128)S(1)} %get-tuple-element.76), channel_id=1, source_target_pairs={{0,2},{1,3},{2,0},{3,1},{4,6},{5,7},{6,4},{7,5},{8,10},{9,11},{10,... | collective-permute-start | bytes 393224 | tf_op jit(solution)/shard_map/ppermute | solution.py:355
  39.2 9.3 %collective-permute-start.16 = (f32[32,1024]{1,0:T(8,128)S(1)}, f32[32,1024]{1,0:T(8,128)S(1)}, u32[]{:S(2)}, u32[]{:S(2)}) collective-permute-start(f32[32,1024]{1,0:T(8,128)S(1)} %get-tuple-element.77), channel_id=1, source_target_pairs={{0,1},{1,0},{2,3},{3,2},{4,5},{5,4},{6,7},{7,6},{8,9},{9,8},{10,11... | collective-permute-start | bytes 393224 | tf_op jit(solution)/shard_map/ppermute | solution.py:355
  39.5 9.1 %collective-permute-start.17 = (f32[32,1024]{1,0:T(8,128)S(1)}, f32[32,1024]{1,0:T(8,128)S(1)}, u32[]{:S(2)}, u32[]{:S(2)}) collective-permute-start(f32[32,1024]{1,0:T(8,128)S(1)} %get-tuple-element.78), channel_id=1, source_target_pairs={{0,3},{1,2},{2,1},{3,0},{4,7},{5,6},{6,5},{7,4},{8,11},{9,10},{10,... | collective-permute-start | bytes 393224 | tf_op jit(solution)/shard_map/ppermute | solution.py:355
  45.7 6.6 %collective-permute-start.14 = (f32[32,1024]{1,0:T(8,128)S(1)}, f32[32,1024]{1,0:T(8,128)S(1)}, u32[]{:S(2)}, u32[]{:S(2)}) collective-permute-start(f32[32,1024]{1,0:T(8,128)S(1)} %get-tuple-element.74.refs_1_), channel_id=1, source_target_pairs={{0,4},{1,5},{2,6},{3,7},{4,0},{5,1},{6,2},{7,3},{8,12},{9,13},{10,... | collective-permute-start | bytes 393224 | tf_op jit(solution)/shard_map/ppermute | solution.py:355
  48.5 3.8 %collective-permute-start.18 = (f32[32,1024]{1,0:T(8,128)S(1)}, f32[32,1024]{1,0:T(8,128)S(1)}, u32[]{:S(2)}, u32[]{:S(2)}) collective-permute-start(f32[32,1024]{1,0:T(8,128)S(1)} %get-tuple-element.82.refs_2_), channel_id=1, source_target_pairs={{0,1},{1,0},{2,3},{3,2},{4,8},{5,9},{6,10},{7,11},{8,4},{9,5},{10,... | collective-permute-start | bytes 393224 | tf_op jit(solution)/shard_map/ppermute | solution.py:355
  48.8 6.0 %collective-permute-start.13 = (f32[32,1024]{1,0:T(8,128)S(1)}, f32[32,1024]{1,0:T(8,128)S(1)}, u32[]{:S(2)}, u32[]{:S(2)}) collective-permute-start(f32[32,1024]{1,0:T(8,128)S(1)} %get-tuple-element.73.refs_1_), channel_id=1, source_target_pairs={{0,4},{1,5},{2,6},{3,7},{4,0},{5,1},{6,2},{7,3},{8,12},{9,13},{10,... | collective-permute-start | bytes 393224 | tf_op jit(solution)/shard_map/ppermute | solution.py:355
  50.8 3.9 %collective-permute-start.19 = (f32[32,1024]{1,0:T(8,128)S(1)}, f32[32,1024]{1,0:T(8,128)S(1)}, u32[]{:S(2)}, u32[]{:S(2)}) collective-permute-start(f32[32,1024]{1,0:T(8,128)S(1)} %get-tuple-element.85.refs_2_), channel_id=1, source_target_pairs={{0,1},{1,0},{2,3},{3,2},{4,8},{5,9},{6,10},{7,11},{8,4},{9,5},{10,... | collective-permute-start | bytes 393224 | tf_op jit(solution)/shard_map/ppermute | solution.py:355
  52.6 5.8 %collective-permute-start.22 = (f32[32,1024]{1,0:T(8,128)S(1)}, f32[32,1024]{1,0:T(8,128)S(1)}, u32[]{:S(2)}, u32[]{:S(2)}) collective-permute-start(f32[32,1024]{1,0:T(8,128)S(1)} %get-tuple-element.91), channel_id=1, source_target_pairs={{0,2},{1,3},{2,0},{3,1},{4,6},{5,7},{6,4},{7,5},{8,10},{9,11},{10,... | collective-permute-start | bytes 393224 | tf_op jit(solution)/shard_map/ppermute | solution.py:355
  55.0 4.3 %collective-permute-start.20 = (f32[32,1024]{1,0:T(8,128)S(1)}, f32[32,1024]{1,0:T(8,128)S(1)}, u32[]{:S(2)}, u32[]{:S(2)}) collective-permute-start(f32[32,1024]{1,0:T(8,128)S(1)} %get-tuple-element.86), channel_id=1, source_target_pairs={{0,1},{1,0},{2,3},{3,2},{4,5},{5,4},{6,7},{7,6},{8,9},{9,8},{10,11... | collective-permute-start | bytes 393224 | tf_op jit(solution)/shard_map/ppermute | solution.py:355
  55.0 5.6 %collective-permute-start.21 = (f32[32,1024]{1,0:T(8,128)S(1)}, f32[32,1024]{1,0:T(8,128)S(1)}, u32[]{:S(2)}, u32[]{:S(2)}) collective-permute-start(f32[32,1024]{1,0:T(8,128)S(1)} %get-tuple-element.87), channel_id=1, source_target_pairs={{0,3},{1,2},{2,1},{3,0},{4,7},{5,6},{6,5},{7,4},{8,11},{9,10},{10,... | collective-permute-start | bytes 393224 | tf_op jit(solution)/shard_map/ppermute | solution.py:355
  (8 other events, 21.9 us)

commit v4 on v3

--- a/solution.py
+++ b/solution.py
@@ -101,7 +101,7 @@
         out.wait()
 
 
-def order_kernel(own_ref, core_ref, pair_ref, diag_ref, lead_ref, trail_ref):
+def order_kernel(own_ref, pair_ref, diag_ref, core_ref, lead_ref, trail_ref):
     size = own_ref.shape[1]
     for i, (own, pair) in enumerate(((own_ref, pair_ref), (core_ref, diag_ref))):
         lead, trail = lead_trail(own[...], pair[...])
@@ -237,19 +237,34 @@
     return above + below + lateral
 
 
+def rim(ref, last):
+    if ref.shape[0] > 8:
+        return ref[ref.shape[0] - 8 :, :] if last else ref[:8, :]
+    size, groups = ref.shape[1] // 2, HALF // 8
+    width = (size - 128) // groups
+    start = width * (groups - 1) if last else 0
+    return jnp.concatenate(
+        [ref[:, size * half + start : size * half + start + width] for half in range(2)], axis=1
+    )
+
+
 def prior_kernel(pairs, *refs):
-    fields = [load(ref) for ref in refs[:4]]
+    lead_ref, trail_ref = refs[0], refs[3]
+    inside = [load(ref) for ref in refs[1:3]]
     lead_edge, trail_edge = edge_row(refs[4]), edge_row(refs[5])
     out_ref, ext, wide, inner = refs[10:]
     k, y, _ = place()
-    rows, length = fields[0].shape
+    rows, length = inside[0].shape
     flip = lax.rem(k, 2) == 1
-    lead_open, trail_open = open_sides(pairs)
-    fields[0] = fields[0] * lead_open
-    fields[3] = fields[3] * trail_open
-    for block, field in enumerate(fields):
-        where = rows * jnp.where(flip, block, 3 - block)
-        ext[pl.ds(pl.multiple_of(where, rows), rows), :] = field
+    north_open = jnp.where(k == 0, 0.0, 1.0)
+    south_open = jnp.where(k == pairs - 1, 0.0, 1.0)
+    for block, field in enumerate(inside):
+        where = 16 + rows * jnp.where(flip, block, 1 - block)
+        ext[pl.ds(pl.multiple_of(where, 8), rows), :] = field
+    north = jnp.where(flip, rim(lead_ref, True), rim(trail_ref, True))
+    south = jnp.where(flip, rim(trail_ref, False), rim(lead_ref, False))
+    ext[8:16, :] = north * north_open
+    ext[16 + 2 * rows : 24 + 2 * rows, :] = south * south_open
     for block, (left, right) in enumerate(map_pairs(refs[6:10])):
         where = pl.multiple_of(8 + rows * jnp.where(y == 0, block, 1 - block), 8)
         coef = jnp.concatenate([left[0], right[0]], axis=1) + 4.0
@@ -258,17 +273,20 @@
     south = jnp.where(flip, trail_edge, lead_edge) + 4.0
     wide[:8, :] = jnp.broadcast_to(north, (8, length))
     wide[8 + 2 * rows :, :] = jnp.broadcast_to(south, (8, length))
-    low, count = rows - 8, 2 * rows + 16
-    center = ext[low : low + count, :]
-    around = beside(center, ext[low - 1 : low - 1 + count, :], ext[low + 1 : low + 1 + count, :])
+    count = 2 * rows + 16
+    ext[:8, :] = jnp.zeros((8, length), F32)
+    ext[8 + count :, :] = jnp.zeros((8, length), F32)
+    center = ext[8 : 8 + count, :]
+    around = beside(center, ext[7 : 7 + count, :], ext[9 : 9 + count, :])
     inner[...] = wide[...] * center - around
-    inner[:8, :] = inner[:8, :] * jnp.where(k == 0, 0.0, 1.0)
-    inner[8 + 2 * rows :, :] = inner[8 + 2 * rows :, :] * jnp.where(k == pairs - 1, 0.0, 1.0)
+    inner[:8, :] = inner[:8, :] * north_open
+    inner[8 + 2 * rows :, :] = inner[8 + 2 * rows :, :] * south_open
     center = inner[8 : 8 + 2 * rows, :]
     around = beside(center, inner[7 : 7 + 2 * rows, :], inner[9 : 9 + 2 * rows, :])
-    ext[: 2 * rows, :] = wide[8 : 8 + 2 * rows, :] * center - around
-    out_ref[:rows, :] = ext[pl.ds(pl.multiple_of(rows * y, rows), rows), :]
-    out_ref[rows:, :] = ext[pl.ds(pl.multiple_of(rows * (1 - y), rows), rows), :]
+    outer = wide[8 : 8 + 2 * rows, :] * center - around
+    top, bottom = outer[:rows], outer[rows:]
+    out_ref[:rows, :] = jnp.where(y == 0, top, bottom)
+    out_ref[rows:, :] = jnp.where(y == 0, bottom, top)
 
 
 def map_pairs(refs):
@@ -304,7 +322,7 @@
 
 def days_of():
     _, y, c = place()
-    return 2 * c + y, 2 * c + (1 - y), 2 * (1 - c) + y, 2 * (1 - c) + (1 - y)
+    return 2 * c + y, 2 * c + (1 - y), 2 * (1 - c) + (1 - y), 2 * (1 - c) + y
 
 
 def early_kernel(*refs):
@@ -396,7 +414,7 @@
     v_lead, v_trail = call(
         order_kernel,
         [shape(8, 2 * packed.shape[1])] * 2,
-        [own, by_core, by_pair, by_diag],
+        [own, by_pair, by_diag, by_core],
         flops=ADJOINT_COST,
         name="order",
     )
@@ -440,7 +458,7 @@
             [shape(2 * rows, length)],
             fields + edges + maps,
             scratch=[
-                pltpu.VMEM((4 * rows, length), F32),
+                pltpu.VMEM((2 * rows + 32, length), F32),
                 pltpu.VMEM((2 * rows + 16, length), F32),
                 pltpu.VMEM((2 * rows + 16, length), F32),
             ],
@@ -463,7 +481,7 @@
                 name="update",
             )
             fields = [lead(v_lead), v_lead, v_trail, trail(v_trail)]
-            pieces = [pieces[0], pair(pieces[1]), core(pieces[2]), diag(pieces[3])]
+            pieces = [pieces[0], pair(pieces[1]), diag(pieces[3]), core(pieces[2])]
             early = call(
                 early_kernel,
                 [shape(days, rows, width)] * 2,
@@ -486,7 +504,7 @@
         flops=conv,
         name="update",
     )
-    pieces = [left_own, pair(left_pair), core(right_own), diag(right_pair)]
+    pieces = [left_own, pair(left_pair), diag(right_pair), core(right_own)]
     result = []
     for half in range(2):
         args = pieces[2 * half : 2 * half + 2] + early

time: 61.7 us -> 60.7 us (0.984)
  starting transfers between devices: 23 us -> 22.3 us
    ppermute x23, starting transfers between devices: 23 us -> 22.3 us  [permute(): return lax.ppermute(array, AXES, moves)]
  transfers between devices with their start and end apart: 23 -> 23, of which waited for: 11 -> 12; matrix products, arithmetic and copies ran while one was open for 0% -> 0% of each run, Pallas kernels for 12% -> 12%
where the time goes in v4:
time: 60.7 us; the launch traced here: 60.5 us
  waiting for transfers between devices  24.8 us (41%)
  starting transfers between devices  22.3 us (37%)
  Pallas kernels  11.9 us (20%)
  between operations  0.88 us (1%)
  local copies, waits for them, and re-layouts  0.63 us (1%)
    ppermute x23, waiting for transfers between devices, permute(): return lax.ppermute(array, AXES, moves)  24.8 us
    ppermute x23, starting transfers between devices, permute(): return lax.ppermute(array, AXES, moves)  22.3 us
    pallas_call x17, Pallas kernels, call(): pl.pallas_call(kernel, out_shape=out_shape, in_specs=specs or [VMEM] * le...  11.9 us
  transfers between devices with their start and end apart: 23, of which 12 were waited for; matrix products, arithmetic and copies ran while one was open for 0% of the time, Pallas kernels for 12%

profile of v4, /device:TPU:0, one launch (start us, length us, event | category | flops | bytes accessed | tf_op | source)
XLA Modules:
  0.0 60.5 jit_solution(9557206907842660541)
XLA Ops:
  0.6 2.0 %pack.1 = (f32[8,4224]{1,0:T(8,128)}, f32[8,4224]{1,0:T(8,128)}, f32[8,4224]{1,0:T(8,128)}, f32[8,4224]{1,0:T(8,128)}) custom-call(f32[4,32,1024]{2,1,0:T(8,128)} %refs_4_.1, s32[32,1024]{1,0:T(8,128)} %refs_5_.1, f32[32,1024]{1,0:T(8,128)} %coef_ref.1), custom_call_target="tpu_custom_call" | custom-call | tf_op jit(solution)/shard_map/pack/pallas_call | solution.py:59
  2.6 3.0 %collective-permute-start = (f32[8,4224]{1,0:T(8,128)}, f32[8,4224]{1,0:T(8,128)S(1)}, u32[]{:S(2)}, u32[]{:S(2)}) collective-permute-start(f32[8,4224]{1,0:T(8,128)} %get-tuple-element.50), channel_id=1, source_target_pairs={{0,2},{1,3},{2,0},{3,1},{4,6},{5,7},{6,4},{7,5},{8,10},{9,11},{10,... | collective-permute-start | bytes 405512 | tf_op jit(solution)/shard_map/ppermute | solution.py:373
  6.6 1.5 %collective-permute-start.6 = (f32[2,32,2048]{2,1,0:T(8,128)S(1)}, f32[2,32,2048]{2,1,0:T(8,128)S(1)}, u32[]{:S(2)}, u32[]{:S(2)}) collective-permute-start(f32[2,32,2048]{2,1,0:T(8,128)S(1)} %get-tuple-element.63), channel_id=1, source_target_pairs={{0,2},{1,3},{2,0},{3,1},{4,6},{5,7},{6,4},{7,5},{8,10},{9,11},{10,... | collective-permute-start | bytes 1572872 | tf_op jit(solution)/shard_map/ppermute | solution.py:373
  8.2 1.8 %collective-permute-done.pair_ref = f32[8,4224]{1,0:T(8,128)S(1)} collective-permute-done((f32[8,4224]{1,0:T(8,128)}, f32[8,4224]{1,0:T(8,128)S(1)}, u32[]{:S(2)}, u32[]{:S(2)}) %collective-permute-start) | collective-permute-done | bytes 135200 | tf_op jit(solution)/shard_map/ppermute | solution.py:373
  10.0 2.9 %collective-permute-done.1.diag_ref = f32[8,4224]{1,0:T(8,128)S(1)} collective-permute-done((f32[8,4224]{1,0:T(8,128)}, f32[8,4224]{1,0:T(8,128)S(1)}, u32[]{:S(2)}, u32[]{:S(2)}) %collective-permute-start.1) | collective-permute-done | bytes 135200 | tf_op jit(solution)/shard_map/ppermute | solution.py:373
  13.0 1.6 %collective-permute-start.3 = (f32[8,8448]{1,0:T(8,128)S(1)}, f32[8,8448]{1,0:T(8,128)S(1)}, u32[]{:S(2)}, u32[]{:S(2)}) collective-permute-start(f32[8,8448]{1,0:T(8,128)S(1)} %get-tuple-element.55.refs_1_.refs_4_), channel_id=1, source_target_pairs={{0,4},{1,5},{2,6},{3,7},{4,0},{5,1},{6,2},{7,3},{8,12},{9,13},{10,... | collective-permute-start | bytes 811016 | tf_op jit(solution)/shard_map/ppermute | solution.py:373
  15.1 2.1 %matrices.1 = (bf16[128,256]{1,0:T(8,128)(2,1)S(1)}, bf16[128,256]{1,0:T(8,128)(2,1)S(1)}, bf16[2,512,256]{2,1,0:T(8,128)(2,1)S(1)}, bf16[2,512,256]{2,1,0:T(8,128)(2,1)S(1)}) custom-call(f32[65]{0:T(128)S(1)} %copy-done.5, f32[65]{0:T(128)S(1)} %copy-done.6), custom_call_target="tpu_custom_call" | custom-call | flops 36400000 | bytes 520 | tf_op jit(solution)/shard_map/matrices/pallas_call | solution.py:59
  17.3 4.4 %collective-permute-done.3.refs_0_.refs_4_ = f32[8,8448]{1,0:T(8,128)S(1)} collective-permute-done((f32[8,8448]{1,0:T(8,128)S(1)}, f32[8,8448]{1,0:T(8,128)S(1)}, u32[]{:S(2)}, u32[]{:S(2)}) %collective-permute-start.3) | collective-permute-done | bytes 270368 | tf_op jit(solution)/shard_map/ppermute | solution.py:373
  22.5 1.1 %collective-permute-done.6.sent_ref = f32[2,32,2048]{2,1,0:T(8,128)S(1)} collective-permute-done((f32[2,32,2048]{2,1,0:T(8,128)S(1)}, f32[2,32,2048]{2,1,0:T(8,128)S(1)}, u32[]{:S(2)}, u32[]{:S(2)}) %collective-permute-start.6) | collective-permute-done | bytes 524320 | tf_op jit(solution)/shard_map/ppermute | solution.py:373
  24.2 1.8 %collective-permute-start.9 = (f32[2,32,1024]{2,1,0:T(8,128)S(1)}, f32[2,32,1024]{2,1,0:T(8,128)S(1)}, u32[]{:S(2)}, u32[]{:S(2)}) collective-permute-start(f32[2,32,1024]{2,1,0:T(8,128)S(1)} %pad_maximum_fusion.refs_6_.refs_0_), channel_id=1, source_target_pairs={{0,2},{1,3},{2,0},{3,1},{4,6},{5,7},{6,4},{7,5},{8,10},{9,11},{10,... | collective-permute-start | bytes 786440 | tf_op jit(solution)/shard_map/ppermute | solution.py:373
  26.0 1.6 %collective-permute-start.7 = (f32[32,2048]{1,0:T(8,128)S(1)}, f32[32,2048]{1,0:T(8,128)S(1)}, u32[]{:S(2)}, u32[]{:S(2)}) collective-permute-start(f32[32,2048]{1,0:T(8,128)S(1)} %get-tuple-element.66.refs_1_), channel_id=1, source_target_pairs={{0,4},{1,5},{2,6},{3,7},{4,0},{5,1},{6,2},{7,3},{8,12},{9,13},{10,... | collective-permute-start | bytes 786440 | tf_op jit(solution)/shard_map/ppermute | solution.py:373
  27.6 4.5 %collective-permute-done.9.refs_8_.refs_2_ = f32[2,32,1024]{2,1,0:T(8,128)S(1)} collective-permute-done((f32[2,32,1024]{2,1,0:T(8,128)S(1)}, f32[2,32,1024]{2,1,0:T(8,128)S(1)}, u32[]{:S(2)}, u32[]{:S(2)}) %collective-permute-start.9) | collective-permute-done | bytes 262176 | tf_op jit(solution)/shard_map/ppermute | solution.py:373
  32.1 1.1 %collective-permute-done.7.refs_0_ = f32[32,2048]{1,0:T(8,128)S(1)} collective-permute-done((f32[32,2048]{1,0:T(8,128)S(1)}, f32[32,2048]{1,0:T(8,128)S(1)}, u32[]{:S(2)}, u32[]{:S(2)}) %collective-permute-start.7) | collective-permute-done | bytes 262176 | tf_op jit(solution)/shard_map/ppermute | solution.py:373
  33.6 1.0 %prior.2.prior_ref = f32[64,2048]{1,0:T(8,128)S(1)} custom-call(f32[8,8448]{1,0:T(8,128)S(1)} %collective-permute-done.3.refs_0_.refs_4_, f32[8,8448]{1,0:T(8,128)S(1)} %get-tuple-element.55.refs_1_.refs_4_, f32[8,8448]{1,0:T(8,128)S(1)} %get-tuple-element.57.refs_2_.refs_5_, f32[8,8448]{1,0:T(8,128)S(1)} %collective-permute-done.5.refs_3_.refs_5_, ...), custom_call_target="tpu_custom_call" | custom-call | tf_op jit(solution)/shard_map/prior/pallas_call | solution.py:59
  34.8 2.4 %collective-permute-start.11 = (f32[32,2048]{1,0:T(8,128)S(1)}, f32[32,2048]{1,0:T(8,128)S(1)}, u32[]{:S(2)}, u32[]{:S(2)}) collective-permute-start(f32[32,2048]{1,0:T(8,128)S(1)} %get-tuple-element.71.refs_1_), channel_id=1, source_target_pairs={{0,4},{1,5},{2,6},{3,7},{4,0},{5,1},{6,2},{7,3},{8,12},{9,13},{10,... | collective-permute-start | bytes 786440 | tf_op jit(solution)/shard_map/ppermute | solution.py:373
  38.0 1.0 %collective-permute-start.16 = (f32[32,1024]{1,0:T(8,128)S(1)}, f32[32,1024]{1,0:T(8,128)S(1)}, u32[]{:S(2)}, u32[]{:S(2)}) collective-permute-start(f32[32,1024]{1,0:T(8,128)S(1)} %get-tuple-element.77), channel_id=1, source_target_pairs={{0,3},{1,2},{2,1},{3,0},{4,7},{5,6},{6,5},{7,4},{8,11},{9,10},{10,... | collective-permute-start | bytes 393224 | tf_op jit(solution)/shard_map/ppermute | solution.py:373
  39.3 3.9 %collective-permute-done.11.refs_0_ = f32[32,2048]{1,0:T(8,128)S(1)} collective-permute-done((f32[32,2048]{1,0:T(8,128)S(1)}, f32[32,2048]{1,0:T(8,128)S(1)}, u32[]{:S(2)}, u32[]{:S(2)}) %collective-permute-start.11) | collective-permute-done | bytes 262176 | tf_op jit(solution)/shard_map/ppermute | solution.py:373
  44.6 2.7 %collective-permute-start.14 = (f32[32,1024]{1,0:T(8,128)S(1)}, f32[32,1024]{1,0:T(8,128)S(1)}, u32[]{:S(2)}, u32[]{:S(2)}) collective-permute-start(f32[32,1024]{1,0:T(8,128)S(1)} %get-tuple-element.74.refs_1_), channel_id=1, source_target_pairs={{0,4},{1,5},{2,6},{3,7},{4,0},{5,1},{6,2},{7,3},{8,12},{9,13},{10,... | collective-permute-start | bytes 393224 | tf_op jit(solution)/shard_map/ppermute | solution.py:373
  47.5 2.1 %collective-permute-start.13 = (f32[32,1024]{1,0:T(8,128)S(1)}, f32[32,1024]{1,0:T(8,128)S(1)}, u32[]{:S(2)}, u32[]{:S(2)}) collective-permute-start(f32[32,1024]{1,0:T(8,128)S(1)} %get-tuple-element.73.refs_1_), channel_id=1, source_target_pairs={{0,4},{1,5},{2,6},{3,7},{4,0},{5,1},{6,2},{7,3},{8,12},{9,13},{10,... | collective-permute-start | bytes 393224 | tf_op jit(solution)/shard_map/ppermute | solution.py:373
  49.6 1.0 %prior.3.refs_5_ = f32[64,2048]{1,0:T(8,128)S(1)} custom-call(f32[32,2048]{1,0:T(8,128)S(1)} %collective-permute-done.11.refs_0_, f32[32,2048]{1,0:T(8,128)S(1)} %get-tuple-element.71.refs_1_, f32[32,2048]{1,0:T(8,128)S(1)} %get-tuple-element.72.refs_2_, f32[32,2048]{1,0:T(8,128)S(1)} %collective-permute-done.12.refs_3_, ...), custom_call_target="tpu_custom_call" | custom-call | tf_op jit(solution)/shard_map/prior/pallas_call | solution.py:59
  51.4 1.3 %collective-permute-start.22 = (f32[32,1024]{1,0:T(8,128)S(1)}, f32[32,1024]{1,0:T(8,128)S(1)}, u32[]{:S(2)}, u32[]{:S(2)}) collective-permute-start(f32[32,1024]{1,0:T(8,128)S(1)} %get-tuple-element.91), channel_id=1, source_target_pairs={{0,2},{1,3},{2,0},{3,1},{4,6},{5,7},{6,4},{7,5},{8,10},{9,11},{10,... | collective-permute-start | bytes 393224 | tf_op jit(solution)/shard_map/ppermute | solution.py:373
  52.6 0.9 %collective-permute-done.13.refs_0_ = f32[32,1024]{1,0:T(8,128)S(1)} collective-permute-done((f32[32,1024]{1,0:T(8,128)S(1)}, f32[32,1024]{1,0:T(8,128)S(1)}, u32[]{:S(2)}, u32[]{:S(2)}) %collective-permute-start.13) | collective-permute-done | bytes 131104 | tf_op jit(solution)/shard_map/ppermute | solution.py:373
  55.1 1.8 %collective-permute-done.22.refs_1_ = f32[32,1024]{1,0:T(8,128)S(1)} collective-permute-done((f32[32,1024]{1,0:T(8,128)S(1)}, f32[32,1024]{1,0:T(8,128)S(1)}, u32[]{:S(2)}, u32[]{:S(2)}) %collective-permute-start.22) | collective-permute-done | bytes 131104 | tf_op jit(solution)/shard_map/ppermute | solution.py:373
  57.7 1.9 %collective-permute-done.20.refs_0_ = f32[32,1024]{1,0:T(8,128)S(1)} collective-permute-done((f32[32,1024]{1,0:T(8,128)S(1)}, f32[32,1024]{1,0:T(8,128)S(1)}, u32[]{:S(2)}, u32[]{:S(2)}) %collective-permute-start.20) | collective-permute-done | bytes 131104 | tf_op jit(solution)/shard_map/ppermute | solution.py:373
  (60 shorter events, 10.3 us)
Async XLA Ops:
  0.6 5.8 %copy-start.2 = (bf16[2,32,2048]{2,1,0:T(8,128)(2,1)S(1)}, bf16[2,32,2048]{2,1,0:T(8,128)(2,1)}, u32[]{:S(2)}) copy-start(bf16[2,32,2048]{2,1,0:T(8,128)(2,1)} %obs_ref) | copy-start | bytes 786436
  2.6 7.4 %collective-permute-start = (f32[8,4224]{1,0:T(8,128)}, f32[8,4224]{1,0:T(8,128)S(1)}, u32[]{:S(2)}, u32[]{:S(2)}) collective-permute-start(f32[8,4224]{1,0:T(8,128)} %get-tuple-element.50), channel_id=1, source_target_pairs={{0,2},{1,3},{2,0},{3,1},{4,6},{5,7},{6,4},{7,5},{8,10},{9,11},{10,... | collective-permute-start | bytes 405512 | tf_op jit(solution)/shard_map/ppermute | solution.py:373
  5.7 7.2 %collective-permute-start.1 = (f32[8,4224]{1,0:T(8,128)}, f32[8,4224]{1,0:T(8,128)S(1)}, u32[]{:S(2)}, u32[]{:S(2)}) collective-permute-start(f32[8,4224]{1,0:T(8,128)} %get-tuple-element.51), channel_id=1, source_target_pairs={{0,3},{1,2},{2,1},{3,0},{4,7},{5,6},{6,5},{7,4},{8,11},{9,10},{10,... | collective-permute-start | bytes 405512 | tf_op jit(solution)/shard_map/ppermute | solution.py:373
  5.7 7.2 %collective-permute-start.2 = (f32[8,4224]{1,0:T(8,128)}, f32[8,4224]{1,0:T(8,128)S(1)}, u32[]{:S(2)}, u32[]{:S(2)}) collective-permute-start(f32[8,4224]{1,0:T(8,128)} %get-tuple-element.52), channel_id=1, source_target_pairs={{0,1},{1,0},{2,3},{3,2},{4,5},{5,4},{6,7},{7,6},{8,9},{9,8},{10,11... | collective-permute-start | bytes 405512 | tf_op jit(solution)/shard_map/ppermute | solution.py:373
  6.6 17.0 %collective-permute-start.6 = (f32[2,32,2048]{2,1,0:T(8,128)S(1)}, f32[2,32,2048]{2,1,0:T(8,128)S(1)}, u32[]{:S(2)}, u32[]{:S(2)}) collective-permute-start(f32[2,32,2048]{2,1,0:T(8,128)S(1)} %get-tuple-element.63), channel_id=1, source_target_pairs={{0,2},{1,3},{2,0},{3,1},{4,6},{5,7},{6,4},{7,5},{8,10},{9,11},{10,... | collective-permute-start | bytes 1572872 | tf_op jit(solution)/shard_map/ppermute | solution.py:373
  13.0 8.6 %collective-permute-start.3 = (f32[8,8448]{1,0:T(8,128)S(1)}, f32[8,8448]{1,0:T(8,128)S(1)}, u32[]{:S(2)}, u32[]{:S(2)}) collective-permute-start(f32[8,8448]{1,0:T(8,128)S(1)} %get-tuple-element.55.refs_1_.refs_4_), channel_id=1, source_target_pairs={{0,4},{1,5},{2,6},{3,7},{4,0},{5,1},{6,2},{7,3},{8,12},{9,13},{10,... | collective-permute-start | bytes 811016 | tf_op jit(solution)/shard_map/ppermute | solution.py:373
  14.6 7.0 %collective-permute-start.5 = (f32[8,8448]{1,0:T(8,128)S(1)}, f32[8,8448]{1,0:T(8,128)S(1)}, u32[]{:S(2)}, u32[]{:S(2)}) collective-permute-start(f32[8,8448]{1,0:T(8,128)S(1)} %get-tuple-element.57.refs_2_.refs_5_), channel_id=1, source_target_pairs={{0,1},{1,0},{2,3},{3,2},{4,8},{5,9},{6,10},{7,11},{8,4},{9,5},{10,... | collective-permute-start | bytes 811016 | tf_op jit(solution)/shard_map/ppermute | solution.py:373
  14.7 2.6 %collective-permute-start.4 = (f32[2,32,1024]{2,1,0:T(8,128)S(1)}, f32[2,32,1024]{2,1,0:T(8,128)S(1)}, u32[]{:S(2)}, u32[]{:S(2)}) collective-permute-start(f32[2,32,1024]{2,1,0:T(8,128)S(1)} %pad_maximum_fusion.refs_6_.refs_0_), channel_id=1, source_target_pairs={{0,1},{1,0},{2,3},{3,2},{4,5},{5,4},{6,7},{7,6},{8,9},{9,8},{10,11... | collective-permute-start | bytes 786440 | tf_op jit(solution)/shard_map/ppermute | solution.py:373
  24.2 7.9 %collective-permute-start.9 = (f32[2,32,1024]{2,1,0:T(8,128)S(1)}, f32[2,32,1024]{2,1,0:T(8,128)S(1)}, u32[]{:S(2)}, u32[]{:S(2)}) collective-permute-start(f32[2,32,1024]{2,1,0:T(8,128)S(1)} %pad_maximum_fusion.refs_6_.refs_0_), channel_id=1, source_target_pairs={{0,2},{1,3},{2,0},{3,1},{4,6},{5,7},{6,4},{7,5},{8,10},{9,11},{10,... | collective-permute-start | bytes 786440 | tf_op jit(solution)/shard_map/ppermute | solution.py:373
  26.0 7.1 %collective-permute-start.7 = (f32[32,2048]{1,0:T(8,128)S(1)}, f32[32,2048]{1,0:T(8,128)S(1)}, u32[]{:S(2)}, u32[]{:S(2)}) collective-permute-start(f32[32,2048]{1,0:T(8,128)S(1)} %get-tuple-element.66.refs_1_), channel_id=1, source_target_pairs={{0,4},{1,5},{2,6},{3,7},{4,0},{5,1},{6,2},{7,3},{8,12},{9,13},{10,... | collective-permute-start | bytes 786440 | tf_op jit(solution)/shard_map/ppermute | solution.py:373
  27.6 5.5 %collective-permute-start.8 = (f32[32,2048]{1,0:T(8,128)S(1)}, f32[32,2048]{1,0:T(8,128)S(1)}, u32[]{:S(2)}, u32[]{:S(2)}) collective-permute-start(f32[32,2048]{1,0:T(8,128)S(1)} %get-tuple-element.67.refs_2_), channel_id=1, source_target_pairs={{0,1},{1,0},{2,3},{3,2},{4,8},{5,9},{6,10},{7,11},{8,4},{9,5},{10,... | collective-permute-start | bytes 786440 | tf_op jit(solution)/shard_map/ppermute | solution.py:373
  32.0 1.5 %collective-permute-start.10 = (f32[2,32,1024]{2,1,0:T(8,128)S(1)}, f32[2,32,1024]{2,1,0:T(8,128)S(1)}, u32[]{:S(2)}, u32[]{:S(2)}) collective-permute-start(f32[2,32,1024]{2,1,0:T(8,128)S(1)} %collective-permute-done.9.refs_8_.refs_2_), channel_id=1, source_target_pairs={{0,1},{1,0},{2,3},{3,2},{4,5},{5,4},{6,7},{7,6},{8,9},{9,8},{10,11... | collective-permute-start | bytes 786440 | tf_op jit(solution)/shard_map/ppermute | solution.py:373
  34.8 8.4 %collective-permute-start.11 = (f32[32,2048]{1,0:T(8,128)S(1)}, f32[32,2048]{1,0:T(8,128)S(1)}, u32[]{:S(2)}, u32[]{:S(2)}) collective-permute-start(f32[32,2048]{1,0:T(8,128)S(1)} %get-tuple-element.71.refs_1_), channel_id=1, source_target_pairs={{0,4},{1,5},{2,6},{3,7},{4,0},{5,1},{6,2},{7,3},{8,12},{9,13},{10,... | collective-permute-start | bytes 786440 | tf_op jit(solution)/shard_map/ppermute | solution.py:373
  37.2 6.0 %collective-permute-start.12 = (f32[32,2048]{1,0:T(8,128)S(1)}, f32[32,2048]{1,0:T(8,128)S(1)}, u32[]{:S(2)}, u32[]{:S(2)}) collective-permute-start(f32[32,2048]{1,0:T(8,128)S(1)} %get-tuple-element.72.refs_2_), channel_id=1, source_target_pairs={{0,1},{1,0},{2,3},{3,2},{4,8},{5,9},{6,10},{7,11},{8,4},{9,5},{10,... | collective-permute-start | bytes 786440 | tf_op jit(solution)/shard_map/ppermute | solution.py:373
  37.2 10.2 %collective-permute-start.15 = (f32[32,1024]{1,0:T(8,128)S(1)}, f32[32,1024]{1,0:T(8,128)S(1)}, u32[]{:S(2)}, u32[]{:S(2)}) collective-permute-start(f32[32,1024]{1,0:T(8,128)S(1)} %get-tuple-element.76), channel_id=1, source_target_pairs={{0,2},{1,3},{2,0},{3,1},{4,6},{5,7},{6,4},{7,5},{8,10},{9,11},{10,... | collective-permute-start | bytes 393224 | tf_op jit(solution)/shard_map/ppermute | solution.py:373
  38.0 9.3 %collective-permute-start.16 = (f32[32,1024]{1,0:T(8,128)S(1)}, f32[32,1024]{1,0:T(8,128)S(1)}, u32[]{:S(2)}, u32[]{:S(2)}) collective-permute-start(f32[32,1024]{1,0:T(8,128)S(1)} %get-tuple-element.77), channel_id=1, source_target_pairs={{0,3},{1,2},{2,1},{3,0},{4,7},{5,6},{6,5},{7,4},{8,11},{9,10},{10,... | collective-permute-start | bytes 393224 | tf_op jit(solution)/shard_map/ppermute | solution.py:373
  39.0 8.3 %collective-permute-start.17 = (f32[32,1024]{1,0:T(8,128)S(1)}, f32[32,1024]{1,0:T(8,128)S(1)}, u32[]{:S(2)}, u32[]{:S(2)}) collective-permute-start(f32[32,1024]{1,0:T(8,128)S(1)} %get-tuple-element.78), channel_id=1, source_target_pairs={{0,1},{1,0},{2,3},{3,2},{4,5},{5,4},{6,7},{7,6},{8,9},{9,8},{10,11... | collective-permute-start | bytes 393224 | tf_op jit(solution)/shard_map/ppermute | solution.py:373
  44.6 6.5 %collective-permute-start.14 = (f32[32,1024]{1,0:T(8,128)S(1)}, f32[32,1024]{1,0:T(8,128)S(1)}, u32[]{:S(2)}, u32[]{:S(2)}) collective-permute-start(f32[32,1024]{1,0:T(8,128)S(1)} %get-tuple-element.74.refs_1_), channel_id=1, source_target_pairs={{0,4},{1,5},{2,6},{3,7},{4,0},{5,1},{6,2},{7,3},{8,12},{9,13},{10,... | collective-permute-start | bytes 393224 | tf_op jit(solution)/shard_map/ppermute | solution.py:373
  47.3 3.8 %collective-permute-start.18 = (f32[32,1024]{1,0:T(8,128)S(1)}, f32[32,1024]{1,0:T(8,128)S(1)}, u32[]{:S(2)}, u32[]{:S(2)}) collective-permute-start(f32[32,1024]{1,0:T(8,128)S(1)} %get-tuple-element.82.refs_2_), channel_id=1, source_target_pairs={{0,1},{1,0},{2,3},{3,2},{4,8},{5,9},{6,10},{7,11},{8,4},{9,5},{10,... | collective-permute-start | bytes 393224 | tf_op jit(solution)/shard_map/ppermute | solution.py:373
  47.5 6.0 %collective-permute-start.13 = (f32[32,1024]{1,0:T(8,128)S(1)}, f32[32,1024]{1,0:T(8,128)S(1)}, u32[]{:S(2)}, u32[]{:S(2)}) collective-permute-start(f32[32,1024]{1,0:T(8,128)S(1)} %get-tuple-element.73.refs_1_), channel_id=1, source_target_pairs={{0,4},{1,5},{2,6},{3,7},{4,0},{5,1},{6,2},{7,3},{8,12},{9,13},{10,... | collective-permute-start | bytes 393224 | tf_op jit(solution)/shard_map/ppermute | solution.py:373
  49.6 3.9 %collective-permute-start.19 = (f32[32,1024]{1,0:T(8,128)S(1)}, f32[32,1024]{1,0:T(8,128)S(1)}, u32[]{:S(2)}, u32[]{:S(2)}) collective-permute-start(f32[32,1024]{1,0:T(8,128)S(1)} %get-tuple-element.85.refs_2_), channel_id=1, source_target_pairs={{0,1},{1,0},{2,3},{3,2},{4,8},{5,9},{6,10},{7,11},{8,4},{9,5},{10,... | collective-permute-start | bytes 393224 | tf_op jit(solution)/shard_map/ppermute | solution.py:373
  51.4 5.5 %collective-permute-start.22 = (f32[32,1024]{1,0:T(8,128)S(1)}, f32[32,1024]{1,0:T(8,128)S(1)}, u32[]{:S(2)}, u32[]{:S(2)}) collective-permute-start(f32[32,1024]{1,0:T(8,128)S(1)} %get-tuple-element.91), channel_id=1, source_target_pairs={{0,2},{1,3},{2,0},{3,1},{4,6},{5,7},{6,4},{7,5},{8,10},{9,11},{10,... | collective-permute-start | bytes 393224 | tf_op jit(solution)/shard_map/ppermute | solution.py:373
  53.7 5.9 %collective-permute-start.20 = (f32[32,1024]{1,0:T(8,128)S(1)}, f32[32,1024]{1,0:T(8,128)S(1)}, u32[]{:S(2)}, u32[]{:S(2)}) collective-permute-start(f32[32,1024]{1,0:T(8,128)S(1)} %get-tuple-element.86), channel_id=1, source_target_pairs={{0,3},{1,2},{2,1},{3,0},{4,7},{5,6},{6,5},{7,4},{8,11},{9,10},{10,... | collective-permute-start | bytes 393224 | tf_op jit(solution)/shard_map/ppermute | solution.py:373
  54.3 5.3 %collective-permute-start.21 = (f32[32,1024]{1,0:T(8,128)S(1)}, f32[32,1024]{1,0:T(8,128)S(1)}, u32[]{:S(2)}, u32[]{:S(2)}) collective-permute-start(f32[32,1024]{1,0:T(8,128)S(1)} %get-tuple-element.87), channel_id=1, source_target_pairs={{0,1},{1,0},{2,3},{3,2},{4,5},{5,4},{6,7},{7,6},{8,9},{9,8},{10,11... | collective-permute-start | bytes 393224 | tf_op jit(solution)/shard_map/ppermute | solution.py:373
  (8 other events, 22.1 us)

commit v5 on v4

--- a/solution.py
+++ b/solution.py
@@ -69,10 +69,11 @@
     )(*args))
 
 
-def pack_kernel(guess_ref, land_ref, coef_ref, own_ref, core_ref, pair_ref, diag_ref, *scratch):
+def pack_kernel(own, guess_ref, land_ref, coef_ref, first_ref, second_ref, *scratch):
     guess, land, coef, packed, sems = scratch
     _, y, c = place()
-    days = (2 * c + (1 - y), 2 * (1 - c) + (1 - y), 2 * (1 - c) + y, 2 * c + y)
+    row = y if own else 1 - y
+    days = (2 * c + row, 2 * (1 - c) + row)
     rows, width = land.shape
     start = pl.multiple_of((rows - 8) * y, 8)
     copies = [
@@ -88,14 +89,14 @@
     edge = jnp.where(y == 0, coef[:1, :], coef[7:, :])
     edge = jnp.concatenate([edge[:, i : i + 128] for i in range(0, width, 128)], axis=0)
     outs = []
-    for i, ref in enumerate((pair_ref, diag_ref, core_ref, own_ref)):
+    for i, ref in enumerate((first_ref, second_ref)):
         copies[2 + i].wait()
         for group in range(rows // 8):
             part = slice(8 * group, 8 * group + 8)
             sea = land[part, :].astype(F32)
             packed[i, :, width * group : width * (group + 1)] = guess[i, part, :] * sea
         packed[i, :, width * (rows // 8) :] = edge
-        outs.append(pltpu.make_async_copy(packed.at[i], ref, sems.at[6 + i]))
+        outs.append(pltpu.make_async_copy(packed.at[i], ref, sems.at[4 + i]))
         outs[-1].start()
     for out in outs:
         out.wait()
@@ -384,22 +385,27 @@
 
     piece = shape(rows, width)
     packed = shape(8, rows // 8 * width + 128)
-    own, to_core, to_pair, to_diag = call(
-        pack_kernel,
-        [packed] * 4,
-        [first_guess, land_sea, range_coef],
-        [HBM] * 3,
-        scratch=[
-            pltpu.VMEM((4, rows, width), F32),
-            pltpu.VMEM((rows, width), jnp.int32),
-            pltpu.VMEM((8, width), F32),
-            pltpu.VMEM((4,) + packed.shape, F32),
-            pltpu.SemaphoreType.DMA((10,)),
-        ],
-        outs=[HBM] * 4,
-        vmem=PACK_VMEM,
-        name="pack",
-    )
+    def pack(is_own, land):
+        return call(
+            functools.partial(pack_kernel, is_own),
+            [packed] * 2,
+            [first_guess, land, range_coef],
+            [HBM] * 3,
+            outs=[HBM] * 2,
+            scratch=[
+                pltpu.VMEM((2, rows, width), F32),
+                pltpu.VMEM((rows, width), jnp.int32),
+                pltpu.VMEM((8, width), F32),
+                pltpu.VMEM((2,) + packed.shape, F32),
+                pltpu.SemaphoreType.DMA((6,)),
+            ],
+            vmem=PACK_VMEM,
+            name="pack",
+        )
+
+    to_pair, to_diag = pack(False, land_sea)
+    land, to_pair = lax.optimization_barrier((land_sea, to_pair))
+    own, to_core = pack(True, land)
     by_pair, by_diag = pair(to_pair), diag(to_diag)
     observations, own = lax.optimization_barrier((observations, own))
     by_core = core(to_core)

time: 60.7 us -> 60.5 us (level)
  waiting for transfers between devices: 24.8 us -> 22.2 us
  Pallas kernels: 11.9 us -> 13.5 us
  starting transfers between devices: 22.3 us -> 23 us
    ppermute x23, waiting for transfers between devices: 24.8 us -> 22.2 us  [permute(): return lax.ppermute(array, AXES, moves)]
    pallas_call x17 -> x18, Pallas kernels: 11.9 us -> 13.5 us  [call(): pl.pallas_call(kernel, out_shape=out_shape, in_specs=specs or [VMEM] * le...]
    ppermute x23, starting transfers between devices: 22.3 us -> 23 us  [permute(): return lax.ppermute(array, AXES, moves)]
  transfers between devices with their start and end apart: 23 -> 23, of which waited for: 12 -> 11; matrix products, arithmetic and copies ran while one was open for 0% -> 0% of each run, Pallas kernels for 12% -> 15%
where the time goes in v5:
time: 60.5 us; the launch traced here: 60.3 us
  starting transfers between devices  23 us (38%)
  waiting for transfers between devices  22.2 us (37%)
  Pallas kernels  13.5 us (22%)
  between operations  0.88 us (1%)
    ppermute x23, starting transfers between devices, permute(): return lax.ppermute(array, AXES, moves)  23 us
    ppermute x23, waiting for transfers between devices, permute(): return lax.ppermute(array, AXES, moves)  22.2 us
    pallas_call x18, Pallas kernels, call(): pl.pallas_call(kernel, out_shape=out_shape, in_specs=specs or [VMEM] * le...  13.5 us
  transfers between devices with their start and end apart: 23, of which 11 were waited for; matrix products, arithmetic and copies ran while one was open for 0% of the time, Pallas kernels for 15%

profile of v5, /device:TPU:0, one launch (start us, length us, event | category | flops | bytes accessed | tf_op | source)
XLA Modules:
  0.0 60.3 jit_solution(9958730488002022171)
XLA Ops:
  0.6 1.8 %pack.2 = (f32[8,4224]{1,0:T(8,128)}, f32[8,4224]{1,0:T(8,128)}) custom-call(f32[4,32,1024]{2,1,0:T(8,128)} %refs_4_.1, s32[32,1024]{1,0:T(8,128)} %refs_5_.1, f32[32,1024]{1,0:T(8,128)} %coef_ref.3), custom_call_target="tpu_custom_call" | custom-call | tf_op jit(solution)/shard_map/pack/pallas_call | solution.py:59
  2.4 3.0 %collective-permute-start = (f32[8,4224]{1,0:T(8,128)}, f32[8,4224]{1,0:T(8,128)S(1)}, u32[]{:S(2)}, u32[]{:S(2)}) collective-permute-start(f32[8,4224]{1,0:T(8,128)} %get-tuple-element.54), channel_id=1, source_target_pairs={{0,2},{1,3},{2,0},{3,1},{4,6},{5,7},{6,4},{7,5},{8,10},{9,11},{10,... | collective-permute-start | bytes 405512 | tf_op jit(solution)/shard_map/ppermute | solution.py:374
  5.4 1.8 %pack.3 = (f32[8,4224]{1,0:T(8,128)}, f32[8,4224]{1,0:T(8,128)}) custom-call(f32[4,32,1024]{2,1,0:T(8,128)} %refs_4_.1, s32[32,1024]{1,0:T(8,128)} %refs_5_.1, f32[32,1024]{1,0:T(8,128)} %coef_ref.3), custom_call_target="tpu_custom_call" | custom-call | tf_op jit(solution)/shard_map/pack/pallas_call | solution.py:59
  8.2 1.5 %collective-permute-start.6 = (f32[2,32,2048]{2,1,0:T(8,128)S(1)}, f32[2,32,2048]{2,1,0:T(8,128)S(1)}, u32[]{:S(2)}, u32[]{:S(2)}) collective-permute-start(f32[2,32,2048]{2,1,0:T(8,128)S(1)} %get-tuple-element.67), channel_id=1, source_target_pairs={{0,2},{1,3},{2,0},{3,1},{4,6},{5,7},{6,4},{7,5},{8,10},{9,11},{10,... | collective-permute-start | bytes 1572872 | tf_op jit(solution)/shard_map/ppermute | solution.py:374
  9.8 2.5 %collective-permute-done.1.diag_ref = f32[8,4224]{1,0:T(8,128)S(1)} collective-permute-done((f32[8,4224]{1,0:T(8,128)}, f32[8,4224]{1,0:T(8,128)S(1)}, u32[]{:S(2)}, u32[]{:S(2)}) %collective-permute-start.1) | collective-permute-done | bytes 135200 | tf_op jit(solution)/shard_map/ppermute | solution.py:374
  12.4 1.6 %collective-permute-start.3 = (f32[8,8448]{1,0:T(8,128)S(1)}, f32[8,8448]{1,0:T(8,128)S(1)}, u32[]{:S(2)}, u32[]{:S(2)}) collective-permute-start(f32[8,8448]{1,0:T(8,128)S(1)} %get-tuple-element.59.refs_1_.refs_4_), channel_id=1, source_target_pairs={{0,4},{1,5},{2,6},{3,7},{4,0},{5,1},{6,2},{7,3},{8,12},{9,13},{10,... | collective-permute-start | bytes 811016 | tf_op jit(solution)/shard_map/ppermute | solution.py:374
  14.6 2.1 %matrices.1 = (bf16[128,256]{1,0:T(8,128)(2,1)S(1)}, bf16[128,256]{1,0:T(8,128)(2,1)S(1)}, bf16[2,512,256]{2,1,0:T(8,128)(2,1)S(1)}, bf16[2,512,256]{2,1,0:T(8,128)(2,1)S(1)}) custom-call(f32[65]{0:T(128)S(1)} %copy-done.5, f32[65]{0:T(128)S(1)} %copy-done.6), custom_call_target="tpu_custom_call" | custom-call | flops 36400000 | bytes 520 | tf_op jit(solution)/shard_map/matrices/pallas_call | solution.py:59
  16.7 4.6 %collective-permute-done.3.refs_0_.refs_4_ = f32[8,8448]{1,0:T(8,128)S(1)} collective-permute-done((f32[8,8448]{1,0:T(8,128)S(1)}, f32[8,8448]{1,0:T(8,128)S(1)}, u32[]{:S(2)}, u32[]{:S(2)}) %collective-permute-start.3) | collective-permute-done | bytes 270368 | tf_op jit(solution)/shard_map/ppermute | solution.py:374
  22.2 1.1 %collective-permute-done.6.sent_ref = f32[2,32,2048]{2,1,0:T(8,128)S(1)} collective-permute-done((f32[2,32,2048]{2,1,0:T(8,128)S(1)}, f32[2,32,2048]{2,1,0:T(8,128)S(1)}, u32[]{:S(2)}, u32[]{:S(2)}) %collective-permute-start.6) | collective-permute-done | bytes 524320 | tf_op jit(solution)/shard_map/ppermute | solution.py:374
  24.0 1.8 %collective-permute-start.9 = (f32[2,32,1024]{2,1,0:T(8,128)S(1)}, f32[2,32,1024]{2,1,0:T(8,128)S(1)}, u32[]{:S(2)}, u32[]{:S(2)}) collective-permute-start(f32[2,32,1024]{2,1,0:T(8,128)S(1)} %pad_maximum_fusion.refs_6_.refs_0_), channel_id=1, source_target_pairs={{0,2},{1,3},{2,0},{3,1},{4,6},{5,7},{6,4},{7,5},{8,10},{9,11},{10,... | collective-permute-start | bytes 786440 | tf_op jit(solution)/shard_map/ppermute | solution.py:374
  25.8 1.6 %collective-permute-start.7 = (f32[32,2048]{1,0:T(8,128)S(1)}, f32[32,2048]{1,0:T(8,128)S(1)}, u32[]{:S(2)}, u32[]{:S(2)}) collective-permute-start(f32[32,2048]{1,0:T(8,128)S(1)} %get-tuple-element.70.refs_1_), channel_id=1, source_target_pairs={{0,4},{1,5},{2,6},{3,7},{4,0},{5,1},{6,2},{7,3},{8,12},{9,13},{10,... | collective-permute-start | bytes 786440 | tf_op jit(solution)/shard_map/ppermute | solution.py:374
  27.3 4.5 %collective-permute-done.9.refs_8_.refs_2_ = f32[2,32,1024]{2,1,0:T(8,128)S(1)} collective-permute-done((f32[2,32,1024]{2,1,0:T(8,128)S(1)}, f32[2,32,1024]{2,1,0:T(8,128)S(1)}, u32[]{:S(2)}, u32[]{:S(2)}) %collective-permute-start.9) | collective-permute-done | bytes 262176 | tf_op jit(solution)/shard_map/ppermute | solution.py:374
  31.8 1.1 %collective-permute-done.7.refs_0_ = f32[32,2048]{1,0:T(8,128)S(1)} collective-permute-done((f32[32,2048]{1,0:T(8,128)S(1)}, f32[32,2048]{1,0:T(8,128)S(1)}, u32[]{:S(2)}, u32[]{:S(2)}) %collective-permute-start.7) | collective-permute-done | bytes 262176 | tf_op jit(solution)/shard_map/ppermute | solution.py:374
  33.4 1.0 %prior.2.prior_ref = f32[64,2048]{1,0:T(8,128)S(1)} custom-call(f32[8,8448]{1,0:T(8,128)S(1)} %collective-permute-done.3.refs_0_.refs_4_, f32[8,8448]{1,0:T(8,128)S(1)} %get-tuple-element.59.refs_1_.refs_4_, f32[8,8448]{1,0:T(8,128)S(1)} %get-tuple-element.61.refs_2_.refs_5_, f32[8,8448]{1,0:T(8,128)S(1)} %collective-permute-done.5.refs_3_.refs_5_, ...), custom_call_target="tpu_custom_call" | custom-call | tf_op jit(solution)/shard_map/prior/pallas_call | solution.py:59
  34.5 2.7 %collective-permute-start.11 = (f32[32,2048]{1,0:T(8,128)S(1)}, f32[32,2048]{1,0:T(8,128)S(1)}, u32[]{:S(2)}, u32[]{:S(2)}) collective-permute-start(f32[32,2048]{1,0:T(8,128)S(1)} %get-tuple-element.75.refs_1_), channel_id=1, source_target_pairs={{0,4},{1,5},{2,6},{3,7},{4,0},{5,1},{6,2},{7,3},{8,12},{9,13},{10,... | collective-permute-start | bytes 786440 | tf_op jit(solution)/shard_map/ppermute | solution.py:374
  37.8 1.3 %collective-permute-start.16 = (f32[32,1024]{1,0:T(8,128)S(1)}, f32[32,1024]{1,0:T(8,128)S(1)}, u32[]{:S(2)}, u32[]{:S(2)}) collective-permute-start(f32[32,1024]{1,0:T(8,128)S(1)} %get-tuple-element.81), channel_id=1, source_target_pairs={{0,3},{1,2},{2,1},{3,0},{4,7},{5,6},{6,5},{7,4},{8,11},{9,10},{10,... | collective-permute-start | bytes 393224 | tf_op jit(solution)/shard_map/ppermute | solution.py:374
  39.4 3.8 %collective-permute-done.11.refs_0_ = f32[32,2048]{1,0:T(8,128)S(1)} collective-permute-done((f32[32,2048]{1,0:T(8,128)S(1)}, f32[32,2048]{1,0:T(8,128)S(1)}, u32[]{:S(2)}, u32[]{:S(2)}) %collective-permute-start.11) | collective-permute-done | bytes 262176 | tf_op jit(solution)/shard_map/ppermute | solution.py:374
  44.6 2.5 %collective-permute-start.14 = (f32[32,1024]{1,0:T(8,128)S(1)}, f32[32,1024]{1,0:T(8,128)S(1)}, u32[]{:S(2)}, u32[]{:S(2)}) collective-permute-start(f32[32,1024]{1,0:T(8,128)S(1)} %get-tuple-element.78.refs_1_), channel_id=1, source_target_pairs={{0,4},{1,5},{2,6},{3,7},{4,0},{5,1},{6,2},{7,3},{8,12},{9,13},{10,... | collective-permute-start | bytes 393224 | tf_op jit(solution)/shard_map/ppermute | solution.py:374
  47.3 2.1 %collective-permute-start.13 = (f32[32,1024]{1,0:T(8,128)S(1)}, f32[32,1024]{1,0:T(8,128)S(1)}, u32[]{:S(2)}, u32[]{:S(2)}) collective-permute-start(f32[32,1024]{1,0:T(8,128)S(1)} %get-tuple-element.77.refs_1_), channel_id=1, source_target_pairs={{0,4},{1,5},{2,6},{3,7},{4,0},{5,1},{6,2},{7,3},{8,12},{9,13},{10,... | collective-permute-start | bytes 393224 | tf_op jit(solution)/shard_map/ppermute | solution.py:374
  49.4 1.0 %prior.3.refs_5_ = f32[64,2048]{1,0:T(8,128)S(1)} custom-call(f32[32,2048]{1,0:T(8,128)S(1)} %collective-permute-done.11.refs_0_, f32[32,2048]{1,0:T(8,128)S(1)} %get-tuple-element.75.refs_1_, f32[32,2048]{1,0:T(8,128)S(1)} %get-tuple-element.76.refs_2_, f32[32,2048]{1,0:T(8,128)S(1)} %collective-permute-done.12.refs_3_, ...), custom_call_target="tpu_custom_call" | custom-call | tf_op jit(solution)/shard_map/prior/pallas_call | solution.py:59
  51.1 1.6 %collective-permute-start.22 = (f32[32,1024]{1,0:T(8,128)S(1)}, f32[32,1024]{1,0:T(8,128)S(1)}, u32[]{:S(2)}, u32[]{:S(2)}) collective-permute-start(f32[32,1024]{1,0:T(8,128)S(1)} %get-tuple-element.95), channel_id=1, source_target_pairs={{0,2},{1,3},{2,0},{3,1},{4,6},{5,7},{6,4},{7,5},{8,10},{9,11},{10,... | collective-permute-start | bytes 393224 | tf_op jit(solution)/shard_map/ppermute | solution.py:374
  53.5 0.9 %collective-permute-start.20 = (f32[32,1024]{1,0:T(8,128)S(1)}, f32[32,1024]{1,0:T(8,128)S(1)}, u32[]{:S(2)}, u32[]{:S(2)}) collective-permute-start(f32[32,1024]{1,0:T(8,128)S(1)} %get-tuple-element.90), channel_id=1, source_target_pairs={{0,3},{1,2},{2,1},{3,0},{4,7},{5,6},{6,5},{7,4},{8,11},{9,10},{10,... | collective-permute-start | bytes 393224 | tf_op jit(solution)/shard_map/ppermute | solution.py:374
  55.2 1.5 %collective-permute-done.22.refs_1_ = f32[32,1024]{1,0:T(8,128)S(1)} collective-permute-done((f32[32,1024]{1,0:T(8,128)S(1)}, f32[32,1024]{1,0:T(8,128)S(1)}, u32[]{:S(2)}, u32[]{:S(2)}) %collective-permute-start.22) | collective-permute-done | bytes 131104 | tf_op jit(solution)/shard_map/ppermute | solution.py:374
  57.5 1.9 %collective-permute-done.20.refs_0_ = f32[32,1024]{1,0:T(8,128)S(1)} collective-permute-done((f32[32,1024]{1,0:T(8,128)S(1)}, f32[32,1024]{1,0:T(8,128)S(1)}, u32[]{:S(2)}, u32[]{:S(2)}) %collective-permute-start.20) | collective-permute-done | bytes 131104 | tf_op jit(solution)/shard_map/ppermute | solution.py:374
  (61 shorter events, 9.9 us)
Async XLA Ops:
  2.4 7.4 %collective-permute-start = (f32[8,4224]{1,0:T(8,128)}, f32[8,4224]{1,0:T(8,128)S(1)}, u32[]{:S(2)}, u32[]{:S(2)}) collective-permute-start(f32[8,4224]{1,0:T(8,128)} %get-tuple-element.54), channel_id=1, source_target_pairs={{0,2},{1,3},{2,0},{3,1},{4,6},{5,7},{6,4},{7,5},{8,10},{9,11},{10,... | collective-permute-start | bytes 405512 | tf_op jit(solution)/shard_map/ppermute | solution.py:374
  5.4 6.9 %collective-permute-start.1 = (f32[8,4224]{1,0:T(8,128)}, f32[8,4224]{1,0:T(8,128)S(1)}, u32[]{:S(2)}, u32[]{:S(2)}) collective-permute-start(f32[8,4224]{1,0:T(8,128)} %get-tuple-element.55), channel_id=1, source_target_pairs={{0,3},{1,2},{2,1},{3,0},{4,7},{5,6},{6,5},{7,4},{8,11},{9,10},{10,... | collective-permute-start | bytes 405512 | tf_op jit(solution)/shard_map/ppermute | solution.py:374
  7.3 5.1 %collective-permute-start.2 = (f32[8,4224]{1,0:T(8,128)}, f32[8,4224]{1,0:T(8,128)S(1)}, u32[]{:S(2)}, u32[]{:S(2)}) collective-permute-start(f32[8,4224]{1,0:T(8,128)} %get-tuple-element.56), channel_id=1, source_target_pairs={{0,1},{1,0},{2,3},{3,2},{4,5},{5,4},{6,7},{7,6},{8,9},{9,8},{10,11... | collective-permute-start | bytes 405512 | tf_op jit(solution)/shard_map/ppermute | solution.py:374
  8.2 15.2 %collective-permute-start.6 = (f32[2,32,2048]{2,1,0:T(8,128)S(1)}, f32[2,32,2048]{2,1,0:T(8,128)S(1)}, u32[]{:S(2)}, u32[]{:S(2)}) collective-permute-start(f32[2,32,2048]{2,1,0:T(8,128)S(1)} %get-tuple-element.67), channel_id=1, source_target_pairs={{0,2},{1,3},{2,0},{3,1},{4,6},{5,7},{6,4},{7,5},{8,10},{9,11},{10,... | collective-permute-start | bytes 1572872 | tf_op jit(solution)/shard_map/ppermute | solution.py:374
  12.4 8.9 %collective-permute-start.3 = (f32[8,8448]{1,0:T(8,128)S(1)}, f32[8,8448]{1,0:T(8,128)S(1)}, u32[]{:S(2)}, u32[]{:S(2)}) collective-permute-start(f32[8,8448]{1,0:T(8,128)S(1)} %get-tuple-element.59.refs_1_.refs_4_), channel_id=1, source_target_pairs={{0,4},{1,5},{2,6},{3,7},{4,0},{5,1},{6,2},{7,3},{8,12},{9,13},{10,... | collective-permute-start | bytes 811016 | tf_op jit(solution)/shard_map/ppermute | solution.py:374
  14.1 7.3 %collective-permute-start.5 = (f32[8,8448]{1,0:T(8,128)S(1)}, f32[8,8448]{1,0:T(8,128)S(1)}, u32[]{:S(2)}, u32[]{:S(2)}) collective-permute-start(f32[8,8448]{1,0:T(8,128)S(1)} %get-tuple-element.61.refs_2_.refs_5_), channel_id=1, source_target_pairs={{0,1},{1,0},{2,3},{3,2},{4,8},{5,9},{6,10},{7,11},{8,4},{9,5},{10,... | collective-permute-start | bytes 811016 | tf_op jit(solution)/shard_map/ppermute | solution.py:374
  14.5 2.3 %collective-permute-start.4 = (f32[2,32,1024]{2,1,0:T(8,128)S(1)}, f32[2,32,1024]{2,1,0:T(8,128)S(1)}, u32[]{:S(2)}, u32[]{:S(2)}) collective-permute-start(f32[2,32,1024]{2,1,0:T(8,128)S(1)} %pad_maximum_fusion.refs_6_.refs_0_), channel_id=1, source_target_pairs={{0,1},{1,0},{2,3},{3,2},{4,5},{5,4},{6,7},{7,6},{8,9},{9,8},{10,11... | collective-permute-start | bytes 786440 | tf_op jit(solution)/shard_map/ppermute | solution.py:374
  24.0 7.9 %collective-permute-start.9 = (f32[2,32,1024]{2,1,0:T(8,128)S(1)}, f32[2,32,1024]{2,1,0:T(8,128)S(1)}, u32[]{:S(2)}, u32[]{:S(2)}) collective-permute-start(f32[2,32,1024]{2,1,0:T(8,128)S(1)} %pad_maximum_fusion.refs_6_.refs_0_), channel_id=1, source_target_pairs={{0,2},{1,3},{2,0},{3,1},{4,6},{5,7},{6,4},{7,5},{8,10},{9,11},{10,... | collective-permute-start | bytes 786440 | tf_op jit(solution)/shard_map/ppermute | solution.py:374
  25.8 7.2 %collective-permute-start.7 = (f32[32,2048]{1,0:T(8,128)S(1)}, f32[32,2048]{1,0:T(8,128)S(1)}, u32[]{:S(2)}, u32[]{:S(2)}) collective-permute-start(f32[32,2048]{1,0:T(8,128)S(1)} %get-tuple-element.70.refs_1_), channel_id=1, source_target_pairs={{0,4},{1,5},{2,6},{3,7},{4,0},{5,1},{6,2},{7,3},{8,12},{9,13},{10,... | collective-permute-start | bytes 786440 | tf_op jit(solution)/shard_map/ppermute | solution.py:374
  27.3 5.6 %collective-permute-start.8 = (f32[32,2048]{1,0:T(8,128)S(1)}, f32[32,2048]{1,0:T(8,128)S(1)}, u32[]{:S(2)}, u32[]{:S(2)}) collective-permute-start(f32[32,2048]{1,0:T(8,128)S(1)} %get-tuple-element.71.refs_2_), channel_id=1, source_target_pairs={{0,1},{1,0},{2,3},{3,2},{4,8},{5,9},{6,10},{7,11},{8,4},{9,5},{10,... | collective-permute-start | bytes 786440 | tf_op jit(solution)/shard_map/ppermute | solution.py:374
  31.8 1.5 %collective-permute-start.10 = (f32[2,32,1024]{2,1,0:T(8,128)S(1)}, f32[2,32,1024]{2,1,0:T(8,128)S(1)}, u32[]{:S(2)}, u32[]{:S(2)}) collective-permute-start(f32[2,32,1024]{2,1,0:T(8,128)S(1)} %collective-permute-done.9.refs_8_.refs_2_), channel_id=1, source_target_pairs={{0,1},{1,0},{2,3},{3,2},{4,5},{5,4},{6,7},{7,6},{8,9},{9,8},{10,11... | collective-permute-start | bytes 786440 | tf_op jit(solution)/shard_map/ppermute | solution.py:374
  34.5 8.6 %collective-permute-start.11 = (f32[32,2048]{1,0:T(8,128)S(1)}, f32[32,2048]{1,0:T(8,128)S(1)}, u32[]{:S(2)}, u32[]{:S(2)}) collective-permute-start(f32[32,2048]{1,0:T(8,128)S(1)} %get-tuple-element.75.refs_1_), channel_id=1, source_target_pairs={{0,4},{1,5},{2,6},{3,7},{4,0},{5,1},{6,2},{7,3},{8,12},{9,13},{10,... | collective-permute-start | bytes 786440 | tf_op jit(solution)/shard_map/ppermute | solution.py:374
  37.2 5.9 %collective-permute-start.12 = (f32[32,2048]{1,0:T(8,128)S(1)}, f32[32,2048]{1,0:T(8,128)S(1)}, u32[]{:S(2)}, u32[]{:S(2)}) collective-permute-start(f32[32,2048]{1,0:T(8,128)S(1)} %get-tuple-element.76.refs_2_), channel_id=1, source_target_pairs={{0,1},{1,0},{2,3},{3,2},{4,8},{5,9},{6,10},{7,11},{8,4},{9,5},{10,... | collective-permute-start | bytes 786440 | tf_op jit(solution)/shard_map/ppermute | solution.py:374
  37.2 9.9 %collective-permute-start.15 = (f32[32,1024]{1,0:T(8,128)S(1)}, f32[32,1024]{1,0:T(8,128)S(1)}, u32[]{:S(2)}, u32[]{:S(2)}) collective-permute-start(f32[32,1024]{1,0:T(8,128)S(1)} %get-tuple-element.80), channel_id=1, source_target_pairs={{0,2},{1,3},{2,0},{3,1},{4,6},{5,7},{6,4},{7,5},{8,10},{9,11},{10,... | collective-permute-start | bytes 393224 | tf_op jit(solution)/shard_map/ppermute | solution.py:374
  37.8 9.3 %collective-permute-start.16 = (f32[32,1024]{1,0:T(8,128)S(1)}, f32[32,1024]{1,0:T(8,128)S(1)}, u32[]{:S(2)}, u32[]{:S(2)}) collective-permute-start(f32[32,1024]{1,0:T(8,128)S(1)} %get-tuple-element.81), channel_id=1, source_target_pairs={{0,3},{1,2},{2,1},{3,0},{4,7},{5,6},{6,5},{7,4},{8,11},{9,10},{10,... | collective-permute-start | bytes 393224 | tf_op jit(solution)/shard_map/ppermute | solution.py:374
  39.1 8.0 %collective-permute-start.17 = (f32[32,1024]{1,0:T(8,128)S(1)}, f32[32,1024]{1,0:T(8,128)S(1)}, u32[]{:S(2)}, u32[]{:S(2)}) collective-permute-start(f32[32,1024]{1,0:T(8,128)S(1)} %get-tuple-element.82), channel_id=1, source_target_pairs={{0,1},{1,0},{2,3},{3,2},{4,5},{5,4},{6,7},{7,6},{8,9},{9,8},{10,11... | collective-permute-start | bytes 393224 | tf_op jit(solution)/shard_map/ppermute | solution.py:374
  44.0 3.1 %copy-start = (f32[4,32,1024]{2,1,0:T(8,128)S(1)}, f32[4,32,1024]{2,1,0:T(8,128)}, u32[]{:S(2)}) copy-start(f32[4,32,1024]{2,1,0:T(8,128)} %refs_4_.1) | copy-start | bytes 1572868
  44.6 6.3 %collective-permute-start.14 = (f32[32,1024]{1,0:T(8,128)S(1)}, f32[32,1024]{1,0:T(8,128)S(1)}, u32[]{:S(2)}, u32[]{:S(2)}) collective-permute-start(f32[32,1024]{1,0:T(8,128)S(1)} %get-tuple-element.78.refs_1_), channel_id=1, source_target_pairs={{0,4},{1,5},{2,6},{3,7},{4,0},{5,1},{6,2},{7,3},{8,12},{9,13},{10,... | collective-permute-start | bytes 393224 | tf_op jit(solution)/shard_map/ppermute | solution.py:374
  47.1 3.8 %collective-permute-start.18 = (f32[32,1024]{1,0:T(8,128)S(1)}, f32[32,1024]{1,0:T(8,128)S(1)}, u32[]{:S(2)}, u32[]{:S(2)}) collective-permute-start(f32[32,1024]{1,0:T(8,128)S(1)} %get-tuple-element.86.refs_2_), channel_id=1, source_target_pairs={{0,1},{1,0},{2,3},{3,2},{4,8},{5,9},{6,10},{7,11},{8,4},{9,5},{10,... | collective-permute-start | bytes 393224 | tf_op jit(solution)/shard_map/ppermute | solution.py:374
  47.3 6.0 %collective-permute-start.13 = (f32[32,1024]{1,0:T(8,128)S(1)}, f32[32,1024]{1,0:T(8,128)S(1)}, u32[]{:S(2)}, u32[]{:S(2)}) collective-permute-start(f32[32,1024]{1,0:T(8,128)S(1)} %get-tuple-element.77.refs_1_), channel_id=1, source_target_pairs={{0,4},{1,5},{2,6},{3,7},{4,0},{5,1},{6,2},{7,3},{8,12},{9,13},{10,... | collective-permute-start | bytes 393224 | tf_op jit(solution)/shard_map/ppermute | solution.py:374
  49.4 3.9 %collective-permute-start.19 = (f32[32,1024]{1,0:T(8,128)S(1)}, f32[32,1024]{1,0:T(8,128)S(1)}, u32[]{:S(2)}, u32[]{:S(2)}) collective-permute-start(f32[32,1024]{1,0:T(8,128)S(1)} %get-tuple-element.89.refs_2_), channel_id=1, source_target_pairs={{0,1},{1,0},{2,3},{3,2},{4,8},{5,9},{6,10},{7,11},{8,4},{9,5},{10,... | collective-permute-start | bytes 393224 | tf_op jit(solution)/shard_map/ppermute | solution.py:374
  51.1 5.5 %collective-permute-start.22 = (f32[32,1024]{1,0:T(8,128)S(1)}, f32[32,1024]{1,0:T(8,128)S(1)}, u32[]{:S(2)}, u32[]{:S(2)}) collective-permute-start(f32[32,1024]{1,0:T(8,128)S(1)} %get-tuple-element.95), channel_id=1, source_target_pairs={{0,2},{1,3},{2,0},{3,1},{4,6},{5,7},{6,4},{7,5},{8,10},{9,11},{10,... | collective-permute-start | bytes 393224 | tf_op jit(solution)/shard_map/ppermute | solution.py:374
  53.5 5.9 %collective-permute-start.20 = (f32[32,1024]{1,0:T(8,128)S(1)}, f32[32,1024]{1,0:T(8,128)S(1)}, u32[]{:S(2)}, u32[]{:S(2)}) collective-permute-start(f32[32,1024]{1,0:T(8,128)S(1)} %get-tuple-element.90), channel_id=1, source_target_pairs={{0,3},{1,2},{2,1},{3,0},{4,7},{5,6},{6,5},{7,4},{8,11},{9,10},{10,... | collective-permute-start | bytes 393224 | tf_op jit(solution)/shard_map/ppermute | solution.py:374
  54.4 5.0 %collective-permute-start.21 = (f32[32,1024]{1,0:T(8,128)S(1)}, f32[32,1024]{1,0:T(8,128)S(1)}, u32[]{:S(2)}, u32[]{:S(2)}) collective-permute-start(f32[32,1024]{1,0:T(8,128)S(1)} %get-tuple-element.91), channel_id=1, source_target_pairs={{0,1},{1,0},{2,3},{3,2},{4,5},{5,4},{6,7},{7,6},{8,9},{9,8},{10,11... | collective-permute-start | bytes 393224 | tf_op jit(solution)/shard_map/ppermute | solution.py:374
  (8 other events, 16.1 us)

commit v6 on v5

--- a/solution.py
+++ b/solution.py
@@ -36,15 +36,15 @@
 
 
 def open_sides(pairs):
-    k, _, _ = place()
+    k, y, _ = place()
     north, south = jnp.where(k == 0, 0.0, 1.0), jnp.where(k == pairs - 1, 0.0, 1.0)
-    flip = lax.rem(k, 2) == 1
+    flip = lax.rem(k + y, 2) == 1
     return jnp.where(flip, north, south), jnp.where(flip, south, north)
 
 
 def lead_trail(own, pair):
     k, y, _ = place()
-    straight = lax.rem(k + y, 2) == 1
+    straight = lax.rem(k, 2) == 1
     return jnp.where(straight, own, pair), jnp.where(straight, pair, own)
 
 
@@ -141,7 +141,7 @@
     k, y, _ = place()
     dims = (2 * rows, 4 * rows)
 
-    flip = lax.rem(k, 2) == 1
+    flip = lax.rem(k + y, 2) == 1
     out = lax.broadcasted_iota(jnp.int32, dims, 0)
     col = lax.broadcasted_iota(jnp.int32, dims, 1)
     target = rows * jnp.where(y == 0, out // rows, 1 - out // rows) + out % rows
@@ -256,7 +256,7 @@
     out_ref, ext, wide, inner = refs[10:]
     k, y, _ = place()
     rows, length = inside[0].shape
-    flip = lax.rem(k, 2) == 1
+    flip = lax.rem(k + y, 2) == 1
     north_open = jnp.where(k == 0, 0.0, 1.0)
     south_open = jnp.where(k == pairs - 1, 0.0, 1.0)
     for block, field in enumerate(inside):
@@ -374,7 +374,7 @@
         return lax.ppermute(array, AXES, moves)
 
     def swap(k, y, c, parity):
-        target = k + 1 if k % 2 == parity else k - 1
+        target = k + 1 if (k + y) % 2 == parity else k - 1
         return (target, y, c) if 0 <= target < pairs else (k, y, 1 - c)
 
     core = lambda array: permute(array, lambda k, y, c: (k, y, 1 - c))

time: 60.5 us -> 60.3 us (level)
  waiting for transfers between devices: 22.2 us -> 20.7 us
  starting transfers between devices: 23 us -> 24.3 us
    ppermute x23, waiting for transfers between devices: 22.2 us -> 20.7 us  [permute(): return lax.ppermute(array, AXES, moves)]
    ppermute x23, starting transfers between devices: 23 us -> 24.3 us  [permute(): return lax.ppermute(array, AXES, moves)]
  transfers between devices with their start and end apart: 23 -> 23, of which waited for: 11 -> 9; matrix products, arithmetic and copies ran while one was open for 0% -> 0% of each run, Pallas kernels for 15% -> 15%
where the time goes in v6:
time: 60.3 us; the launch traced here: 60.1 us
  starting transfers between devices  24.3 us (40%)
  waiting for transfers between devices  20.7 us (34%)
  Pallas kernels  13.5 us (22%)
  between operations  0.89 us (1%)
    ppermute x23, starting transfers between devices, permute(): return lax.ppermute(array, AXES, moves)  24.3 us
    ppermute x23, waiting for transfers between devices, permute(): return lax.ppermute(array, AXES, moves)  20.7 us
    pallas_call x18, Pallas kernels, call(): pl.pallas_call(kernel, out_shape=out_shape, in_specs=specs or [VMEM] * le...  13.5 us
  transfers between devices with their start and end apart: 23, of which 9 were waited for; matrix products, arithmetic and copies ran while one was open for 0% of the time, Pallas kernels for 15%

profile of v6, /device:TPU:0, one launch (start us, length us, event | category | flops | bytes accessed | tf_op | source)
XLA Modules:
  0.0 60.1 jit_solution(14142937630055651707)
XLA Ops:
  0.6 1.8 %pack.2 = (f32[8,4224]{1,0:T(8,128)}, f32[8,4224]{1,0:T(8,128)}) custom-call(f32[4,32,1024]{2,1,0:T(8,128)} %refs_4_.1, s32[32,1024]{1,0:T(8,128)} %refs_5_.1, f32[32,1024]{1,0:T(8,128)} %coef_ref.3), custom_call_target="tpu_custom_call" | custom-call | tf_op jit(solution)/shard_map/pack/pallas_call | solution.py:59
  2.4 3.0 %collective-permute-start = (f32[8,4224]{1,0:T(8,128)}, f32[8,4224]{1,0:T(8,128)S(1)}, u32[]{:S(2)}, u32[]{:S(2)}) collective-permute-start(f32[8,4224]{1,0:T(8,128)} %get-tuple-element.54), channel_id=1, source_target_pairs={{0,2},{1,3},{2,0},{3,1},{4,6},{5,7},{6,4},{7,5},{8,10},{9,11},{10,... | collective-permute-start | bytes 405512 | tf_op jit(solution)/shard_map/ppermute | solution.py:374
  5.4 1.8 %pack.3 = (f32[8,4224]{1,0:T(8,128)}, f32[8,4224]{1,0:T(8,128)}) custom-call(f32[4,32,1024]{2,1,0:T(8,128)} %refs_4_.1, s32[32,1024]{1,0:T(8,128)} %refs_5_.1, f32[32,1024]{1,0:T(8,128)} %coef_ref.3), custom_call_target="tpu_custom_call" | custom-call | tf_op jit(solution)/shard_map/pack/pallas_call | solution.py:59
  8.2 1.5 %collective-permute-start.6 = (f32[2,32,2048]{2,1,0:T(8,128)S(1)}, f32[2,32,2048]{2,1,0:T(8,128)S(1)}, u32[]{:S(2)}, u32[]{:S(2)}) collective-permute-start(f32[2,32,2048]{2,1,0:T(8,128)S(1)} %get-tuple-element.67), channel_id=1, source_target_pairs={{0,2},{1,3},{2,0},{3,1},{4,6},{5,7},{6,4},{7,5},{8,10},{9,11},{10,... | collective-permute-start | bytes 1572872 | tf_op jit(solution)/shard_map/ppermute | solution.py:374
  9.8 2.5 %collective-permute-done.1.diag_ref = f32[8,4224]{1,0:T(8,128)S(1)} collective-permute-done((f32[8,4224]{1,0:T(8,128)}, f32[8,4224]{1,0:T(8,128)S(1)}, u32[]{:S(2)}, u32[]{:S(2)}) %collective-permute-start.1) | collective-permute-done | bytes 135200 | tf_op jit(solution)/shard_map/ppermute | solution.py:374
  12.4 1.6 %collective-permute-start.3 = (f32[8,8448]{1,0:T(8,128)S(1)}, f32[8,8448]{1,0:T(8,128)S(1)}, u32[]{:S(2)}, u32[]{:S(2)}) collective-permute-start(f32[8,8448]{1,0:T(8,128)S(1)} %get-tuple-element.59.refs_1_.refs_4_), channel_id=1, source_target_pairs={{0,4},{1,5},{2,3},{3,2},{4,0},{5,1},{6,10},{7,11},{8,12},{9,13},{1... | collective-permute-start | bytes 811016 | tf_op jit(solution)/shard_map/ppermute | solution.py:374
  14.6 2.1 %matrices.1 = (bf16[128,256]{1,0:T(8,128)(2,1)S(1)}, bf16[128,256]{1,0:T(8,128)(2,1)S(1)}, bf16[2,512,256]{2,1,0:T(8,128)(2,1)S(1)}, bf16[2,512,256]{2,1,0:T(8,128)(2,1)S(1)}) custom-call(f32[65]{0:T(128)S(1)} %copy-done.5, f32[65]{0:T(128)S(1)} %copy-done.6), custom_call_target="tpu_custom_call" | custom-call | flops 36400000 | bytes 520 | tf_op jit(solution)/shard_map/matrices/pallas_call | solution.py:59
  16.7 4.6 %collective-permute-done.3.refs_0_.refs_4_ = f32[8,8448]{1,0:T(8,128)S(1)} collective-permute-done((f32[8,8448]{1,0:T(8,128)S(1)}, f32[8,8448]{1,0:T(8,128)S(1)}, u32[]{:S(2)}, u32[]{:S(2)}) %collective-permute-start.3) | collective-permute-done | bytes 270368 | tf_op jit(solution)/shard_map/ppermute | solution.py:374
  22.2 1.1 %collective-permute-done.6.sent_ref = f32[2,32,2048]{2,1,0:T(8,128)S(1)} collective-permute-done((f32[2,32,2048]{2,1,0:T(8,128)S(1)}, f32[2,32,2048]{2,1,0:T(8,128)S(1)}, u32[]{:S(2)}, u32[]{:S(2)}) %collective-permute-start.6) | collective-permute-done | bytes 524320 | tf_op jit(solution)/shard_map/ppermute | solution.py:374
  24.0 1.8 %collective-permute-start.9 = (f32[2,32,1024]{2,1,0:T(8,128)S(1)}, f32[2,32,1024]{2,1,0:T(8,128)S(1)}, u32[]{:S(2)}, u32[]{:S(2)}) collective-permute-start(f32[2,32,1024]{2,1,0:T(8,128)S(1)} %pad_maximum_fusion.refs_6_.refs_0_), channel_id=1, source_target_pairs={{0,2},{1,3},{2,0},{3,1},{4,6},{5,7},{6,4},{7,5},{8,10},{9,11},{10,... | collective-permute-start | bytes 786440 | tf_op jit(solution)/shard_map/ppermute | solution.py:374
  25.8 1.6 %collective-permute-start.7 = (f32[32,2048]{1,0:T(8,128)S(1)}, f32[32,2048]{1,0:T(8,128)S(1)}, u32[]{:S(2)}, u32[]{:S(2)}) collective-permute-start(f32[32,2048]{1,0:T(8,128)S(1)} %get-tuple-element.70.refs_1_), channel_id=1, source_target_pairs={{0,4},{1,5},{2,3},{3,2},{4,0},{5,1},{6,10},{7,11},{8,12},{9,13},{1... | collective-permute-start | bytes 786440 | tf_op jit(solution)/shard_map/ppermute | solution.py:374
  27.3 4.8 %collective-permute-done.9.refs_8_.refs_2_ = f32[2,32,1024]{2,1,0:T(8,128)S(1)} collective-permute-done((f32[2,32,1024]{2,1,0:T(8,128)S(1)}, f32[2,32,1024]{2,1,0:T(8,128)S(1)}, u32[]{:S(2)}, u32[]{:S(2)}) %collective-permute-start.9) | collective-permute-done | bytes 262176 | tf_op jit(solution)/shard_map/ppermute | solution.py:374
  32.2 1.5 %collective-permute-done.7.refs_0_ = f32[32,2048]{1,0:T(8,128)S(1)} collective-permute-done((f32[32,2048]{1,0:T(8,128)S(1)}, f32[32,2048]{1,0:T(8,128)S(1)}, u32[]{:S(2)}, u32[]{:S(2)}) %collective-permute-start.7) | collective-permute-done | bytes 262176 | tf_op jit(solution)/shard_map/ppermute | solution.py:374
  33.9 1.0 %prior.2.prior_ref = f32[64,2048]{1,0:T(8,128)S(1)} custom-call(f32[8,8448]{1,0:T(8,128)S(1)} %collective-permute-done.3.refs_0_.refs_4_, f32[8,8448]{1,0:T(8,128)S(1)} %get-tuple-element.59.refs_1_.refs_4_, f32[8,8448]{1,0:T(8,128)S(1)} %get-tuple-element.61.refs_2_.refs_5_, f32[8,8448]{1,0:T(8,128)S(1)} %collective-permute-done.5.refs_3_.refs_5_, ...), custom_call_target="tpu_custom_call" | custom-call | tf_op jit(solution)/shard_map/prior/pallas_call | solution.py:59
  35.1 2.1 %collective-permute-start.11 = (f32[32,2048]{1,0:T(8,128)S(1)}, f32[32,2048]{1,0:T(8,128)S(1)}, u32[]{:S(2)}, u32[]{:S(2)}) collective-permute-start(f32[32,2048]{1,0:T(8,128)S(1)} %get-tuple-element.75.refs_1_), channel_id=1, source_target_pairs={{0,4},{1,5},{2,3},{3,2},{4,0},{5,1},{6,10},{7,11},{8,12},{9,13},{1... | collective-permute-start | bytes 786440 | tf_op jit(solution)/shard_map/ppermute | solution.py:374
  37.2 2.3 %collective-permute-start.15 = (f32[32,1024]{1,0:T(8,128)S(1)}, f32[32,1024]{1,0:T(8,128)S(1)}, u32[]{:S(2)}, u32[]{:S(2)}) collective-permute-start(f32[32,1024]{1,0:T(8,128)S(1)} %get-tuple-element.80), channel_id=1, source_target_pairs={{0,2},{1,3},{2,0},{3,1},{4,6},{5,7},{6,4},{7,5},{8,10},{9,11},{10,... | collective-permute-start | bytes 393224 | tf_op jit(solution)/shard_map/ppermute | solution.py:374
  39.7 3.6 %collective-permute-done.11.refs_0_ = f32[32,2048]{1,0:T(8,128)S(1)} collective-permute-done((f32[32,2048]{1,0:T(8,128)S(1)}, f32[32,2048]{1,0:T(8,128)S(1)}, u32[]{:S(2)}, u32[]{:S(2)}) %collective-permute-start.11) | collective-permute-done | bytes 262176 | tf_op jit(solution)/shard_map/ppermute | solution.py:374
  44.7 2.4 %collective-permute-start.14 = (f32[32,1024]{1,0:T(8,128)S(1)}, f32[32,1024]{1,0:T(8,128)S(1)}, u32[]{:S(2)}, u32[]{:S(2)}) collective-permute-start(f32[32,1024]{1,0:T(8,128)S(1)} %get-tuple-element.78.refs_1_), channel_id=1, source_target_pairs={{0,4},{1,5},{2,3},{3,2},{4,0},{5,1},{6,10},{7,11},{8,12},{9,13},{1... | collective-permute-start | bytes 393224 | tf_op jit(solution)/shard_map/ppermute | solution.py:374
  47.3 2.1 %collective-permute-start.13 = (f32[32,1024]{1,0:T(8,128)S(1)}, f32[32,1024]{1,0:T(8,128)S(1)}, u32[]{:S(2)}, u32[]{:S(2)}) collective-permute-start(f32[32,1024]{1,0:T(8,128)S(1)} %get-tuple-element.77.refs_1_), channel_id=1, source_target_pairs={{0,4},{1,5},{2,3},{3,2},{4,0},{5,1},{6,10},{7,11},{8,12},{9,13},{1... | collective-permute-start | bytes 393224 | tf_op jit(solution)/shard_map/ppermute | solution.py:374
  49.4 1.0 %prior.3.refs_5_ = f32[64,2048]{1,0:T(8,128)S(1)} custom-call(f32[32,2048]{1,0:T(8,128)S(1)} %collective-permute-done.11.refs_0_, f32[32,2048]{1,0:T(8,128)S(1)} %get-tuple-element.75.refs_1_, f32[32,2048]{1,0:T(8,128)S(1)} %get-tuple-element.76.refs_2_, f32[32,2048]{1,0:T(8,128)S(1)} %collective-permute-done.12.refs_3_, ...), custom_call_target="tpu_custom_call" | custom-call | tf_op jit(solution)/shard_map/prior/pallas_call | solution.py:59
  51.1 2.1 %collective-permute-start.22 = (f32[32,1024]{1,0:T(8,128)S(1)}, f32[32,1024]{1,0:T(8,128)S(1)}, u32[]{:S(2)}, u32[]{:S(2)}) collective-permute-start(f32[32,1024]{1,0:T(8,128)S(1)} %get-tuple-element.95), channel_id=1, source_target_pairs={{0,2},{1,3},{2,0},{3,1},{4,6},{5,7},{6,4},{7,5},{8,10},{9,11},{10,... | collective-permute-start | bytes 393224 | tf_op jit(solution)/shard_map/ppermute | solution.py:374
  53.5 2.0 %collective-permute-start.20 = (f32[32,1024]{1,0:T(8,128)S(1)}, f32[32,1024]{1,0:T(8,128)S(1)}, u32[]{:S(2)}, u32[]{:S(2)}) collective-permute-start(f32[32,1024]{1,0:T(8,128)S(1)} %get-tuple-element.90), channel_id=1, source_target_pairs={{0,3},{1,2},{2,1},{3,0},{4,7},{5,6},{6,5},{7,4},{8,11},{9,10},{10,... | collective-permute-start | bytes 393224 | tf_op jit(solution)/shard_map/ppermute | solution.py:374
  55.5 0.9 %collective-permute-start.21 = (f32[32,1024]{1,0:T(8,128)S(1)}, f32[32,1024]{1,0:T(8,128)S(1)}, u32[]{:S(2)}, u32[]{:S(2)}) collective-permute-start(f32[32,1024]{1,0:T(8,128)S(1)} %get-tuple-element.91), channel_id=1, source_target_pairs={{0,1},{1,0},{2,3},{3,2},{4,5},{5,4},{6,7},{7,6},{8,9},{9,8},{10,11... | collective-permute-start | bytes 393224 | tf_op jit(solution)/shard_map/ppermute | solution.py:374
  57.5 1.8 %collective-permute-done.20.refs_0_ = f32[32,1024]{1,0:T(8,128)S(1)} collective-permute-done((f32[32,1024]{1,0:T(8,128)S(1)}, f32[32,1024]{1,0:T(8,128)S(1)}, u32[]{:S(2)}, u32[]{:S(2)}) %collective-permute-start.20) | collective-permute-done | bytes 131104 | tf_op jit(solution)/shard_map/ppermute | solution.py:374
  (61 shorter events, 8.1 us)
Async XLA Ops:
  2.4 7.4 %collective-permute-start = (f32[8,4224]{1,0:T(8,128)}, f32[8,4224]{1,0:T(8,128)S(1)}, u32[]{:S(2)}, u32[]{:S(2)}) collective-permute-start(f32[8,4224]{1,0:T(8,128)} %get-tuple-element.54), channel_id=1, source_target_pairs={{0,2},{1,3},{2,0},{3,1},{4,6},{5,7},{6,4},{7,5},{8,10},{9,11},{10,... | collective-permute-start | bytes 405512 | tf_op jit(solution)/shard_map/ppermute | solution.py:374
  5.4 6.9 %collective-permute-start.1 = (f32[8,4224]{1,0:T(8,128)}, f32[8,4224]{1,0:T(8,128)S(1)}, u32[]{:S(2)}, u32[]{:S(2)}) collective-permute-start(f32[8,4224]{1,0:T(8,128)} %get-tuple-element.55), channel_id=1, source_target_pairs={{0,3},{1,2},{2,1},{3,0},{4,7},{5,6},{6,5},{7,4},{8,11},{9,10},{10,... | collective-permute-start | bytes 405512 | tf_op jit(solution)/shard_map/ppermute | solution.py:374
  7.3 5.1 %collective-permute-start.2 = (f32[8,4224]{1,0:T(8,128)}, f32[8,4224]{1,0:T(8,128)S(1)}, u32[]{:S(2)}, u32[]{:S(2)}) collective-permute-start(f32[8,4224]{1,0:T(8,128)} %get-tuple-element.56), channel_id=1, source_target_pairs={{0,1},{1,0},{2,3},{3,2},{4,5},{5,4},{6,7},{7,6},{8,9},{9,8},{10,11... | collective-permute-start | bytes 405512 | tf_op jit(solution)/shard_map/ppermute | solution.py:374
  8.2 15.2 %collective-permute-start.6 = (f32[2,32,2048]{2,1,0:T(8,128)S(1)}, f32[2,32,2048]{2,1,0:T(8,128)S(1)}, u32[]{:S(2)}, u32[]{:S(2)}) collective-permute-start(f32[2,32,2048]{2,1,0:T(8,128)S(1)} %get-tuple-element.67), channel_id=1, source_target_pairs={{0,2},{1,3},{2,0},{3,1},{4,6},{5,7},{6,4},{7,5},{8,10},{9,11},{10,... | collective-permute-start | bytes 1572872 | tf_op jit(solution)/shard_map/ppermute | solution.py:374
  12.4 8.9 %collective-permute-start.3 = (f32[8,8448]{1,0:T(8,128)S(1)}, f32[8,8448]{1,0:T(8,128)S(1)}, u32[]{:S(2)}, u32[]{:S(2)}) collective-permute-start(f32[8,8448]{1,0:T(8,128)S(1)} %get-tuple-element.59.refs_1_.refs_4_), channel_id=1, source_target_pairs={{0,4},{1,5},{2,3},{3,2},{4,0},{5,1},{6,10},{7,11},{8,12},{9,13},{1... | collective-permute-start | bytes 811016 | tf_op jit(solution)/shard_map/ppermute | solution.py:374
  14.1 7.3 %collective-permute-start.5 = (f32[8,8448]{1,0:T(8,128)S(1)}, f32[8,8448]{1,0:T(8,128)S(1)}, u32[]{:S(2)}, u32[]{:S(2)}) collective-permute-start(f32[8,8448]{1,0:T(8,128)S(1)} %get-tuple-element.61.refs_2_.refs_5_), channel_id=1, source_target_pairs={{0,1},{1,0},{2,6},{3,7},{4,8},{5,9},{6,2},{7,3},{8,4},{9,5},{10,14... | collective-permute-start | bytes 811016 | tf_op jit(solution)/shard_map/ppermute | solution.py:374
  14.5 2.3 %collective-permute-start.4 = (f32[2,32,1024]{2,1,0:T(8,128)S(1)}, f32[2,32,1024]{2,1,0:T(8,128)S(1)}, u32[]{:S(2)}, u32[]{:S(2)}) collective-permute-start(f32[2,32,1024]{2,1,0:T(8,128)S(1)} %pad_maximum_fusion.refs_6_.refs_0_), channel_id=1, source_target_pairs={{0,1},{1,0},{2,3},{3,2},{4,5},{5,4},{6,7},{7,6},{8,9},{9,8},{10,11... | collective-permute-start | bytes 786440 | tf_op jit(solution)/shard_map/ppermute | solution.py:374
  24.0 8.2 %collective-permute-start.9 = (f32[2,32,1024]{2,1,0:T(8,128)S(1)}, f32[2,32,1024]{2,1,0:T(8,128)S(1)}, u32[]{:S(2)}, u32[]{:S(2)}) collective-permute-start(f32[2,32,1024]{2,1,0:T(8,128)S(1)} %pad_maximum_fusion.refs_6_.refs_0_), channel_id=1, source_target_pairs={{0,2},{1,3},{2,0},{3,1},{4,6},{5,7},{6,4},{7,5},{8,10},{9,11},{10,... | collective-permute-start | bytes 786440 | tf_op jit(solution)/shard_map/ppermute | solution.py:374
  25.8 7.8 %collective-permute-start.7 = (f32[32,2048]{1,0:T(8,128)S(1)}, f32[32,2048]{1,0:T(8,128)S(1)}, u32[]{:S(2)}, u32[]{:S(2)}) collective-permute-start(f32[32,2048]{1,0:T(8,128)S(1)} %get-tuple-element.70.refs_1_), channel_id=1, source_target_pairs={{0,4},{1,5},{2,3},{3,2},{4,0},{5,1},{6,10},{7,11},{8,12},{9,13},{1... | collective-permute-start | bytes 786440 | tf_op jit(solution)/shard_map/ppermute | solution.py:374
  27.3 6.3 %collective-permute-start.8 = (f32[32,2048]{1,0:T(8,128)S(1)}, f32[32,2048]{1,0:T(8,128)S(1)}, u32[]{:S(2)}, u32[]{:S(2)}) collective-permute-start(f32[32,2048]{1,0:T(8,128)S(1)} %get-tuple-element.71.refs_2_), channel_id=1, source_target_pairs={{0,1},{1,0},{2,6},{3,7},{4,8},{5,9},{6,2},{7,3},{8,4},{9,5},{10,14... | collective-permute-start | bytes 786440 | tf_op jit(solution)/shard_map/ppermute | solution.py:374
  32.2 1.8 %collective-permute-start.10 = (f32[2,32,1024]{2,1,0:T(8,128)S(1)}, f32[2,32,1024]{2,1,0:T(8,128)S(1)}, u32[]{:S(2)}, u32[]{:S(2)}) collective-permute-start(f32[2,32,1024]{2,1,0:T(8,128)S(1)} %collective-permute-done.9.refs_8_.refs_2_), channel_id=1, source_target_pairs={{0,1},{1,0},{2,3},{3,2},{4,5},{5,4},{6,7},{7,6},{8,9},{9,8},{10,11... | collective-permute-start | bytes 786440 | tf_op jit(solution)/shard_map/ppermute | solution.py:374
  35.1 8.2 %collective-permute-start.11 = (f32[32,2048]{1,0:T(8,128)S(1)}, f32[32,2048]{1,0:T(8,128)S(1)}, u32[]{:S(2)}, u32[]{:S(2)}) collective-permute-start(f32[32,2048]{1,0:T(8,128)S(1)} %get-tuple-element.75.refs_1_), channel_id=1, source_target_pairs={{0,4},{1,5},{2,3},{3,2},{4,0},{5,1},{6,10},{7,11},{8,12},{9,13},{1... | collective-permute-start | bytes 786440 | tf_op jit(solution)/shard_map/ppermute | solution.py:374
  37.2 6.0 %collective-permute-start.12 = (f32[32,2048]{1,0:T(8,128)S(1)}, f32[32,2048]{1,0:T(8,128)S(1)}, u32[]{:S(2)}, u32[]{:S(2)}) collective-permute-start(f32[32,2048]{1,0:T(8,128)S(1)} %get-tuple-element.76.refs_2_), channel_id=1, source_target_pairs={{0,1},{1,0},{2,6},{3,7},{4,8},{5,9},{6,2},{7,3},{8,4},{9,5},{10,14... | collective-permute-start | bytes 786440 | tf_op jit(solution)/shard_map/ppermute | solution.py:374
  37.2 9.8 %collective-permute-start.15 = (f32[32,1024]{1,0:T(8,128)S(1)}, f32[32,1024]{1,0:T(8,128)S(1)}, u32[]{:S(2)}, u32[]{:S(2)}) collective-permute-start(f32[32,1024]{1,0:T(8,128)S(1)} %get-tuple-element.80), channel_id=1, source_target_pairs={{0,2},{1,3},{2,0},{3,1},{4,6},{5,7},{6,4},{7,5},{8,10},{9,11},{10,... | collective-permute-start | bytes 393224 | tf_op jit(solution)/shard_map/ppermute | solution.py:374
  39.5 7.5 %collective-permute-start.16 = (f32[32,1024]{1,0:T(8,128)S(1)}, f32[32,1024]{1,0:T(8,128)S(1)}, u32[]{:S(2)}, u32[]{:S(2)}) collective-permute-start(f32[32,1024]{1,0:T(8,128)S(1)} %get-tuple-element.81), channel_id=1, source_target_pairs={{0,3},{1,2},{2,1},{3,0},{4,7},{5,6},{6,5},{7,4},{8,11},{9,10},{10,... | collective-permute-start | bytes 393224 | tf_op jit(solution)/shard_map/ppermute | solution.py:374
  39.5 7.5 %collective-permute-start.17 = (f32[32,1024]{1,0:T(8,128)S(1)}, f32[32,1024]{1,0:T(8,128)S(1)}, u32[]{:S(2)}, u32[]{:S(2)}) collective-permute-start(f32[32,1024]{1,0:T(8,128)S(1)} %get-tuple-element.82), channel_id=1, source_target_pairs={{0,1},{1,0},{2,3},{3,2},{4,5},{5,4},{6,7},{7,6},{8,9},{9,8},{10,11... | collective-permute-start | bytes 393224 | tf_op jit(solution)/shard_map/ppermute | solution.py:374
  44.1 3.0 %copy-start = (f32[4,32,1024]{2,1,0:T(8,128)S(1)}, f32[4,32,1024]{2,1,0:T(8,128)}, u32[]{:S(2)}) copy-start(f32[4,32,1024]{2,1,0:T(8,128)} %refs_4_.1) | copy-start | bytes 1572868
  44.7 6.2 %collective-permute-start.14 = (f32[32,1024]{1,0:T(8,128)S(1)}, f32[32,1024]{1,0:T(8,128)S(1)}, u32[]{:S(2)}, u32[]{:S(2)}) collective-permute-start(f32[32,1024]{1,0:T(8,128)S(1)} %get-tuple-element.78.refs_1_), channel_id=1, source_target_pairs={{0,4},{1,5},{2,3},{3,2},{4,0},{5,1},{6,10},{7,11},{8,12},{9,13},{1... | collective-permute-start | bytes 393224 | tf_op jit(solution)/shard_map/ppermute | solution.py:374
  47.1 3.8 %collective-permute-start.18 = (f32[32,1024]{1,0:T(8,128)S(1)}, f32[32,1024]{1,0:T(8,128)S(1)}, u32[]{:S(2)}, u32[]{:S(2)}) collective-permute-start(f32[32,1024]{1,0:T(8,128)S(1)} %get-tuple-element.86.refs_2_), channel_id=1, source_target_pairs={{0,1},{1,0},{2,6},{3,7},{4,8},{5,9},{6,2},{7,3},{8,4},{9,5},{10,14... | collective-permute-start | bytes 393224 | tf_op jit(solution)/shard_map/ppermute | solution.py:374
  47.3 6.0 %collective-permute-start.13 = (f32[32,1024]{1,0:T(8,128)S(1)}, f32[32,1024]{1,0:T(8,128)S(1)}, u32[]{:S(2)}, u32[]{:S(2)}) collective-permute-start(f32[32,1024]{1,0:T(8,128)S(1)} %get-tuple-element.77.refs_1_), channel_id=1, source_target_pairs={{0,4},{1,5},{2,3},{3,2},{4,0},{5,1},{6,10},{7,11},{8,12},{9,13},{1... | collective-permute-start | bytes 393224 | tf_op jit(solution)/shard_map/ppermute | solution.py:374
  49.4 3.9 %collective-permute-start.19 = (f32[32,1024]{1,0:T(8,128)S(1)}, f32[32,1024]{1,0:T(8,128)S(1)}, u32[]{:S(2)}, u32[]{:S(2)}) collective-permute-start(f32[32,1024]{1,0:T(8,128)S(1)} %get-tuple-element.89.refs_2_), channel_id=1, source_target_pairs={{0,1},{1,0},{2,6},{3,7},{4,8},{5,9},{6,2},{7,3},{8,4},{9,5},{10,14... | collective-permute-start | bytes 393224 | tf_op jit(solution)/shard_map/ppermute | solution.py:374
  51.1 5.5 %collective-permute-start.22 = (f32[32,1024]{1,0:T(8,128)S(1)}, f32[32,1024]{1,0:T(8,128)S(1)}, u32[]{:S(2)}, u32[]{:S(2)}) collective-permute-start(f32[32,1024]{1,0:T(8,128)S(1)} %get-tuple-element.95), channel_id=1, source_target_pairs={{0,2},{1,3},{2,0},{3,1},{4,6},{5,7},{6,4},{7,5},{8,10},{9,11},{10,... | collective-permute-start | bytes 393224 | tf_op jit(solution)/shard_map/ppermute | solution.py:374
  53.5 5.8 %collective-permute-start.20 = (f32[32,1024]{1,0:T(8,128)S(1)}, f32[32,1024]{1,0:T(8,128)S(1)}, u32[]{:S(2)}, u32[]{:S(2)}) collective-permute-start(f32[32,1024]{1,0:T(8,128)S(1)} %get-tuple-element.90), channel_id=1, source_target_pairs={{0,3},{1,2},{2,1},{3,0},{4,7},{5,6},{6,5},{7,4},{8,11},{9,10},{10,... | collective-permute-start | bytes 393224 | tf_op jit(solution)/shard_map/ppermute | solution.py:374
  55.5 3.7 %collective-permute-start.21 = (f32[32,1024]{1,0:T(8,128)S(1)}, f32[32,1024]{1,0:T(8,128)S(1)}, u32[]{:S(2)}, u32[]{:S(2)}) collective-permute-start(f32[32,1024]{1,0:T(8,128)S(1)} %get-tuple-element.91), channel_id=1, source_target_pairs={{0,1},{1,0},{2,3},{3,2},{4,5},{5,4},{6,7},{7,6},{8,9},{9,8},{10,11... | collective-permute-start | bytes 393224 | tf_op jit(solution)/shard_map/ppermute | solution.py:374
  (8 other events, 16.1 us)

commit v7 on v6

--- a/solution.py
+++ b/solution.py
@@ -502,7 +502,6 @@
         flops=LEFT_COST,
         name="update",
     )
-    moved[2], left_own = lax.optimization_barrier((moved[2], left_own))
     right_own, right_pair = call(
         functools.partial(last_kernel, 1),
         [piece] * 2,

time: 60.3 us -> 60.3 us (level)
  no operation moved by 1% of the time
where the time goes in v7:
time: 60.3 us; the launch traced here: 60.1 us
  starting transfers between devices  24.3 us (40%)
  waiting for transfers between devices  20.7 us (34%)
  Pallas kernels  13.5 us (22%)
  between operations  0.89 us (1%)
    ppermute x23, starting transfers between devices, permute(): return lax.ppermute(array, AXES, moves)  24.3 us
    ppermute x23, waiting for transfers between devices, permute(): return lax.ppermute(array, AXES, moves)  20.7 us
    pallas_call x18, Pallas kernels, call(): pl.pallas_call(kernel, out_shape=out_shape, in_specs=specs or [VMEM] * le...  13.5 us
  transfers between devices with their start and end apart: 23, of which 9 were waited for; matrix products, arithmetic and copies ran while one was open for 0% of the time, Pallas kernels for 15%

profile of v7, /device:TPU:0, one launch (start us, length us, event | category | flops | bytes accessed | tf_op | source)
XLA Modules:
  0.0 60.1 jit_solution(4818871472298369842)
XLA Ops:
  0.6 1.8 %pack.2 = (f32[8,4224]{1,0:T(8,128)}, f32[8,4224]{1,0:T(8,128)}) custom-call(f32[4,32,1024]{2,1,0:T(8,128)} %refs_4_.1, s32[32,1024]{1,0:T(8,128)} %refs_5_.1, f32[32,1024]{1,0:T(8,128)} %coef_ref.3), custom_call_target="tpu_custom_call" | custom-call | tf_op jit(solution)/shard_map/pack/pallas_call | solution.py:59
  2.4 3.0 %collective-permute-start = (f32[8,4224]{1,0:T(8,128)}, f32[8,4224]{1,0:T(8,128)S(1)}, u32[]{:S(2)}, u32[]{:S(2)}) collective-permute-start(f32[8,4224]{1,0:T(8,128)} %get-tuple-element.52), channel_id=1, source_target_pairs={{0,2},{1,3},{2,0},{3,1},{4,6},{5,7},{6,4},{7,5},{8,10},{9,11},{10,... | collective-permute-start | bytes 405512 | tf_op jit(solution)/shard_map/ppermute | solution.py:374
  5.4 1.8 %pack.3 = (f32[8,4224]{1,0:T(8,128)}, f32[8,4224]{1,0:T(8,128)}) custom-call(f32[4,32,1024]{2,1,0:T(8,128)} %refs_4_.1, s32[32,1024]{1,0:T(8,128)} %refs_5_.1, f32[32,1024]{1,0:T(8,128)} %coef_ref.3), custom_call_target="tpu_custom_call" | custom-call | tf_op jit(solution)/shard_map/pack/pallas_call | solution.py:59
  8.2 1.5 %collective-permute-start.6 = (f32[2,32,2048]{2,1,0:T(8,128)S(1)}, f32[2,32,2048]{2,1,0:T(8,128)S(1)}, u32[]{:S(2)}, u32[]{:S(2)}) collective-permute-start(f32[2,32,2048]{2,1,0:T(8,128)S(1)} %get-tuple-element.65), channel_id=1, source_target_pairs={{0,2},{1,3},{2,0},{3,1},{4,6},{5,7},{6,4},{7,5},{8,10},{9,11},{10,... | collective-permute-start | bytes 1572872 | tf_op jit(solution)/shard_map/ppermute | solution.py:374
  9.8 2.5 %collective-permute-done.1.diag_ref = f32[8,4224]{1,0:T(8,128)S(1)} collective-permute-done((f32[8,4224]{1,0:T(8,128)}, f32[8,4224]{1,0:T(8,128)S(1)}, u32[]{:S(2)}, u32[]{:S(2)}) %collective-permute-start.1) | collective-permute-done | bytes 135200 | tf_op jit(solution)/shard_map/ppermute | solution.py:374
  12.4 1.6 %collective-permute-start.3 = (f32[8,8448]{1,0:T(8,128)S(1)}, f32[8,8448]{1,0:T(8,128)S(1)}, u32[]{:S(2)}, u32[]{:S(2)}) collective-permute-start(f32[8,8448]{1,0:T(8,128)S(1)} %get-tuple-element.57.refs_1_.refs_4_), channel_id=1, source_target_pairs={{0,4},{1,5},{2,3},{3,2},{4,0},{5,1},{6,10},{7,11},{8,12},{9,13},{1... | collective-permute-start | bytes 811016 | tf_op jit(solution)/shard_map/ppermute | solution.py:374
  14.6 2.1 %matrices.1 = (bf16[128,256]{1,0:T(8,128)(2,1)S(1)}, bf16[128,256]{1,0:T(8,128)(2,1)S(1)}, bf16[2,512,256]{2,1,0:T(8,128)(2,1)S(1)}, bf16[2,512,256]{2,1,0:T(8,128)(2,1)S(1)}) custom-call(f32[65]{0:T(128)S(1)} %copy-done.5, f32[65]{0:T(128)S(1)} %copy-done.6), custom_call_target="tpu_custom_call" | custom-call | flops 36400000 | bytes 520 | tf_op jit(solution)/shard_map/matrices/pallas_call | solution.py:59
  16.7 4.6 %collective-permute-done.3.refs_0_.refs_4_ = f32[8,8448]{1,0:T(8,128)S(1)} collective-permute-done((f32[8,8448]{1,0:T(8,128)S(1)}, f32[8,8448]{1,0:T(8,128)S(1)}, u32[]{:S(2)}, u32[]{:S(2)}) %collective-permute-start.3) | collective-permute-done | bytes 270368 | tf_op jit(solution)/shard_map/ppermute | solution.py:374
  22.2 1.1 %collective-permute-done.6.sent_ref = f32[2,32,2048]{2,1,0:T(8,128)S(1)} collective-permute-done((f32[2,32,2048]{2,1,0:T(8,128)S(1)}, f32[2,32,2048]{2,1,0:T(8,128)S(1)}, u32[]{:S(2)}, u32[]{:S(2)}) %collective-permute-start.6) | collective-permute-done | bytes 524320 | tf_op jit(solution)/shard_map/ppermute | solution.py:374
  24.0 1.8 %collective-permute-start.9 = (f32[2,32,1024]{2,1,0:T(8,128)S(1)}, f32[2,32,1024]{2,1,0:T(8,128)S(1)}, u32[]{:S(2)}, u32[]{:S(2)}) collective-permute-start(f32[2,32,1024]{2,1,0:T(8,128)S(1)} %pad_maximum_fusion.refs_6_.refs_0_), channel_id=1, source_target_pairs={{0,2},{1,3},{2,0},{3,1},{4,6},{5,7},{6,4},{7,5},{8,10},{9,11},{10,... | collective-permute-start | bytes 786440 | tf_op jit(solution)/shard_map/ppermute | solution.py:374
  25.8 1.6 %collective-permute-start.7 = (f32[32,2048]{1,0:T(8,128)S(1)}, f32[32,2048]{1,0:T(8,128)S(1)}, u32[]{:S(2)}, u32[]{:S(2)}) collective-permute-start(f32[32,2048]{1,0:T(8,128)S(1)} %get-tuple-element.68.refs_1_), channel_id=1, source_target_pairs={{0,4},{1,5},{2,3},{3,2},{4,0},{5,1},{6,10},{7,11},{8,12},{9,13},{1... | collective-permute-start | bytes 786440 | tf_op jit(solution)/shard_map/ppermute | solution.py:374
  27.3 4.8 %collective-permute-done.9.refs_8_.refs_2_ = f32[2,32,1024]{2,1,0:T(8,128)S(1)} collective-permute-done((f32[2,32,1024]{2,1,0:T(8,128)S(1)}, f32[2,32,1024]{2,1,0:T(8,128)S(1)}, u32[]{:S(2)}, u32[]{:S(2)}) %collective-permute-start.9) | collective-permute-done | bytes 262176 | tf_op jit(solution)/shard_map/ppermute | solution.py:374
  32.2 1.5 %collective-permute-done.7.refs_0_ = f32[32,2048]{1,0:T(8,128)S(1)} collective-permute-done((f32[32,2048]{1,0:T(8,128)S(1)}, f32[32,2048]{1,0:T(8,128)S(1)}, u32[]{:S(2)}, u32[]{:S(2)}) %collective-permute-start.7) | collective-permute-done | bytes 262176 | tf_op jit(solution)/shard_map/ppermute | solution.py:374
  33.9 1.0 %prior.2.prior_ref = f32[64,2048]{1,0:T(8,128)S(1)} custom-call(f32[8,8448]{1,0:T(8,128)S(1)} %collective-permute-done.3.refs_0_.refs_4_, f32[8,8448]{1,0:T(8,128)S(1)} %get-tuple-element.57.refs_1_.refs_4_, f32[8,8448]{1,0:T(8,128)S(1)} %get-tuple-element.59.refs_2_.refs_5_, f32[8,8448]{1,0:T(8,128)S(1)} %collective-permute-done.5.refs_3_.refs_5_, ...), custom_call_target="tpu_custom_call" | custom-call | tf_op jit(solution)/shard_map/prior/pallas_call | solution.py:59
  35.1 2.1 %collective-permute-start.11 = (f32[32,2048]{1,0:T(8,128)S(1)}, f32[32,2048]{1,0:T(8,128)S(1)}, u32[]{:S(2)}, u32[]{:S(2)}) collective-permute-start(f32[32,2048]{1,0:T(8,128)S(1)} %get-tuple-element.73.refs_1_), channel_id=1, source_target_pairs={{0,4},{1,5},{2,3},{3,2},{4,0},{5,1},{6,10},{7,11},{8,12},{9,13},{1... | collective-permute-start | bytes 786440 | tf_op jit(solution)/shard_map/ppermute | solution.py:374
  37.2 2.3 %collective-permute-start.18 = (f32[32,1024]{1,0:T(8,128)S(1)}, f32[32,1024]{1,0:T(8,128)S(1)}, u32[]{:S(2)}, u32[]{:S(2)}) collective-permute-start(f32[32,1024]{1,0:T(8,128)S(1)} %get-tuple-element.81), channel_id=1, source_target_pairs={{0,2},{1,3},{2,0},{3,1},{4,6},{5,7},{6,4},{7,5},{8,10},{9,11},{10,... | collective-permute-start | bytes 393224 | tf_op jit(solution)/shard_map/ppermute | solution.py:374
  39.7 3.6 %collective-permute-done.11.refs_0_ = f32[32,2048]{1,0:T(8,128)S(1)} collective-permute-done((f32[32,2048]{1,0:T(8,128)S(1)}, f32[32,2048]{1,0:T(8,128)S(1)}, u32[]{:S(2)}, u32[]{:S(2)}) %collective-permute-start.11) | collective-permute-done | bytes 262176 | tf_op jit(solution)/shard_map/ppermute | solution.py:374
  44.7 2.4 %collective-permute-start.17 = (f32[32,1024]{1,0:T(8,128)S(1)}, f32[32,1024]{1,0:T(8,128)S(1)}, u32[]{:S(2)}, u32[]{:S(2)}) collective-permute-start(f32[32,1024]{1,0:T(8,128)S(1)} %get-tuple-element.79.refs_1_), channel_id=1, source_target_pairs={{0,4},{1,5},{2,3},{3,2},{4,0},{5,1},{6,10},{7,11},{8,12},{9,13},{1... | collective-permute-start | bytes 393224 | tf_op jit(solution)/shard_map/ppermute | solution.py:374
  47.3 2.1 %collective-permute-start.13 = (f32[32,1024]{1,0:T(8,128)S(1)}, f32[32,1024]{1,0:T(8,128)S(1)}, u32[]{:S(2)}, u32[]{:S(2)}) collective-permute-start(f32[32,1024]{1,0:T(8,128)S(1)} %get-tuple-element.75.refs_1_), channel_id=1, source_target_pairs={{0,4},{1,5},{2,3},{3,2},{4,0},{5,1},{6,10},{7,11},{8,12},{9,13},{1... | collective-permute-start | bytes 393224 | tf_op jit(solution)/shard_map/ppermute | solution.py:374
  49.4 1.0 %prior.3.refs_5_ = f32[64,2048]{1,0:T(8,128)S(1)} custom-call(f32[32,2048]{1,0:T(8,128)S(1)} %collective-permute-done.11.refs_0_, f32[32,2048]{1,0:T(8,128)S(1)} %get-tuple-element.73.refs_1_, f32[32,2048]{1,0:T(8,128)S(1)} %get-tuple-element.74.refs_2_, f32[32,2048]{1,0:T(8,128)S(1)} %collective-permute-done.12.refs_3_, ...), custom_call_target="tpu_custom_call" | custom-call | tf_op jit(solution)/shard_map/prior/pallas_call | solution.py:59
  51.1 2.1 %collective-permute-start.22 = (f32[32,1024]{1,0:T(8,128)S(1)}, f32[32,1024]{1,0:T(8,128)S(1)}, u32[]{:S(2)}, u32[]{:S(2)}) collective-permute-start(f32[32,1024]{1,0:T(8,128)S(1)} %get-tuple-element.91), channel_id=1, source_target_pairs={{0,2},{1,3},{2,0},{3,1},{4,6},{5,7},{6,4},{7,5},{8,10},{9,11},{10,... | collective-permute-start | bytes 393224 | tf_op jit(solution)/shard_map/ppermute | solution.py:374
  53.5 2.0 %collective-permute-start.15 = (f32[32,1024]{1,0:T(8,128)S(1)}, f32[32,1024]{1,0:T(8,128)S(1)}, u32[]{:S(2)}, u32[]{:S(2)}) collective-permute-start(f32[32,1024]{1,0:T(8,128)S(1)} %get-tuple-element.77), channel_id=1, source_target_pairs={{0,3},{1,2},{2,1},{3,0},{4,7},{5,6},{6,5},{7,4},{8,11},{9,10},{10,... | collective-permute-start | bytes 393224 | tf_op jit(solution)/shard_map/ppermute | solution.py:374
  55.5 0.9 %collective-permute-start.16 = (f32[32,1024]{1,0:T(8,128)S(1)}, f32[32,1024]{1,0:T(8,128)S(1)}, u32[]{:S(2)}, u32[]{:S(2)}) collective-permute-start(f32[32,1024]{1,0:T(8,128)S(1)} %get-tuple-element.78), channel_id=1, source_target_pairs={{0,1},{1,0},{2,3},{3,2},{4,5},{5,4},{6,7},{7,6},{8,9},{9,8},{10,11... | collective-permute-start | bytes 393224 | tf_op jit(solution)/shard_map/ppermute | solution.py:374
  57.5 1.8 %collective-permute-done.15.refs_0_ = f32[32,1024]{1,0:T(8,128)S(1)} collective-permute-done((f32[32,1024]{1,0:T(8,128)S(1)}, f32[32,1024]{1,0:T(8,128)S(1)}, u32[]{:S(2)}, u32[]{:S(2)}) %collective-permute-start.15) | collective-permute-done | bytes 131104 | tf_op jit(solution)/shard_map/ppermute | solution.py:374
  (61 shorter events, 8.1 us)
Async XLA Ops:
  2.4 7.4 %collective-permute-start = (f32[8,4224]{1,0:T(8,128)}, f32[8,4224]{1,0:T(8,128)S(1)}, u32[]{:S(2)}, u32[]{:S(2)}) collective-permute-start(f32[8,4224]{1,0:T(8,128)} %get-tuple-element.52), channel_id=1, source_target_pairs={{0,2},{1,3},{2,0},{3,1},{4,6},{5,7},{6,4},{7,5},{8,10},{9,11},{10,... | collective-permute-start | bytes 405512 | tf_op jit(solution)/shard_map/ppermute | solution.py:374
  5.4 6.9 %collective-permute-start.1 = (f32[8,4224]{1,0:T(8,128)}, f32[8,4224]{1,0:T(8,128)S(1)}, u32[]{:S(2)}, u32[]{:S(2)}) collective-permute-start(f32[8,4224]{1,0:T(8,128)} %get-tuple-element.53), channel_id=1, source_target_pairs={{0,3},{1,2},{2,1},{3,0},{4,7},{5,6},{6,5},{7,4},{8,11},{9,10},{10,... | collective-permute-start | bytes 405512 | tf_op jit(solution)/shard_map/ppermute | solution.py:374
  7.3 5.1 %collective-permute-start.2 = (f32[8,4224]{1,0:T(8,128)}, f32[8,4224]{1,0:T(8,128)S(1)}, u32[]{:S(2)}, u32[]{:S(2)}) collective-permute-start(f32[8,4224]{1,0:T(8,128)} %get-tuple-element.54), channel_id=1, source_target_pairs={{0,1},{1,0},{2,3},{3,2},{4,5},{5,4},{6,7},{7,6},{8,9},{9,8},{10,11... | collective-permute-start | bytes 405512 | tf_op jit(solution)/shard_map/ppermute | solution.py:374
  8.2 15.2 %collective-permute-start.6 = (f32[2,32,2048]{2,1,0:T(8,128)S(1)}, f32[2,32,2048]{2,1,0:T(8,128)S(1)}, u32[]{:S(2)}, u32[]{:S(2)}) collective-permute-start(f32[2,32,2048]{2,1,0:T(8,128)S(1)} %get-tuple-element.65), channel_id=1, source_target_pairs={{0,2},{1,3},{2,0},{3,1},{4,6},{5,7},{6,4},{7,5},{8,10},{9,11},{10,... | collective-permute-start | bytes 1572872 | tf_op jit(solution)/shard_map/ppermute | solution.py:374
  12.4 8.9 %collective-permute-start.3 = (f32[8,8448]{1,0:T(8,128)S(1)}, f32[8,8448]{1,0:T(8,128)S(1)}, u32[]{:S(2)}, u32[]{:S(2)}) collective-permute-start(f32[8,8448]{1,0:T(8,128)S(1)} %get-tuple-element.57.refs_1_.refs_4_), channel_id=1, source_target_pairs={{0,4},{1,5},{2,3},{3,2},{4,0},{5,1},{6,10},{7,11},{8,12},{9,13},{1... | collective-permute-start | bytes 811016 | tf_op jit(solution)/shard_map/ppermute | solution.py:374
  14.1 7.3 %collective-permute-start.5 = (f32[8,8448]{1,0:T(8,128)S(1)}, f32[8,8448]{1,0:T(8,128)S(1)}, u32[]{:S(2)}, u32[]{:S(2)}) collective-permute-start(f32[8,8448]{1,0:T(8,128)S(1)} %get-tuple-element.59.refs_2_.refs_5_), channel_id=1, source_target_pairs={{0,1},{1,0},{2,6},{3,7},{4,8},{5,9},{6,2},{7,3},{8,4},{9,5},{10,14... | collective-permute-start | bytes 811016 | tf_op jit(solution)/shard_map/ppermute | solution.py:374
  14.5 2.3 %collective-permute-start.4 = (f32[2,32,1024]{2,1,0:T(8,128)S(1)}, f32[2,32,1024]{2,1,0:T(8,128)S(1)}, u32[]{:S(2)}, u32[]{:S(2)}) collective-permute-start(f32[2,32,1024]{2,1,0:T(8,128)S(1)} %pad_maximum_fusion.refs_6_.refs_0_), channel_id=1, source_target_pairs={{0,1},{1,0},{2,3},{3,2},{4,5},{5,4},{6,7},{7,6},{8,9},{9,8},{10,11... | collective-permute-start | bytes 786440 | tf_op jit(solution)/shard_map/ppermute | solution.py:374
  24.0 8.2 %collective-permute-start.9 = (f32[2,32,1024]{2,1,0:T(8,128)S(1)}, f32[2,32,1024]{2,1,0:T(8,128)S(1)}, u32[]{:S(2)}, u32[]{:S(2)}) collective-permute-start(f32[2,32,1024]{2,1,0:T(8,128)S(1)} %pad_maximum_fusion.refs_6_.refs_0_), channel_id=1, source_target_pairs={{0,2},{1,3},{2,0},{3,1},{4,6},{5,7},{6,4},{7,5},{8,10},{9,11},{10,... | collective-permute-start | bytes 786440 | tf_op jit(solution)/shard_map/ppermute | solution.py:374
  25.8 7.8 %collective-permute-start.7 = (f32[32,2048]{1,0:T(8,128)S(1)}, f32[32,2048]{1,0:T(8,128)S(1)}, u32[]{:S(2)}, u32[]{:S(2)}) collective-permute-start(f32[32,2048]{1,0:T(8,128)S(1)} %get-tuple-element.68.refs_1_), channel_id=1, source_target_pairs={{0,4},{1,5},{2,3},{3,2},{4,0},{5,1},{6,10},{7,11},{8,12},{9,13},{1... | collective-permute-start | bytes 786440 | tf_op jit(solution)/shard_map/ppermute | solution.py:374
  27.3 6.3 %collective-permute-start.8 = (f32[32,2048]{1,0:T(8,128)S(1)}, f32[32,2048]{1,0:T(8,128)S(1)}, u32[]{:S(2)}, u32[]{:S(2)}) collective-permute-start(f32[32,2048]{1,0:T(8,128)S(1)} %get-tuple-element.69.refs_2_), channel_id=1, source_target_pairs={{0,1},{1,0},{2,6},{3,7},{4,8},{5,9},{6,2},{7,3},{8,4},{9,5},{10,14... | collective-permute-start | bytes 786440 | tf_op jit(solution)/shard_map/ppermute | solution.py:374
  32.2 1.8 %collective-permute-start.10 = (f32[2,32,1024]{2,1,0:T(8,128)S(1)}, f32[2,32,1024]{2,1,0:T(8,128)S(1)}, u32[]{:S(2)}, u32[]{:S(2)}) collective-permute-start(f32[2,32,1024]{2,1,0:T(8,128)S(1)} %collective-permute-done.9.refs_8_.refs_2_), channel_id=1, source_target_pairs={{0,1},{1,0},{2,3},{3,2},{4,5},{5,4},{6,7},{7,6},{8,9},{9,8},{10,11... | collective-permute-start | bytes 786440 | tf_op jit(solution)/shard_map/ppermute | solution.py:374
  35.1 8.2 %collective-permute-start.11 = (f32[32,2048]{1,0:T(8,128)S(1)}, f32[32,2048]{1,0:T(8,128)S(1)}, u32[]{:S(2)}, u32[]{:S(2)}) collective-permute-start(f32[32,2048]{1,0:T(8,128)S(1)} %get-tuple-element.73.refs_1_), channel_id=1, source_target_pairs={{0,4},{1,5},{2,3},{3,2},{4,0},{5,1},{6,10},{7,11},{8,12},{9,13},{1... | collective-permute-start | bytes 786440 | tf_op jit(solution)/shard_map/ppermute | solution.py:374
  37.2 6.0 %collective-permute-start.12 = (f32[32,2048]{1,0:T(8,128)S(1)}, f32[32,2048]{1,0:T(8,128)S(1)}, u32[]{:S(2)}, u32[]{:S(2)}) collective-permute-start(f32[32,2048]{1,0:T(8,128)S(1)} %get-tuple-element.74.refs_2_), channel_id=1, source_target_pairs={{0,1},{1,0},{2,6},{3,7},{4,8},{5,9},{6,2},{7,3},{8,4},{9,5},{10,14... | collective-permute-start | bytes 786440 | tf_op jit(solution)/shard_map/ppermute | solution.py:374
  37.2 9.8 %collective-permute-start.18 = (f32[32,1024]{1,0:T(8,128)S(1)}, f32[32,1024]{1,0:T(8,128)S(1)}, u32[]{:S(2)}, u32[]{:S(2)}) collective-permute-start(f32[32,1024]{1,0:T(8,128)S(1)} %get-tuple-element.81), channel_id=1, source_target_pairs={{0,2},{1,3},{2,0},{3,1},{4,6},{5,7},{6,4},{7,5},{8,10},{9,11},{10,... | collective-permute-start | bytes 393224 | tf_op jit(solution)/shard_map/ppermute | solution.py:374
  39.5 7.5 %collective-permute-start.19 = (f32[32,1024]{1,0:T(8,128)S(1)}, f32[32,1024]{1,0:T(8,128)S(1)}, u32[]{:S(2)}, u32[]{:S(2)}) collective-permute-start(f32[32,1024]{1,0:T(8,128)S(1)} %get-tuple-element.82), channel_id=1, source_target_pairs={{0,3},{1,2},{2,1},{3,0},{4,7},{5,6},{6,5},{7,4},{8,11},{9,10},{10,... | collective-permute-start | bytes 393224 | tf_op jit(solution)/shard_map/ppermute | solution.py:374
  39.5 7.5 %collective-permute-start.20 = (f32[32,1024]{1,0:T(8,128)S(1)}, f32[32,1024]{1,0:T(8,128)S(1)}, u32[]{:S(2)}, u32[]{:S(2)}) collective-permute-start(f32[32,1024]{1,0:T(8,128)S(1)} %get-tuple-element.83), channel_id=1, source_target_pairs={{0,1},{1,0},{2,3},{3,2},{4,5},{5,4},{6,7},{7,6},{8,9},{9,8},{10,11... | collective-permute-start | bytes 393224 | tf_op jit(solution)/shard_map/ppermute | solution.py:374
  44.1 3.0 %copy-start = (f32[4,32,1024]{2,1,0:T(8,128)S(1)}, f32[4,32,1024]{2,1,0:T(8,128)}, u32[]{:S(2)}) copy-start(f32[4,32,1024]{2,1,0:T(8,128)} %refs_4_.1) | copy-start | bytes 1572868
  44.7 6.2 %collective-permute-start.17 = (f32[32,1024]{1,0:T(8,128)S(1)}, f32[32,1024]{1,0:T(8,128)S(1)}, u32[]{:S(2)}, u32[]{:S(2)}) collective-permute-start(f32[32,1024]{1,0:T(8,128)S(1)} %get-tuple-element.79.refs_1_), channel_id=1, source_target_pairs={{0,4},{1,5},{2,3},{3,2},{4,0},{5,1},{6,10},{7,11},{8,12},{9,13},{1... | collective-permute-start | bytes 393224 | tf_op jit(solution)/shard_map/ppermute | solution.py:374
  47.1 3.8 %collective-permute-start.21 = (f32[32,1024]{1,0:T(8,128)S(1)}, f32[32,1024]{1,0:T(8,128)S(1)}, u32[]{:S(2)}, u32[]{:S(2)}) collective-permute-start(f32[32,1024]{1,0:T(8,128)S(1)} %get-tuple-element.89.refs_2_), channel_id=1, source_target_pairs={{0,1},{1,0},{2,6},{3,7},{4,8},{5,9},{6,2},{7,3},{8,4},{9,5},{10,14... | collective-permute-start | bytes 393224 | tf_op jit(solution)/shard_map/ppermute | solution.py:374
  47.3 6.0 %collective-permute-start.13 = (f32[32,1024]{1,0:T(8,128)S(1)}, f32[32,1024]{1,0:T(8,128)S(1)}, u32[]{:S(2)}, u32[]{:S(2)}) collective-permute-start(f32[32,1024]{1,0:T(8,128)S(1)} %get-tuple-element.75.refs_1_), channel_id=1, source_target_pairs={{0,4},{1,5},{2,3},{3,2},{4,0},{5,1},{6,10},{7,11},{8,12},{9,13},{1... | collective-permute-start | bytes 393224 | tf_op jit(solution)/shard_map/ppermute | solution.py:374
  49.4 3.9 %collective-permute-start.14 = (f32[32,1024]{1,0:T(8,128)S(1)}, f32[32,1024]{1,0:T(8,128)S(1)}, u32[]{:S(2)}, u32[]{:S(2)}) collective-permute-start(f32[32,1024]{1,0:T(8,128)S(1)} %get-tuple-element.76.refs_2_), channel_id=1, source_target_pairs={{0,1},{1,0},{2,6},{3,7},{4,8},{5,9},{6,2},{7,3},{8,4},{9,5},{10,14... | collective-permute-start | bytes 393224 | tf_op jit(solution)/shard_map/ppermute | solution.py:374
  51.1 5.5 %collective-permute-start.22 = (f32[32,1024]{1,0:T(8,128)S(1)}, f32[32,1024]{1,0:T(8,128)S(1)}, u32[]{:S(2)}, u32[]{:S(2)}) collective-permute-start(f32[32,1024]{1,0:T(8,128)S(1)} %get-tuple-element.91), channel_id=1, source_target_pairs={{0,2},{1,3},{2,0},{3,1},{4,6},{5,7},{6,4},{7,5},{8,10},{9,11},{10,... | collective-permute-start | bytes 393224 | tf_op jit(solution)/shard_map/ppermute | solution.py:374
  53.5 5.8 %collective-permute-start.15 = (f32[32,1024]{1,0:T(8,128)S(1)}, f32[32,1024]{1,0:T(8,128)S(1)}, u32[]{:S(2)}, u32[]{:S(2)}) collective-permute-start(f32[32,1024]{1,0:T(8,128)S(1)} %get-tuple-element.77), channel_id=1, source_target_pairs={{0,3},{1,2},{2,1},{3,0},{4,7},{5,6},{6,5},{7,4},{8,11},{9,10},{10,... | collective-permute-start | bytes 393224 | tf_op jit(solution)/shard_map/ppermute | solution.py:374
  55.5 3.7 %collective-permute-start.16 = (f32[32,1024]{1,0:T(8,128)S(1)}, f32[32,1024]{1,0:T(8,128)S(1)}, u32[]{:S(2)}, u32[]{:S(2)}) collective-permute-start(f32[32,1024]{1,0:T(8,128)S(1)} %get-tuple-element.78), channel_id=1, source_target_pairs={{0,1},{1,0},{2,3},{3,2},{4,5},{5,4},{6,7},{7,6},{8,9},{9,8},{10,11... | collective-permute-start | bytes 393224 | tf_op jit(solution)/shard_map/ppermute | solution.py:374
  (8 other events, 16.1 us)
